TPU v7x, 32 devices: a whole 2x2x4 slice. The times are simulated.
32 devices in a mesh: dp: 8 (over z, y), tensor: 4 (over x, core).
Axes of the slice: x: 2, y: 2, z: 4, core: 2. Of those that a mesh axis runs over, the one named last changes fastest.
Arguments:
- block_input: bfloat16 [2560, 2304], P(('dp', 'tensor')), may hold values from -6 to 6
- w_qkv: bfloat16 [3, 2304, 2304], P(None, 'dp', 'tensor'), may hold values from -0.1875 to 0.1875
- w_out: bfloat16 [2304, 2304], P('tensor', 'dp'), may hold values from -1 to 1
- w_gate_up: bfloat16 [2, 2304, 5760], P(None, 'dp', 'tensor'), may hold values from -0.125 to 0.125
- w_down: bfloat16 [5760, 2304], P('tensor', 'dp'), may hold values from -0.25 to 0.25
- norm_gains: bfloat16 [2, 2304], P(None, 'dp'), may hold values from 0.099609375 to 1.8984375
- cotangent: bfloat16 [2560, 2304], P(('dp', 'tensor')), may hold values from -6 to 6
- tok_seg: int32 [2560], P('dp'), may hold values from 0 to 12, as said below
- tok_pos: int32 [2560], P('dp'), may hold values from 0 to 1407, as said below
- seg_parent: int32 [13], replicated, may hold values from -1 to 4, as said below
Outputs:
- output: float32 [2560, 2304], P(('dp', 'tensor'))
- grad_input: float32 [2560, 2304], P(('dp', 'tensor'))
- grad_w_qkv: float32 [3, 2304, 2304], P(None, 'dp', 'tensor')
- grad_w_out: float32 [2304, 2304], P('tensor', 'dp')
- grad_w_gate_up: float32 [2, 2304, 5760], P(None, 'dp', 'tensor')
- grad_w_down: float32 [5760, 2304], P('tensor', 'dp')
- grad_gains: float32 [2, 2304], P(None, ('dp', 'tensor'))
Inputs may be any that keep to these rules, and one draw needn't show every extreme that they name: Segments are numbered in token order, so tok_seg never falls: first the 1 trunks of 1024 tokens, then 4 * 1 branches, then 8 * 1 leaves; branches hold 64 to 192 tokens and leaves 128 - 128 // 2 to 192. Every segment is present. `tok_pos`: A trunk's tokens count from 0; a branch continues after its trunk's 1024, a leaf after its trunk and its branch. Some leaf of the longest length lies under a branch of the longest length, so the largest position is reached. `seg_parent`: A trunk's parent is -1, a branch's is a trunk, a leaf's is a branch; every trunk has four branches and every branch two leaves. The first token and the last token lie in one tree.
All inputs are finite; a program needn't handle non-finite values.
Results may differ from a plain program's by a relative error of at most 0.02.
Values may be sent and summed in bfloat16 or wider, within the bound.
No kernel may reach another device: no remote copies, remote signals or barrier semaphores. Data moves between devices by JAX's collectives and lax.ppermute only.
A program may use at most 256 MiB of HBM per device.

v0:
```python
import math

import jax
import jax.numpy as jnp
from jax import lax
from jax.sharding import PartitionSpec as P

HD = 64


norm_eps = 1e-05
depth_scale = 1.4 / math.sqrt(40.0)
rope_base = 10000.0
far_below = -1e30


def lineage(segments, parents):
    seg_table = jnp.arange(parents.shape[0], dtype=jnp.int32)
    matches = segments[:, None] == seg_table[None, :]
    parent_seg = jnp.sum(jnp.where(matches, parents[None, :], 0), axis=1)
    matches = parent_seg[:, None] == seg_table[None, :]
    grand_seg = jnp.sum(jnp.where(matches, parents[None, :], 0), axis=1)
    grand_seg = jnp.where(parent_seg >= 0, grand_seg, -1)
    return (parent_seg, grand_seg)


def rope_tables(positions, head_width):
    half_size = head_width // 2
    frequency = jnp.power(rope_base, -2.0 * jnp.arange(half_size, dtype=jnp.float32) / head_width)
    angles = positions.astype(jnp.float32)[:, None] * frequency[None, :]
    return (jnp.cos(angles), jnp.sin(angles))


def rotate(values, cosine, sine_table, inverse):
    half_size = values.shape[-1] // 2
    front = values[..., :half_size]
    latter = values[..., half_size:]
    cos_rows = cosine[:, None, :]
    sin_rows = (-sine_table if inverse else sine_table)[:, None, :]
    return jnp.concatenate(
        [front * cos_rows - latter * sin_rows, latter * cos_rows + front * sin_rows], axis=-1
    )


def allowed_pairs(query_info, key_segment, key_index):
    segments, parent_seg, grand_seg, index = query_info
    same = (key_segment[None, :] == segments[:, None]) & (key_index[None, :] <= index[:, None])
    return (
        same
        | (key_segment[None, :] == parent_seg[:, None])
        | (key_segment[None, :] == grand_seg[:, None])
    )


def blocked(step, running, arrays, limit):
    row_count = arrays[0].shape[0]
    block_rows = math.gcd(row_count, limit)
    block_count = row_count // block_rows
    shaped = tuple((array.reshape((block_count, block_rows) + array.shape[1:]) for array in arrays))
    offsets = block_rows * jnp.arange(block_count, dtype=jnp.int32)

    def advance(current, element):
        return (step(current, element[0], element[1]), None)

    result, _ = lax.scan(advance, running, (shaped, offsets))
    return result


def arrange(vector, groups, shares):
    piece_width = vector.shape[0] // (groups * shares)
    return vector.reshape(groups, shares, piece_width).transpose(1, 0, 2).reshape(-1)


def norm_back(upstream, unit_rows, inv_rms):
    return inv_rms * (upstream - unit_rows * jnp.mean(upstream * unit_rows, axis=-1, keepdims=True))


def on_device(
    block_input,
    w_qkv,
    w_out,
    w_gate_up,
    w_down,
    norm_gains,
    cotangent,
    tok_seg,
    tok_pos,
    seg_parent,
):
    data_size = lax.axis_size("dp")
    shares = lax.axis_size("tensor")
    data_index = lax.axis_index("dp")
    tensor_index = lax.axis_index("tensor")
    own_count = block_input.shape[0]
    qkv_full, out_full, gate_up_full, down_full, gain_full = (
        lax.all_gather(w_qkv, "dp", axis=1, tiled=True),
        lax.all_gather(w_out, "dp", axis=1, tiled=True),
        lax.all_gather(w_gate_up, "dp", axis=1, tiled=True),
        lax.all_gather(w_down, "dp", axis=1, tiled=True),
        lax.all_gather(norm_gains, "dp", axis=1, tiled=True),
    )
    gain_attn = gain_full[0].astype(jnp.float32)
    gain_ffn = gain_full[1].astype(jnp.float32)
    group_input = lax.all_gather(block_input, "tensor", axis=0, tiled=True)
    group_count = group_input.shape[0]
    input_rows = group_input.astype(jnp.float32)
    inv_rms_a = lax.rsqrt(jnp.mean(input_rows * input_rows, axis=-1, keepdims=True) + norm_eps)
    unit_a = input_rows * inv_rms_a
    normed_a = (unit_a * gain_attn).astype(jnp.bfloat16)
    q_pre = jnp.dot(normed_a, qkv_full[0], preferred_element_type=jnp.float32)
    k_pre = jnp.dot(normed_a, qkv_full[1], preferred_element_type=jnp.float32)
    v_pre = jnp.dot(normed_a, qkv_full[2], preferred_element_type=jnp.float32)
    local_heads = q_pre.shape[1] // HD
    head_shape = (group_count, local_heads, HD)
    cosine, sine_table = rope_tables(tok_pos, HD)
    queries = rotate(q_pre.reshape(head_shape), cosine, sine_table, False).astype(jnp.bfloat16)
    key_rows = (
        rotate(k_pre.reshape(head_shape), cosine, sine_table, False)
        .astype(jnp.bfloat16)
        .reshape(group_count, -1)
    )
    value_rows = v_pre.astype(jnp.bfloat16)
    key_heads_own = key_rows.reshape(head_shape)
    value_heads_own = value_rows.reshape(head_shape)
    scale_factor = HD ** (-0.5)
    parent_seg, grand_seg = lineage(tok_seg, seg_parent)
    own_index = data_index * group_count + jnp.arange(group_count, dtype=jnp.int32)
    own_info = (tok_seg, parent_seg, grand_seg, own_index)

    def forward_step(running, portion, offset):
        key_part, value_part, seg_part = portion
        key_count = key_part.shape[0]
        allowed = allowed_pairs(own_info, seg_part, offset + jnp.arange(key_count, dtype=jnp.int32))

        def forward_compute(current):
            row_peak, row_total, context = current
            key_heads = key_part.reshape(key_count, local_heads, HD)
            value_heads = value_part.reshape(key_count, local_heads, HD)
            raw_scores = jnp.einsum(
                "qhd,khd->hqk", queries, key_heads, preferred_element_type=jnp.float32
            )
            scores = jnp.where(allowed[None], raw_scores * scale_factor, far_below)
            new_peak = jnp.maximum(row_peak, jnp.max(scores, axis=2))
            weights = jnp.where(allowed[None], jnp.exp(scores - new_peak[:, :, None]), 0.0)
            factor = jnp.exp(row_peak - new_peak)
            row_total = row_total * factor + jnp.sum(weights, axis=2)
            context = context * factor[:, :, None] + jnp.einsum(
                "hqk,khd->hqd",
                weights.astype(jnp.bfloat16),
                value_heads,
                preferred_element_type=jnp.float32,
            )
            return (new_peak, row_total, context)

        return lax.cond(jnp.any(allowed), forward_compute, lambda current: current, running)

    def query_grad_step(running, portion, offset):
        key_part, value_part, seg_part = portion
        key_count = key_part.shape[0]
        allowed = allowed_pairs(own_info, seg_part, offset + jnp.arange(key_count, dtype=jnp.int32))

        def query_compute(current):
            key_heads = key_part.reshape(key_count, local_heads, HD)
            value_heads = value_part.reshape(key_count, local_heads, HD)
            raw_scores = jnp.einsum(
                "qhd,khd->hqk", queries, key_heads, preferred_element_type=jnp.float32
            )
            weights = jnp.where(
                allowed[None], jnp.exp(raw_scores * scale_factor - log_total[:, :, None]), 0.0
            )
            grad_weights = jnp.einsum(
                "qhd,khd->hqk", grad_heads, value_heads, preferred_element_type=jnp.float32
            )
            grad_scores = (weights * (grad_weights - row_delta[:, :, None]) * scale_factor).astype(
                jnp.bfloat16
            )
            return current + jnp.einsum(
                "hqk,khd->hqd", grad_scores, key_heads, preferred_element_type=jnp.float32
            )

        return lax.cond(jnp.any(allowed), query_compute, lambda current: current, running)

    def key_grad_step(running, portion, offset):
        query_part, grad_part, total_part, delta_part, seg_part = portion
        query_count = query_part.shape[0]
        part_parent, part_grand = lineage(seg_part, seg_parent)
        part_info = (
            seg_part,
            part_parent,
            part_grand,
            offset + jnp.arange(query_count, dtype=jnp.int32),
        )
        allowed = allowed_pairs(part_info, tok_seg, own_index)

        def key_compute(current):
            grad_key, grad_value = current
            query_heads = query_part.astype(jnp.bfloat16).reshape(query_count, local_heads, HD)
            grad_part_heads = grad_part.astype(jnp.bfloat16).reshape(query_count, local_heads, HD)
            raw_scores = jnp.einsum(
                "qhd,khd->hqk", query_heads, key_heads_own, preferred_element_type=jnp.float32
            )
            weights = jnp.where(
                allowed[None], jnp.exp(raw_scores * scale_factor - total_part.T[:, :, None]), 0.0
            )
            grad_weights = jnp.einsum(
                "qhd,khd->hqk", grad_part_heads, value_heads_own, preferred_element_type=jnp.float32
            )
            grad_scores = (
                weights * (grad_weights - delta_part.T[:, :, None]) * scale_factor
            ).astype(jnp.bfloat16)
            grad_key = grad_key + jnp.einsum(
                "hqk,qhd->khd", grad_scores, query_heads, preferred_element_type=jnp.float32
            )
            grad_value = grad_value + jnp.einsum(
                "hqk,qhd->khd",
                weights.astype(jnp.bfloat16),
                grad_part_heads,
                preferred_element_type=jnp.float32,
            )
            return (grad_key, grad_value)

        return lax.cond(jnp.any(allowed), key_compute, lambda current: current, running)

    initial = (
        jnp.full((local_heads, group_count), far_below, jnp.float32),
        jnp.zeros((local_heads, group_count), jnp.float32),
        jnp.zeros((local_heads, group_count, HD), jnp.float32),
    )
    row_peak, row_total, context = blocked(
        forward_step,
        initial,
        (
            lax.all_gather(key_rows, "dp", axis=0, tiled=True),
            lax.all_gather(value_rows, "dp", axis=0, tiled=True),
            lax.all_gather(tok_seg, "dp", axis=0, tiled=True),
        ),
        group_count,
    )
    context = context / row_total[:, :, None]
    log_total = row_peak + jnp.log(row_total)
    attended = context.transpose(1, 0, 2).reshape(group_count, -1).astype(jnp.bfloat16)
    branch_attn = lax.psum_scatter(
        jnp.dot(attended, out_full, preferred_element_type=jnp.float32),
        "tensor",
        scatter_dimension=0,
        tiled=True,
    )
    mid_rows = block_input.astype(jnp.float32) + depth_scale * branch_attn
    mid_group = lax.all_gather(mid_rows, "tensor", axis=0, tiled=True)
    inv_rms_f = lax.rsqrt(jnp.mean(mid_group * mid_group, axis=-1, keepdims=True) + norm_eps)
    unit_f = mid_group * inv_rms_f
    normed_f = (unit_f * gain_ffn).astype(jnp.bfloat16)
    gate_pre = jnp.dot(normed_f, gate_up_full[0], preferred_element_type=jnp.float32)
    up_pre = jnp.dot(normed_f, gate_up_full[1], preferred_element_type=jnp.float32)
    sigmoid_gate = jax.nn.sigmoid(gate_pre)
    silu_gate = gate_pre * sigmoid_gate
    hidden = (silu_gate * up_pre).astype(jnp.bfloat16)
    branch_ffn = lax.psum_scatter(
        jnp.dot(hidden, down_full, preferred_element_type=jnp.float32),
        "tensor",
        scatter_dimension=0,
        tiled=True,
    )
    output = mid_rows + depth_scale * branch_ffn
    grad_output = cotangent.astype(jnp.float32)
    grad_branch_f = lax.all_gather(
        (depth_scale * grad_output).astype(jnp.bfloat16), "tensor", axis=0, tiled=True
    )
    grad_hidden = jnp.dot(grad_branch_f, down_full.T, preferred_element_type=jnp.float32)
    grad_down_part = jnp.dot(hidden.T, grad_branch_f, preferred_element_type=jnp.float32)
    grad_gate = (
        grad_hidden * up_pre * sigmoid_gate * (1.0 + gate_pre * (1.0 - sigmoid_gate))
    ).astype(jnp.bfloat16)
    grad_up = (grad_hidden * silu_gate).astype(jnp.bfloat16)
    grad_normed_f = jnp.dot(
        grad_gate, gate_up_full[0].T, preferred_element_type=jnp.float32
    ) + jnp.dot(grad_up, gate_up_full[1].T, preferred_element_type=jnp.float32)
    grad_gate_up_part = jnp.stack(
        [
            jnp.dot(normed_f.T, grad_gate, preferred_element_type=jnp.float32),
            jnp.dot(normed_f.T, grad_up, preferred_element_type=jnp.float32),
        ]
    )
    gain_f_part = arrange(jnp.sum(grad_normed_f * unit_f, axis=0), data_size, shares)
    grad_normed_rows, gain_f_piece = (
        lax.psum_scatter(grad_normed_f, "tensor", scatter_dimension=0, tiled=True),
        lax.psum_scatter(gain_f_part, "tensor", scatter_dimension=0, tiled=True),
    )
    unit_f_own = lax.dynamic_slice_in_dim(unit_f, tensor_index * own_count, own_count, 0)
    inv_rms_f_own = lax.dynamic_slice_in_dim(inv_rms_f, tensor_index * own_count, own_count, 0)
    grad_mid = grad_output + norm_back(grad_normed_rows * gain_ffn, unit_f_own, inv_rms_f_own)
    grad_branch_a = lax.all_gather(
        (depth_scale * grad_mid).astype(jnp.bfloat16), "tensor", axis=0, tiled=True
    )
    grad_out_part = jnp.dot(attended.T, grad_branch_a, preferred_element_type=jnp.float32)
    grad_attended = jnp.dot(grad_branch_a, out_full.T, preferred_element_type=jnp.float32).astype(
        jnp.bfloat16
    )
    grad_heads = grad_attended.reshape(head_shape)
    row_delta = jnp.sum(grad_heads.astype(jnp.float32).transpose(1, 0, 2) * context, axis=2)
    zero_heads = jnp.zeros((local_heads, group_count, HD), jnp.float32)
    grad_queries = blocked(
        query_grad_step,
        zero_heads,
        (
            lax.all_gather(key_rows, "dp", axis=0, tiled=True),
            lax.all_gather(value_rows, "dp", axis=0, tiled=True),
            lax.all_gather(tok_seg, "dp", axis=0, tiled=True),
        ),
        group_count,
    )
    zero_keys = jnp.zeros(head_shape, jnp.float32)
    sent = (
        queries.reshape(group_count, -1).astype(jnp.float32),
        grad_attended.astype(jnp.float32),
        log_total.T,
        row_delta.T,
        tok_seg,
    )
    grad_keys, grad_values = blocked(
        key_grad_step,
        (zero_keys, zero_keys),
        (
            lax.all_gather(sent[0], "dp", axis=0, tiled=True),
            lax.all_gather(sent[1], "dp", axis=0, tiled=True),
            lax.all_gather(sent[2], "dp", axis=0, tiled=True),
            lax.all_gather(sent[3], "dp", axis=0, tiled=True),
            lax.all_gather(sent[4], "dp", axis=0, tiled=True),
        ),
        group_count,
    )
    grad_q_pre = (
        rotate(grad_queries.transpose(1, 0, 2), cosine, sine_table, True)
        .astype(jnp.bfloat16)
        .reshape(group_count, -1)
    )
    grad_k_pre = (
        rotate(grad_keys, cosine, sine_table, True).astype(jnp.bfloat16).reshape(group_count, -1)
    )
    grad_v_pre = grad_values.astype(jnp.bfloat16).reshape(group_count, -1)
    grad_normed_a = (
        jnp.dot(grad_q_pre, qkv_full[0].T, preferred_element_type=jnp.float32)
        + jnp.dot(grad_k_pre, qkv_full[1].T, preferred_element_type=jnp.float32)
        + jnp.dot(grad_v_pre, qkv_full[2].T, preferred_element_type=jnp.float32)
    )
    grad_qkv_part = jnp.stack(
        [
            jnp.dot(normed_a.T, grad_q_pre, preferred_element_type=jnp.float32),
            jnp.dot(normed_a.T, grad_k_pre, preferred_element_type=jnp.float32),
            jnp.dot(normed_a.T, grad_v_pre, preferred_element_type=jnp.float32),
        ]
    )
    gain_a_part = arrange(jnp.sum(grad_normed_a * unit_a, axis=0), data_size, shares)
    grad_norm_rows, gain_a_piece = (
        lax.psum_scatter(grad_normed_a, "tensor", scatter_dimension=0, tiled=True),
        lax.psum_scatter(gain_a_part, "tensor", scatter_dimension=0, tiled=True),
    )
    unit_a_own = lax.dynamic_slice_in_dim(unit_a, tensor_index * own_count, own_count, 0)
    inv_rms_a_own = lax.dynamic_slice_in_dim(inv_rms_a, tensor_index * own_count, own_count, 0)
    grad_input = grad_mid + norm_back(grad_norm_rows * gain_attn, unit_a_own, inv_rms_a_own)
    gain_pieces = jnp.stack([gain_a_piece, gain_f_piece])
    grad_qkv, grad_out, grad_gate_up, grad_down, grad_gains = (
        lax.psum_scatter(grad_qkv_part, "dp", scatter_dimension=1, tiled=True),
        lax.psum_scatter(grad_out_part, "dp", scatter_dimension=1, tiled=True),
        lax.psum_scatter(grad_gate_up_part, "dp", scatter_dimension=1, tiled=True),
        lax.psum_scatter(grad_down_part, "dp", scatter_dimension=1, tiled=True),
        lax.psum_scatter(gain_pieces, "dp", scatter_dimension=1, tiled=True),
    )
    return (output, grad_input, grad_qkv, grad_out, grad_gate_up, grad_down, grad_gains)


def solution(mesh):
    in_specs = (
        P(("dp", "tensor"), None),
        P(None, "dp", "tensor"),
        P("tensor", "dp"),
        P(None, "dp", "tensor"),
        P("tensor", "dp"),
        P(None, "dp"),
        P(("dp", "tensor"), None),
        P("dp"),
        P("dp"),
        P(),
    )
    out_specs = (
        P(("dp", "tensor"), None),
        P(("dp", "tensor"), None),
        P(None, "dp", "tensor"),
        P("tensor", "dp"),
        P(None, "dp", "tensor"),
        P("tensor", "dp"),
        P(None, ("dp", "tensor")),
    )
    return jax.shard_map(
        on_device, mesh=mesh, in_specs=in_specs, out_specs=out_specs, check_vma=False
    )
```

profile of v0, /device:TPU:1, one launch (start us, length us, event | category | flops | bytes accessed | tf_op | source)
XLA Modules:
  0.0 2710.0 jit_solution(436372737371862198)
XLA Ops:
  8.7 22.6 all-gather
  34.9 128.6 %all-gather.18.cloned.1.call-done = bf16[3,2304,576]{2,1,0:T(8,128)(2,1)} async-done(((bf16[3,288,576]{2,1,0:T(8,128)(2,1)}), bf16[3,2304,576]{2,1,0:T(8,128)(2,1)}) %all-gather.18.cloned.1.call-update) | async-done | bytes 7962640 | tf_op jit(solution)/shard_map/all_gather | solution.py:96
  189.3 28.1 %all-reduce = s32[2560]{0:T(1024)S(1)} all-reduce(s32[2560]{0:T(1024)S(1)} %dynamic-update-slice), channel_id=1, replica_groups=mesh['dp'=8,'tensor'=4] {'dp'}, use_global_device_ids=true, to_apply=%add | all-reduce | flops 2560 | bytes 20480
  217.7 25.6 all-gather.20.cloned.1.call-done
  249.2 57.2 %all-gather.22.cloned.1.call-done = bf16[2560,576]{1,0:T(8,128)(2,1)} async-done(((bf16[320,576]{1,0:T(8,128)(2,1)}), bf16[2560,576]{1,0:T(8,128)(2,1)}) %all-gather.22.cloned.1.call-update) | async-done | bytes 2949136 | tf_op jit(solution)/shard_map/all_gather | solution.py:234
  312.5 27.7 %while.42 = (s32[]{:T(128)}, f32[9,320]{1,0:T(8,128)S(1)}, f32[9,320]{1,0:T(8,128)S(1)}, f32[9,320,64]{1,2,0:T(8,128)S(1)}, s32[8,320]{1,0:T(8,128)S(1)}, /*inde...) while((s32[]{:T(128)}, f32[9,320]{1,0:T(8,128)S(1)}, ...), condition=%wide.region_9.10_spmd.clone, body=%wide.region_3.9_spmd.clone.sunk | while | flops 249104640 | bytes 15721255 | solution.py:65
  340.2 25.0 all-gather.24.cloned.1.call-done
  370.2 40.1 %reduce-scatter.11.cloned.1.call-done = f32[80,2304]{1,0:T(8,128)} async-done(((f32[320,2304]{1,0:T(8,128)}), f32[80,2304]{1,0:T(8,128)}) %reduce-scatter.11.cloned.1.call-update) | async-done | bytes 737296 | tf_op jit(solution)/shard_map/reduce_scatter | solution.py:242
  414.9 25.5 all-gather.26.cloned.1.call-done
  445.6 192.1 %all-gather.28.cloned.1.call-done = bf16[2,2304,1440]{2,1,0:T(8,128)(2,1)} async-done(((bf16[2,288,1440]{2,1,0:T(8,128)(2,1)}), bf16[2,2304,1440]{2,1,0:T(8,128)(2,1)}) %all-gather.28.cloned.1.call-update) | async-done | bytes 13271056 | tf_op jit(solution)/shard_map/all_gather | solution.py:98
  637.7 7.3 fusion.51
  650.2 7.9 all-gather.32.cloned.1.call-done
  658.1 110.3 %all-gather.30.cloned.1.call-done = bf16[1440,2304]{0,1:T(8,128)(2,1)} async-done(((bf16[1440,288]{0,1:T(8,128)(2,1)}), bf16[1440,2304]{0,1:T(8,128)(2,1)}) %all-gather.30.cloned.1.call-update) | async-done | bytes 6635536 | tf_op jit(solution)/shard_map/all_gather | solution.py:99
  768.4 8.7 multiply_convert_fusion.8
  777.0 7.8 fusion.50
  784.9 6.8 multiply_reduce_fusion
  791.9 35.4 %reduce-scatter.15.cloned.1.call-done = f32[80,2304]{1,0:T(8,128)} async-done(((f32[320,2304]{1,0:T(8,128)}), f32[80,2304]{1,0:T(8,128)}) %reduce-scatter.15.cloned.1.call-update) | async-done | bytes 737296 | tf_op jit(solution)/shard_map/reduce_scatter | solution.py:286
  832.2 18.5 all-gather.34.cloned.1.call-done
  856.2 57.5 %all-gather.36.cloned.1.call-done = bf16[2560,576]{1,0:T(8,128)(2,1)} async-done(((bf16[320,576]{1,0:T(8,128)(2,1)}), bf16[2560,576]{1,0:T(8,128)(2,1)}) %all-gather.36.cloned.1.call-update) | async-done | bytes 2949136 | tf_op jit(solution)/shard_map/all_gather | solution.py:324
  913.7 5.9 copy.103
  919.7 27.4 %all-gather.1 = f32[8,320,9]{1,2,0:T(8,128)} all-gather(f32[1,320,9]{1,2,0:T(8,128)S(1)} %bitcast.226), channel_id=1, replica_groups=mesh['dp'=8,'tensor'=4] {'dp'}, dimensions={0}, use_global_device_ids=true | all-gather | bytes 103680 | tf_op jit(solution)/shard_map/all_gather | solution.py:326
  947.0 7.4 fusion.81
  955.8 27.2 %all-gather.2 = f32[8,320,9]{1,2,0:T(8,128)} all-gather(f32[1,320,9]{1,2,0:T(8,128)S(1)} %bitcast.227), channel_id=1, replica_groups=mesh['dp'=8,'tensor'=4] {'dp'}, dimensions={0}, use_global_device_ids=true | all-gather | bytes 103680 | tf_op jit(solution)/shard_map/all_gather | solution.py:327
  983.1 32.1 %while.43 = (s32[]{:T(128)}, f32[9,320,64]{1,2,0:T(8,128)S(1)}, s32[8,320]{1,0:T(8,128)S(1)}, s32[320]{0:T(512)S(1)}, s32[8]{0:T(128)S(1)}, /*index=5*/s32[320]{...) while((s32[]{:T(128)}, f32[9,320,64]{1,2,0:T(8,128)S(1)}, ...), condition=%wide.region_20.21_spmd.clone, body=%wide.region_16.20_spmd.clone.sunk | while | flops 361349760 | bytes 12406023 | solution.py:65
  986.0 8.9 conditional.10
  1015.2 6.2 copy.104
  1021.6 133.3 %while.44 = (s32[]{:T(128)}, f32[320,9,64]{0,2,1:T(8,128)S(1)}, f32[320,9,64]{0,2,1:T(8,128)S(1)}, s32[320]{0:T(512)S(1)}, s32[8,320]{1,0:T(8,128)S(1)}, /*index...) while((s32[]{:T(128)}, f32[320,9,64]{0,2,1:T(8,128)S(1)}, ...), condition=%wide.region_27.28_spmd.clone, body=%wide.region_21.0_spmd.clone.sunk | while | flops 483210240 | bytes 18104732 | solution.py:65
  1025.4 12.9 conditional.11
  1042.0 12.9 conditional.11
  1058.6 12.9 conditional.11
  1075.3 12.9 conditional.11
  1091.9 12.9 conditional.11
  1108.5 12.9 conditional.11
  1125.2 12.9 conditional.11
  1141.8 12.9 conditional.11
  1163.6 6.2 multiply_reduce_fusion.1
  1179.8 10.0 pad_maximum_fusion
  1189.8 41.6 %copy.105 = f32[2,2304,1440]{2,0,1:T(2,128)} copy(f32[2,2304,1440]{1,2,0:T(8,128)} %pad_maximum_fusion) | data formatting | bytes 53084160 | tf_op jit(solution)/shard_map/stack | solution.py:278
  1237.4 6.0 pad_maximum_fusion.1
  1243.4 24.1 copy.112
  1267.5 27.9 %reshape.333 = f32[2304,1728]{1,0:T(8,128)} reshape(f32[2304,3,576]{2,1,0:T(4,128)} %bitcast.195) | data formatting | bytes 31850496
  1303.4 7.0 fusion.83
  1316.2 22.4 all-reduce.5
  1338.7 16.0 all-reduce.4
  1359.8 712.8 %all-reduce.8.cloned.1.call-done = f32[2,2304,1440]{2,0,1:T(2,128)} async-done(((f32[2,2304,1440]{2,0,1:T(2,128)}), f32[2,2304,1440]{2,0,1:T(2,128)}) %all-reduce.8.cloned.1.call-update) | async-done | bytes 26542096
  2078.3 275.5 %reduce-scatter.23.cloned.1.call-done = f32[288,1728]{1,0:T(8,128)} async-done(((f32[2304,1728]{1,0:T(8,128)}), f32[288,1728]{1,0:T(8,128)}) %reduce-scatter.23.cloned.1.call-update) | async-done | bytes 1990672
  2358.4 110.8 %reduce-scatter.19.cloned.1.call-done = f32[576,288]{0,1:T(8,128)} async-done(((f32[576,2304]{0,1:T(8,128)}), f32[576,288]{0,1:T(8,128)}) %reduce-scatter.19.cloned.1.call-update) | async-done | bytes 663568 | tf_op jit(solution)/shard_map/reduce_scatter | solution.py:364
  2469.1 233.7 %reduce-scatter.21.cloned.1.call-done = f32[1440,288]{0,1:T(8,128)} async-done(((f32[1440,2304]{0,1:T(8,128)}), f32[1440,288]{0,1:T(8,128)}) %reduce-scatter.21.cloned.1.call-update) | async-done | bytes 1658896 | tf_op jit(solution)/shard_map/reduce_scatter | solution.py:366
  (419 shorter events, 306.4 us)
Async XLA Ops:
  7.2 25.9 all-gather.16.cloned.1.call-start
  7.9 155.6 %all-gather.18.cloned.1.call-start = ((), (), s32[]{:S(2)}) async-start(), calls=%async_computation.8 | async-start | bytes 9953280 | tf_op jit(solution)/shard_map/all_gather | solution.py:96
  8.6 234.7 %all-gather.20.cloned.1.call-start = ((), (), s32[]{:S(2)}) async-start(), calls=%async_computation.9 | async-start | bytes 3686400 | tf_op jit(solution)/shard_map/all_gather | solution.py:233
  32.2 150.9 %copy-start.30 = (f32[2304]{0:T(1024)}, f32[2304]{0:T(1024)S(1)}, u32[]{:S(2)}) copy-start(f32[2304]{0:T(1024)S(1)} %get-tuple-element.817) | copy-start | bytes 27652
  32.2 796.5 %copy-start.32 = (f32[2304]{0:T(1024)}, f32[2304]{0:T(1024)S(1)}, u32[]{:S(2)}) copy-start(f32[2304]{0:T(1024)S(1)} %get-tuple-element.816) | copy-start | bytes 27652
  33.1 148.5 %copy-start.28 = (f32[320,32]{0,1:T(8,128)}, f32[320,32]{0,1:T(8,128)S(1)}, u32[]{:S(2)}) copy-start(f32[320,32]{0,1:T(8,128)S(1)} %get-tuple-element.949) | copy-start | bytes 122884
  34.9 148.2 %copy-start.37 = (f32[320]{0:T(512)}, f32[320]{0:T(512)S(1)}, u32[]{:S(2)}) copy-start(f32[320]{0:T(512)S(1)} %add_rsqrt_fusion.1) | copy-start | bytes 3844
  183.0 34.5 %copy-start.35 = (s32[13]{0:T(128)S(1)}, s32[13]{0:T(128)}, u32[]{:S(2)}) copy-start(s32[13]{0:T(128)} %param.31) | copy-start | bytes 160
  183.0 123.5 %all-gather.22.cloned.1.call-start = ((), (), s32[]{:S(2)}) async-start(), calls=%async_computation.10 | async-start | bytes 3686400 | tf_op jit(solution)/shard_map/all_gather | solution.py:234
  187.0 178.2 %all-gather.24.cloned.1.call-start = ((), (), s32[]{:S(2)}) async-start(), calls=%async_computation.11 | async-start | bytes 3317760 | tf_op jit(solution)/shard_map/all_gather | solution.py:97
  187.6 222.7 %reduce-scatter.11.cloned.1.call-start = ((), (), s32[]{:S(2)}) async-start(), calls=%async_computation.12 | async-start | bytes 3686400 | tf_op jit(solution)/shard_map/reduce_scatter | solution.py:242
  340.2 29.9 %copy-start.10 = (bf16[9,320,64]{1,2,0:T(8,128)(2,1)}, bf16[9,320,64]{1,2,0:T(8,128)(2,1)S(1)}, u32[]{:S(2)}) copy-start(bf16[9,320,64]{1,2,0:T(8,128)(2,1)S(1)} %fusion.70) | copy-start | bytes 1105924
  370.1 40.2 %copy-start.22 = (bf16[80,2304]{1,0:T(8,128)(2,1)S(1)}, bf16[80,2304]{1,0:T(8,128)(2,1)}, u32[]{:S(2)}) copy-start(bf16[80,2304]{1,0:T(8,128)(2,1)} %param.22) | copy-start | bytes 1105924
  370.1 43.1 %copy-start.15 = (bf16[80,2304]{1,0:T(8,128)(2,1)S(1)}, bf16[80,2304]{1,0:T(8,128)(2,1)}, u32[]{:S(2)}) copy-start(bf16[80,2304]{1,0:T(8,128)(2,1)} %param.28) | copy-start | bytes 1105924
  370.2 70.3 %all-gather.26.cloned.1.call-start = ((), (), s32[]{:S(2)}) async-start(), calls=%async_computation.13 | async-start | bytes 3686400 | tf_op jit(solution)/shard_map/all_gather | solution.py:249
  412.5 225.3 %all-gather.28.cloned.1.call-start = ((), (), s32[]{:S(2)}) async-start(), calls=%async_computation.14 | async-start | bytes 15925248 | tf_op jit(solution)/shard_map/all_gather | solution.py:98
  413.2 244.9 %all-gather.32.cloned.1.call-start = ((), (), s32[]{:S(2)}) async-start(), calls=%async_computation.17 | async-start | bytes 1843200 | tf_op jit(solution)/shard_map/all_gather | solution.py:266
  414.1 354.3 %all-gather.30.cloned.1.call-start = ((), (), s32[]{:S(2)}) async-start(), calls=%async_computation.15 | async-start | bytes 7962624 | tf_op jit(solution)/shard_map/all_gather | solution.py:99
  414.7 412.5 %reduce-scatter.15.cloned.1.call-start = ((), (), s32[]{:S(2)}) async-start(), calls=%async_computation.18 | async-start | bytes 3686400 | tf_op jit(solution)/shard_map/reduce_scatter | solution.py:286
  637.7 7.3 copy-start.2
  637.7 8.8 copy-start.45
  768.4 16.5 slice-start
  768.4 16.5 slice-start.1
  768.4 16.5 slice-start.2
  777.0 7.8 copy-start.24
  777.0 7.8 copy-start.26
  777.0 7.9 copy-start.5
  777.0 7.9 slice-start.3
  791.7 59.1 %all-gather.34.cloned.1.call-start = ((), (), s32[]{:S(2)}) async-start(), calls=%async_computation.19 | async-start | bytes 1843200 | tf_op jit(solution)/shard_map/all_gather | solution.py:292
  791.9 63.3 %copy-start.41 = (f32[80]{0:T(128)}, f32[80]{0:T(128)S(1)}, u32[]{:S(2)}) copy-start(f32[80]{0:T(128)S(1)} %dynamic-slice.6) | copy-start | bytes 964
  828.8 26.4 copy-start.43
  831.1 82.6 %all-gather.36.cloned.1.call-start = ((), (), s32[]{:S(2)}) async-start(), calls=%async_computation.20 | async-start | bytes 3686400 | tf_op jit(solution)/shard_map/all_gather | solution.py:324
  832.2 23.1 copy-start.18
  832.2 183.0 %all-gather.38.cloned.1.call-start = ((), (), s32[]{:S(2)}) async-start(), calls=%async_computation.21 | async-start | bytes 3686400 | tf_op jit(solution)/shard_map/all_gather | solution.py:325
  855.2 458.7 %reduce-scatter.13.cloned.1.call-start = ((), (), s32[]{:S(2)}) async-start(), calls=%async_computation.16 | async-start | bytes 3686400 | tf_op jit(solution)/shard_map/reduce_scatter | solution.py:258
  954.5 400.9 %reduce-scatter.17.cloned.1.call-start = ((), (), s32[]{:S(2)}) async-start(), calls=%async_computation.22 | async-start | bytes 3686400 | tf_op jit(solution)/shard_map/reduce_scatter | solution.py:355
  1021.6 133.4 %copy-start.29 = (f32[320,32]{0,1:T(8,128)S(1)}, f32[320,32]{0,1:T(8,128)}, u32[]{:S(2)}) copy-start(f32[320,32]{0,1:T(8,128)} %copy-done.28) | copy-start | bytes 122884
  1021.6 133.4 %copy-start.34 = (f32[320,32]{0,1:T(8,128)S(1)}, f32[320,32]{0,1:T(8,128)}, u32[]{:S(2)}) copy-start(f32[320,32]{0,1:T(8,128)} %get-tuple-element.947) | copy-start | bytes 122884
  1155.0 8.6 copy-start.12
  1169.8 902.8 %all-reduce.8.cloned.1.call-start = ((), (), s32[]{:S(2)}) async-start(), calls=%async_computation.26 | async-start | bytes 56623104
  1231.4 1122.4 %reduce-scatter.23.cloned.1.call-start = ((), (), s32[]{:S(2)}) async-start(), calls=%async_computation.25 | async-start | bytes 18579456
  1295.5 1173.7 %reduce-scatter.19.cloned.1.call-start = ((), (), s32[]{:S(2)}) async-start(), calls=%async_computation.23 | async-start | bytes 6635520 | tf_op jit(solution)/shard_map/reduce_scatter | solution.py:364
  1301.5 1401.3 %reduce-scatter.21.cloned.1.call-start = ((), (), s32[]{:S(2)}) async-start(), calls=%async_computation.24 | async-start | bytes 15925248 | tf_op jit(solution)/shard_map/reduce_scatter | solution.py:366
  1311.1 45.8 %copy-start.7 = (f32[80,2304]{1,0:T(8,128)S(1)}, f32[80,2304]{1,0:T(8,128)}, u32[]{:S(2)}) copy-start(f32[80,2304]{1,0:T(8,128)} %reduce-scatter.15.cloned.1.call-done) | copy-start | bytes 2211844
  1311.1 45.8 %copy-start.16 = (bf16[80,2304]{1,0:T(8,128)(2,1)S(1)}, bf16[80,2304]{1,0:T(8,128)(2,1)}, u32[]{:S(2)}) copy-start(bf16[80,2304]{1,0:T(8,128)(2,1)} %param.28) | copy-start | bytes 1105924
  1311.1 45.8 %copy-start.33 = (f32[2304]{0:T(1024)S(1)}, f32[2304]{0:T(1024)}, u32[]{:S(2)}) copy-start(f32[2304]{0:T(1024)} %copy-done.32) | copy-start | bytes 27652
  1311.1 45.8 %copy-start.42 = (f32[80]{0:T(128)S(1)}, f32[80]{0:T(128)}, u32[]{:S(2)}) copy-start(f32[80]{0:T(128)} %copy-done.41) | copy-start | bytes 964
  1311.1 45.9 %copy-start.44 = (f32[80]{0:T(128)S(1)}, f32[80]{0:T(128)}, u32[]{:S(2)}) copy-start(f32[80]{0:T(128)} %copy-done.43) | copy-start | bytes 964
  (24 other events, 75.3 us)
Sparse Core Ops, SparseCore 0:
  9.6 21.5 all-gather.15
  33.4 130.0 all-gather.17
  183.1 60.1 all-gather.19
  245.9 60.5 all-gather.21
  308.5 56.7 all-gather.23
  370.3 40.0 reduce-scatter.10
  412.6 27.8 all-gather.25
  442.9 194.8 all-gather.27
  639.9 18.0 all-gather.31
  660.3 107.9 all-gather.29
  791.9 35.3 reduce-scatter.14
  831.2 19.4 all-gather.33
  853.0 60.6 all-gather.35
  915.8 63.2 all-gather.37
  981.4 36.3 reduce-scatter.12
  1169.9 46.7 reduce-scatter.16
  1231.5 841.0 all-reduce.7
  2077.0 276.7 reduce-scatter.22
  2358.5 110.6 reduce-scatter.18
  2473.6 229.1 reduce-scatter.20
where the time goes:
time: 2720 us; the launch traced here: 2710 us
  waiting for transfers between devices  2060 us (76%)
  local copies, waits for them, and re-layouts  196 us (7%)
  matrix products  195 us (7%)
  blocking collectives  144 us (5%)
  other arithmetic  79.5 us (3%)
    unnamed x22, waiting for transfers between devices  992 us
    reduce_scatter x1, waiting for transfers between devices, on_device(): lax.psum_scatter(grad_down_part, 'dp', scatter_dimension=1, tiled=True)  234 us
    all_gather x1, waiting for transfers between devices, on_device(): lax.all_gather(w_gate_up, 'dp', axis=1, tiled=True)  192 us
    all_gather x1, waiting for transfers between devices, on_device(): lax.all_gather(w_qkv, 'dp', axis=1, tiled=True)  129 us
    reduce_scatter x1, waiting for transfers between devices, on_device(): lax.psum_scatter(grad_out_part, 'dp', scatter_dimension=1, tiled=True)  111 us
    all_gather x1, waiting for transfers between devices, on_device(): lax.all_gather(w_down, 'dp', axis=1, tiled=True)  110 us
    unnamed x122, local copies, waits for them, and re-layouts  97.9 us
    unnamed x3, blocking collectives  66.5 us
  transfers between devices with their start and end apart: 20, of which 16 were waited for; matrix products, arithmetic and copies ran while one was open for 15% of the time, Pallas kernels for 0%

commit v1 on v0

v1 whole, which is shorter than its diff:
```python
import math

import jax
import jax.numpy as jnp
from jax import lax
from jax.experimental import pallas as pl
from jax.experimental.pallas import tpu as pltpu
from jax.sharding import Mesh, PartitionSpec as P

HD = 64

norm_eps = 1e-05
depth_scale = 1.4 / math.sqrt(40.0)
rope_base = 10000.0
far_below = -1e30
f32 = jnp.float32
bf16 = jnp.bfloat16

PLANE = ("pb", "tx", "tc")
CHIPS = ("pb", "tx")
ROW = "za"


def dot(a, b, dims=((1,), (0,))):
    return lax.dot_general(a, b, (dims, ((), ())), preferred_element_type=f32)


def send_row(array, distance):
    return lax.ppermute(array, ROW, [(i, i ^ distance) for i in range(lax.axis_size(ROW))])


def swap_core(array):
    return lax.ppermute(array, "tc", [(0, 1), (1, 0)])


def row_gather(rows):
    count = lax.axis_size(ROW)
    return jnp.concatenate([rows] + [send_row(rows, k) for k in range(1, count)], axis=0)


def row_scatter(partial):
    count = lax.axis_size(ROW)
    height = partial.shape[0] // count
    total = partial[:height]
    for k in range(1, count):
        total = total + send_row(partial[k * height : (k + 1) * height].astype(bf16), k).astype(f32)
    return total


def after(array, done):
    return lax.optimization_barrier((array, done))[0]


def plane_scatter(left, right):
    core = lax.axis_index("tc")
    chips = lax.axis_size("pb") * lax.axis_size("tx")
    blocks = left.reshape(left.shape[0], chips, 2, -1)

    def half(which):
        part = lax.dynamic_index_in_dim(blocks, which, 2, keepdims=False)
        return dot(part.reshape(left.shape[0], -1), right, ((0,), (0,)))

    other = swap_core(half(1 - core).astype(bf16))
    total = (half(core) + other.astype(f32)).astype(bf16)
    total = total.reshape(chips, -1, total.shape[1])
    total = lax.all_to_all(total, CHIPS, 0, 0, tiled=True)
    return jnp.sum(total.astype(f32), axis=0).astype(bf16)


def turn(array):
    pairs = []
    for z in range(4):
        for tx in range(2):
            for tc in range(2):
                pairs.append((z * 4 + tx * 2 + tc, (tc * 2 + tx) * 4 + (z % 2) * 2 + z // 2))
    return lax.ppermute(array, ("za", "tx", "tc"), pairs)


def lineage(segments, parents):
    seg_table = jnp.arange(parents.shape[0], dtype=jnp.int32)
    matches = segments[:, None] == seg_table[None, :]
    parent_seg = jnp.sum(jnp.where(matches, parents[None, :], 0), axis=1)
    matches = parent_seg[:, None] == seg_table[None, :]
    grand_seg = jnp.sum(jnp.where(matches, parents[None, :], 0), axis=1)
    grand_seg = jnp.where(parent_seg >= 0, grand_seg, -1)
    return (parent_seg, grand_seg)


def rope_tables(positions):
    half_size = HD // 2
    frequency = jnp.power(rope_base, -2.0 * jnp.arange(half_size, dtype=f32) / HD)
    angles = positions.astype(f32)[:, None] * frequency[None, :]
    return (jnp.cos(angles), jnp.sin(angles))


def rotate(flat, cosine, sine_table):
    values = flat.reshape(flat.shape[0], -1, HD)
    front = values[..., : HD // 2]
    latter = values[..., HD // 2 :]
    cos_rows = cosine[:, None, :]
    sin_rows = sine_table[:, None, :]
    return jnp.concatenate(
        [front * cos_rows - latter * sin_rows, latter * cos_rows + front * sin_rows], axis=-1
    ).reshape(flat.shape)


def norm_back(upstream, unit_rows, inv_rms):
    return inv_rms * (upstream - unit_rows * jnp.mean(upstream * unit_rows, axis=-1, keepdims=True))


def inverse_rms(rows):
    return lax.rsqrt(jnp.mean(rows * rows, axis=-1, keepdims=True) + norm_eps)


def heads_of(flat):
    return flat.reshape(flat.shape[0], -1, HD)


def side_by_side(left, right):
    count = (right if left is None else left).shape[0]
    parts = [None if t is None else heads_of(t) for t in (left, right)]
    blank = jnp.zeros_like(next(t for t in parts if t is not None))
    parts = [blank if t is None else t for t in parts]
    return jnp.concatenate(parts, axis=2).reshape(count, -1)


def fill_bias(query_ref, key_ref, bias_ref):
    @pl.when(pl.program_id(0) == 0)
    def _():
        seg, parent, grand, index = (query_ref[:, n : n + 1] for n in range(4))

        def fill(n, none):
            key_seg, key_index = key_ref[n, 0:1, :], key_ref[n, 1:2, :]
            allowed = (
                ((key_seg == seg) & (key_index <= index)) | (key_seg == parent) | (key_seg == grand)
            )
            bias_ref[n] = jnp.where(allowed, 0.0, far_below)
            return none

        lax.fori_loop(0, key_ref.shape[0], fill, 0)


def in_token_order(ref, row, chunks):
    height = ref.shape[0] // chunks
    return jnp.concatenate(
        [ref[pl.ds(pl.multiple_of((n ^ row) * height, 16), height), :] for n in range(chunks)], axis=0
    )


def keys_of(kv_ref, row, quarter, part, spans):
    count = kv_ref.shape[0] // spans
    block = kv_ref[pl.ds(part * count, count), quarter ^ row]
    return block.reshape(-1, 2 * HD)


def lower(top, change, skip):
    if skip == 0:
        return change(top)
    return jnp.concatenate([top[:skip], change(top[skip:])], axis=0)


def attend_kernel(row_ref, query_ref, key_ref, q_ref, kv_ref, out_ref, bias_ref):
    chunks, height = kv_ref.shape[1:3]
    spans = key_ref.shape[0] // chunks
    row = row_ref[0]
    fill_bias(query_ref, key_ref, bias_ref)
    q = in_token_order(q_ref, row, chunks)

    def span(part, carry):
        peak, total, mixed = carry
        keys = [keys_of(kv_ref, row, n, part, spans) for n in range(chunks)]
        scores = [
            dot(q[n * height :], keys[n], ((1,), (1,))) + bias_ref[n * spans + part, n * height :, :]
            for n in range(chunks)
        ]
        new_peak = peak
        for n in range(chunks):
            high = jnp.max(scores[n], axis=1, keepdims=True)
            new_peak = lower(new_peak, lambda p: jnp.maximum(p, high), n * height)
        factor = jnp.exp(peak - new_peak)
        total = total * factor
        mixed = mixed * factor
        for n in range(chunks):
            weights = jnp.exp(scores[n] - new_peak[n * height :])
            added = jnp.sum(weights, axis=1, keepdims=True)
            total = lower(total, lambda v: v + added, n * height)
            values = dot(weights.astype(bf16), keys[n])
            mixed = lower(mixed, lambda v: v + values, n * height)
        return new_peak, total, mixed

    start = (
        jnp.full((q.shape[0], 1), far_below, f32),
        jnp.zeros((q.shape[0], 1), f32),
        jnp.zeros((q.shape[0], 2 * HD), f32),
    )
    peak, total, mixed = span(0, start) if spans == 1 else lax.fori_loop(0, spans, span, start)
    lane = lax.broadcasted_iota(jnp.int32, mixed.shape, 1)
    result = jnp.where(lane < HD, peak + jnp.log(total), mixed / total)
    for n in range(chunks):
        out_ref[pl.ds(pl.multiple_of((n ^ row) * height, 16), height), :] = result[
            n * height : (n + 1) * height
        ]


def attend_back_kernel(
    row_ref, query_ref, key_ref, q_ref, kv_ref, out_ref, grad_ref, grad_q_ref, grad_kv_ref, bias_ref
):
    chunks, height = kv_ref.shape[1:3]
    spans = key_ref.shape[0] // chunks
    count = kv_ref.shape[0] // spans
    row = row_ref[0]
    fill_bias(query_ref, key_ref, bias_ref)
    q = in_token_order(q_ref, row, chunks)
    grad = in_token_order(grad_ref, row, chunks)
    saved = in_token_order(out_ref, row, chunks)
    log_total = saved[:, 0:1]
    delta = jnp.sum(grad.astype(f32) * saved, axis=1, keepdims=True)

    def span(part, grad_q):
        for n in range(chunks):
            skip = n * height
            keys = keys_of(kv_ref, row, n, part, spans)
            scores = dot(q[skip:], keys, ((1,), (1,))) + bias_ref[n * spans + part, skip:, :]
            probs = jnp.exp(scores - log_total[skip:])
            grad_probs = dot(grad[skip:], keys, ((1,), (1,)))
            grad_scores = (probs * (grad_probs - delta[skip:])).astype(bf16)
            added = dot(grad_scores, q[skip:], ((0,), (0,))) + dot(
                probs.astype(bf16), grad[skip:], ((0,), (0,))
            )
            grad_kv_ref[pl.ds(part * count, count), n ^ row] = added.astype(bf16).reshape(
                count, height, 2 * HD
            )
            more = dot(grad_scores, keys)
            grad_q = lower(grad_q, lambda v: v + more, skip)
        return grad_q

    start = jnp.zeros((q.shape[0], 2 * HD), f32)
    grad_q = span(0, start) if spans == 1 else lax.fori_loop(0, spans, span, start)
    for n in range(chunks):
        grad_q_ref[pl.ds(pl.multiple_of((n ^ row) * height, 16), height), :] = grad_q[
            n * height : (n + 1) * height
        ]


def attention_specs(queries, kv, query_info, key_info):
    heads = queries.shape[1] // (2 * HD)
    rows = pl.BlockSpec((queries.shape[0], 2 * HD), lambda h: (0, h))
    keys = pl.BlockSpec(kv.shape[:3] + (2 * HD,), lambda h: (0, 0, 0, h))
    fixed = [
        pl.BlockSpec(memory_space=pltpu.SMEM),
        pl.BlockSpec(query_info.shape, lambda h: (0, 0)),
        pl.BlockSpec(key_info.shape, lambda h: (0, 0, 0)),
    ]
    bias = pltpu.VMEM((key_info.shape[0], queries.shape[0], key_info.shape[2]), f32)
    params = pltpu.CompilerParams(vmem_limit_bytes=56 * 2**20)
    return heads, rows, keys, fixed, bias, params


def attend(row, query_info, key_info, queries, kv):
    heads, rows, keys, fixed, bias, params = attention_specs(queries, kv, query_info, key_info)
    return pl.pallas_call(
        attend_kernel,
        grid=(heads,),
        in_specs=fixed + [rows, keys],
        out_specs=rows,
        out_shape=jax.ShapeDtypeStruct(queries.shape, f32),
        scratch_shapes=[bias],
        compiler_params=params,
    )(row, query_info, key_info, queries, kv)


def attend_back(row, query_info, key_info, queries, kv, saved, grad):
    heads, rows, keys, fixed, bias, params = attention_specs(queries, kv, query_info, key_info)
    return pl.pallas_call(
        attend_back_kernel,
        grid=(heads,),
        in_specs=fixed + [rows, keys, rows, rows],
        out_specs=[rows, keys],
        out_shape=[
            jax.ShapeDtypeStruct(queries.shape, f32),
            jax.ShapeDtypeStruct(kv.shape, bf16),
        ],
        scratch_shapes=[bias],
        compiler_params=params,
    )(row, query_info, key_info, queries, kv, saved, grad)


def on_device(
    block_input,
    w_qkv,
    w_out,
    w_gate_up,
    w_down,
    norm_gains,
    cotangent,
    tok_seg,
    tok_pos,
    seg_parent,
):
    rows_n, b_n, x_n, c_n = (lax.axis_size(n) for n in ("za", "pb", "tx", "tc"))
    z, b, x, c = (lax.axis_index(n) for n in ("za", "pb", "tx", "tc"))
    shares = x_n * c_n
    plane = b_n * shares
    own, width = block_input.shape
    piece = width // plane

    def to_plane(array):
        blocks = array.reshape(-1, c_n, x_n, b_n, piece)
        return blocks.transpose(0, 3, 2, 1, 4).reshape(array.shape)

    def from_plane(array):
        blocks = array.reshape(-1, b_n, x_n, c_n, piece)
        return blocks.transpose(0, 3, 2, 1, 4).reshape(array.shape)

    def untangle(array, axis, index):
        count = array.shape[axis]
        for bit in range(count.bit_length() - 1):
            step = 1 << bit
            shape = array.shape[:axis] + (count // (2 * step), 2, step) + array.shape[axis + 1 :]
            flipped = jnp.flip(array.reshape(shape), axis + 1).reshape(array.shape)
            array = jnp.where((index >> bit) & 1 == 1, flipped, array)
        return array

    small = jnp.concatenate(
        [norm_gains.astype(f32).reshape(-1), tok_seg.astype(f32), tok_pos.astype(f32)]
    )
    small = jnp.stack([small] + [send_row(small, k) for k in range(1, rows_n)])
    across_b = [
        lax.ppermute(small, "pb", [(i, i ^ k) for i in range(b_n)]) for k in range(1, b_n)
    ]
    small = jnp.stack([small] + across_b, axis=1)
    gains = small[..., : 2 * norm_gains.shape[1]].reshape(rows_n, b_n, 2, -1)
    group = tok_seg.shape[0]
    seg_all = small[..., -2 * group : -group].astype(jnp.int32)
    pos_all = small[..., -group:].astype(jnp.int32)
    x_own = to_plane(block_input)
    x_group = row_gather(x_own)
    gains = untangle(untangle(gains, 0, z), 1, b).transpose(2, 0, 1, 3).reshape(2, width)
    gains = to_plane(gains)

    qkv_moved = turn(w_qkv)
    qkv_full = lax.all_gather(qkv_moved, PLANE, axis=1, tiled=True)
    out_moved = turn(after(w_out, x_group))
    out_full = lax.all_gather(out_moved, PLANE, axis=1, tiled=True)
    gate_up_moved = turn(after(w_gate_up, x_group))
    gate_up_full = lax.all_gather(gate_up_moved, PLANE, axis=1, tiled=True)
    down_moved = turn(after(w_down, gate_up_moved))
    down_full = lax.all_gather(down_moved, PLANE, axis=1, tiled=True)

    cot_own = to_plane(cotangent).astype(f32)
    grad_branch_f = row_gather(after((depth_scale * cot_own).astype(bf16), down_moved))

    pos_all = untangle(pos_all, 1, b).reshape(rows_n, b_n, x_n, c_n, own)
    seg_all = untangle(untangle(seg_all, 0, z), 1, b).reshape(pos_all.shape)
    index_all = jnp.arange(seg_all.size, dtype=jnp.int32).reshape(seg_all.shape)

    def for_group(array):
        array = lax.dynamic_slice_in_dim(array, b, 1, 1)
        array = lax.dynamic_slice_in_dim(array, x, 1, 2)
        return lax.dynamic_slice_in_dim(array, c, 1, 3).reshape(-1)

    def for_keys(array):
        array = untangle(array, 3, c).transpose(0, 3, 1, 2, 4)
        return array.reshape(-1, 8 * own)

    own_seg, own_index, pos_group = for_group(seg_all), for_group(index_all), for_group(pos_all)
    parent_seg, grand_seg = lineage(own_seg, seg_parent)
    query_info = jnp.stack([own_seg, parent_seg, grand_seg, own_index], axis=1)
    key_info = jnp.stack([for_keys(seg_all), for_keys(index_all)], axis=1)
    row = z.astype(jnp.int32).reshape(1)

    rows_a = x_group.astype(f32)
    normed_a = ((rows_a * inverse_rms(rows_a)) * gains[0]).astype(bf16)
    cosine, sine_table = rope_tables(pos_group)
    queries = (rotate(dot(normed_a, qkv_full[0]), cosine, sine_table)).astype(bf16) * bf16(HD**-0.5)
    keys = rotate(dot(normed_a, qkv_full[1]), cosine, sine_table).astype(bf16)
    values = dot(normed_a, qkv_full[2]).astype(bf16)
    queries = side_by_side(queries, None)
    kv = side_by_side(keys, values)
    chips = b_n * x_n
    kv = lax.all_to_all(jnp.broadcast_to(kv[None], (chips,) + kv.shape), CHIPS, 0, 0, tiled=True)
    kv = jnp.concatenate([kv, swap_core(kv)], axis=0).reshape(plane, rows_n, own, -1)
    saved = attend(row, query_info, key_info, queries, kv)
    attended = saved.reshape(rows_n * own, -1, 2, HD)[:, :, 1].reshape(rows_n * own, -1).astype(bf16)
    mid = x_own.astype(f32) + depth_scale * row_scatter(dot(attended, out_full))
    inv_f = inverse_rms(mid)
    unit_f = mid * inv_f
    normed_f = row_gather((unit_f * gains[1]).astype(bf16))
    gate = dot(normed_f, gate_up_full[0])
    up = dot(normed_f, gate_up_full[1])
    sig = jax.nn.sigmoid(gate)
    silu = gate * sig
    hidden = (silu * up).astype(bf16)
    output = mid + depth_scale * row_scatter(dot(hidden, down_full))

    grad_hidden = dot(grad_branch_f, down_full, ((1,), (1,)))
    grad_gate = (grad_hidden * up * sig * (1.0 + gate * (1.0 - sig))).astype(bf16)
    grad_up = (grad_hidden * silu).astype(bf16)
    grad_normed_f = row_scatter(
        dot(grad_gate, gate_up_full[0], ((1,), (1,))) + dot(grad_up, gate_up_full[1], ((1,), (1,)))
    )
    gain_f = jnp.sum(grad_normed_f * unit_f, axis=0)
    grad_mid = cot_own + norm_back(grad_normed_f * gains[1], unit_f, inv_f)
    grad_branch_a = row_gather((depth_scale * grad_mid).astype(bf16))

    grad_gate_up = jnp.stack([plane_scatter(normed_f, g) for g in (grad_gate, grad_up)])
    grad_down = plane_scatter(grad_branch_f, hidden)
    grad_out = plane_scatter(grad_branch_a, attended)
    grad_gate_up = turn(grad_gate_up).astype(f32)
    grad_down = turn(grad_down).astype(f32).T
    grad_out = turn(grad_out).astype(f32).T

    grad_attended = dot(grad_branch_a, out_full, ((1,), (1,))).astype(bf16)
    grad_q, grad_kv = attend_back(
        row, query_info, key_info, queries, kv, saved, side_by_side(None, grad_attended)
    )
    grad_kv = grad_kv.reshape(2, chips, rows_n * own, -1)
    grad_kv = (grad_kv[0].astype(f32) + swap_core(grad_kv[1]).astype(f32)).astype(bf16)
    grad_kv = lax.all_to_all(grad_kv, CHIPS, 0, 0, tiled=True)
    grad_kv = jnp.sum(grad_kv.astype(f32), axis=0).reshape(rows_n * own, -1, 2, HD)
    flat = (rows_n * own, w_qkv.shape[2])
    grad_q = grad_q.reshape(rows_n * own, -1, 2, HD)[:, :, 0].reshape(flat) * HD**-0.5
    grad_q = rotate(grad_q, cosine, -sine_table).astype(bf16)
    grad_k = rotate(grad_kv[:, :, 0].reshape(flat), cosine, -sine_table).astype(bf16)
    grad_v = grad_kv[:, :, 1].reshape(flat).astype(bf16)
    grad_normed_a = row_scatter(
        dot(grad_q, qkv_full[0], ((1,), (1,)))
        + dot(grad_k, qkv_full[1], ((1,), (1,)))
        + dot(grad_v, qkv_full[2], ((1,), (1,)))
    )
    grad_qkv = jnp.stack(
        [plane_scatter(normed_a, g) for g in (grad_q, grad_k, grad_v)]
    )
    grad_qkv = turn(grad_qkv).astype(f32)
    rows_own = x_own.astype(f32)
    inv_a = inverse_rms(rows_own)
    unit_a = rows_own * inv_a
    gain_a = jnp.sum(grad_normed_a * unit_a, axis=0)
    grad_input = grad_mid + norm_back(grad_normed_a * gains[0], unit_a, inv_a)
    gain_sum = from_plane(jnp.stack([gain_a, gain_f]))
    for axis, count in (("tc", c_n), ("tx", x_n), ("pb", b_n), ("za", rows_n)):
        for bit in range(count.bit_length() - 1):
            gain_sum = gain_sum + lax.ppermute(
                gain_sum, axis, [(i, i ^ (1 << bit)) for i in range(count)]
            )
    part = width // (rows_n * plane)
    place = ((z * b_n + b) * x_n + x) * c_n + c
    grad_gains = lax.dynamic_slice_in_dim(gain_sum, place * part, part, 1)
    return (from_plane(output), from_plane(grad_input), grad_qkv, grad_out, grad_gate_up, grad_down, grad_gains)


def solution(mesh):
    shares = mesh.shape["tensor"]
    devices = mesh.devices.reshape(shares, -1, shares // 2, 2)
    fine = Mesh(devices, ("za", "pb", "tx", "tc"))
    dp, tensor = ("za", "pb"), ("tx", "tc")
    in_specs = (
        P(dp + tensor, None),
        P(None, dp, tensor),
        P(tensor, dp),
        P(None, dp, tensor),
        P(tensor, dp),
        P(None, dp),
        P(dp + tensor, None),
        P(dp),
        P(dp),
        P(),
    )
    out_specs = (
        P(dp + tensor, None),
        P(dp + tensor, None),
        P(None, dp, tensor),
        P(tensor, dp),
        P(None, dp, tensor),
        P(tensor, dp),
        P(None, dp + tensor),
    )
    return jax.shard_map(
        on_device, mesh=fine, in_specs=in_specs, out_specs=out_specs, check_vma=False
    )
```

time: 2720 us -> 1060 us (0.39)
  the two profiles are of different devices: /device:TPU:1 before, /device:TPU:2 now
where the time goes in v1:
time: 1060 us; the launch traced here: 1040 us
  waiting for transfers between devices  464 us (44%)
  starting transfers between devices  189 us (18%)
  local copies, waits for them, and re-layouts  157 us (15%)
  matrix products  99 us (9%)
  other arithmetic  76.9 us (7%)
  Pallas kernels  39.2 us (4%)
  between operations  15.6 us (1%)
    ppermute x27, waiting for transfers between devices, send_row(): lax.ppermute(array, ROW, [(i, i ^ distance) for i in range(lax.axis_size(...  167 us
    ppermute x8, waiting for transfers between devices, turn(): return lax.ppermute(array, ('za', 'tx', 'tc'), pairs)  162 us
    dot_general x28, matrix products, dot(): return lax.dot_general(a, b, (dims, ((), ())), preferred_element_type=f32)  99 us
    ppermute x8, starting transfers between devices, turn(): return lax.ppermute(array, ('za', 'tx', 'tc'), pairs)  64.4 us
    all_to_all x7, waiting for transfers between devices, plane_scatter(): total = lax.all_to_all(total, CHIPS, 0, 0, tiled=True)  54.6 us
    ppermute x27, starting transfers between devices, send_row(): lax.ppermute(array, ROW, [(i, i ^ distance) for i in range(lax.axis_size(...  53 us
    all_to_all x7, starting transfers between devices, plane_scatter(): total = lax.all_to_all(total, CHIPS, 0, 0, tiled=True)  35.5 us
    all_to_all x1, waiting for transfers between devices, on_device(): lax.all_to_all(jnp.broadcast_to(kv[None], (chips,) + kv.shape), CHIPS, 0,...  28.8 us
  transfers between devices with their start and end apart: 63, of which 31 were waited for; matrix products, arithmetic and copies ran while one was open for 29% of the time, Pallas kernels for 4%

profile of v1, /device:TPU:2, one launch (start us, length us, event | category | flops | bytes accessed | tf_op | source)
XLA Modules:
  0.0 1041.0 jit_solution(833915006431985174)
XLA Ops:
  10.7 39.1 %collective-permute-done.7 = bf16[3,288,576]{2,1,0:T(8,128)(2,1)S(1)} collective-permute-done((bf16[3,288,576]{2,1,0:T(8,128)(2,1)}, bf16[3,288,576]{2,1,0:T(8,128)(2,1)S(1)}, u32[]{:S(2)}, u32[]{:S(2)}) %collective-permute-start.7) | collective-permute-done | bytes 995360 | tf_op jit(solution)/shard_map/ppermute | solution.py:76
  62.6 18.8 %collective-permute-done.5 = bf16[80,2304]{1,0:T(8,128)(2,1)S(1)} collective-permute-done((bf16[80,2304]{1,0:T(8,128)(2,1)S(1)}, bf16[80,2304]{1,0:T(8,128)(2,1)S(1)}, u32[]{:S(2)}, u32[]{:S(2)}) %collective-permute-start.5) | collective-permute-done | bytes 368672 | tf_op jit(solution)/shard_map/ppermute | solution.py:29
  82.3 12.9 %collective-permute-start.9 = (bf16[576,288]{0,1:T(8,128)(2,1)}, bf16[576,288]{0,1:T(8,128)(2,1)}, u32[]{:S(2)}, u32[]{:S(2)}) collective-permute-start(bf16[576,288]{0,1:T(8,128)(2,1)} %param.12), channel_id=1, source_target_pairs={{0,0},{1,16},{2,8},{3,24},{8,2},{9,18},{10,10},{11,26},{16,1},{17,... | collective-permute-start | bytes 995336 | tf_op jit(solution)/shard_map/ppermute | solution.py:76
  95.2 56.1 %collective-permute-done.9 = bf16[576,288]{0,1:T(8,128)(2,1)} collective-permute-done((bf16[576,288]{0,1:T(8,128)(2,1)}, bf16[576,288]{0,1:T(8,128)(2,1)}, u32[]{:S(2)}, u32[]{:S(2)}) %collective-permute-start.9) | collective-permute-done | bytes 331808 | tf_op jit(solution)/shard_map/ppermute | solution.py:76
  153.3 29.0 %collective-permute-done.16 = bf16[2,288,1440]{2,1,0:T(8,128)(2,1)} collective-permute-done((bf16[2,288,1440]{2,1,0:T(8,128)(2,1)}, bf16[2,288,1440]{2,1,0:T(8,128)(2,1)}, u32[]{:S(2)}, u32[]{:S(2)}) %collective-permute-start.16) | collective-permute-done | bytes 1658912 | tf_op jit(solution)/shard_map/ppermute | solution.py:76
  186.9 11.6 %collective-permute-done.17 = bf16[1440,288]{0,1:T(8,128)(2,1)} collective-permute-done((bf16[1440,288]{0,1:T(8,128)(2,1)}, bf16[1440,288]{0,1:T(8,128)(2,1)}, u32[]{:S(2)}, u32[]{:S(2)}) %collective-permute-start.17) | collective-permute-done | bytes 829472 | tf_op jit(solution)/shard_map/ppermute | solution.py:76
  240.3 7.8 all-to-all-start
  258.8 28.8 %all-to-all-done = bf16[4,320,1152]{2,1,0:T(8,128)(2,1)S(1)} async-done(((bf16[4,320,1152]{2,1,0:T(8,128)(2,1)}), bf16[4,320,1152]{2,1,0:T(8,128)(2,1)S(1)}, u32[]{:S(2)}, u32[]{:S(2)}) %all-to-all-start) | async-done | bytes 2949152 | tf_op jit(solution)/shard_map/all_to_all | solution.py:381
  322.3 5.5 collective-permute-done.21
  329.5 16.5 %collective-permute-done.22 = bf16[80,2304]{1,0:T(8,128)(2,1)S(1)} collective-permute-done((bf16[80,2304]{1,0:T(8,128)(2,1)}, bf16[80,2304]{1,0:T(8,128)(2,1)S(1)}, u32[]{:S(2)}, u32[]{:S(2)}) %collective-permute-start.22) | collective-permute-done | bytes 368672 | tf_op jit(solution)/shard_map/ppermute | solution.py:29
  351.0 5.0 pad_maximum_fusion
  356.1 16.2 %shard_map.153.out_ref = f32[320,1152]{1,0:T(8,128)} custom-call(s32[1]{0:T(128)} %bitcast.1.row_ref, s32[320,4]{1,0:T(8,128)} %copy.164.query_ref, s32[4,2,640]{2,1,0:T(2,128)} %pad_add_fusion.key_ref, bf16[320,1152]{1,0:T(8,128)(2,1)} %copy.165.q_ref, bf16[8,4,80,1152]{3,2,1,0:T(8,128)(2,1)} %bitcast.195), custom_call_target="tpu_custom_call" | custom-call | tf_op jit(solution)/shard_map/pallas_call | solution.py:261
  390.5 5.4 collective-permute-done.10
  395.9 12.6 %collective-permute-done.11 = bf16[80,2304]{1,0:T(8,128)(2,1)S(1)} collective-permute-done((bf16[80,2304]{1,0:T(8,128)(2,1)}, bf16[80,2304]{1,0:T(8,128)(2,1)S(1)}, u32[]{:S(2)}, u32[]{:S(2)}) %collective-permute-start.11) | collective-permute-done | bytes 368672 | tf_op jit(solution)/shard_map/ppermute | solution.py:29
  411.3 5.5 collective-permute-start.13
  419.3 7.2 fusion.72
  429.3 15.7 %collective-permute-done.14 = bf16[80,2304]{1,0:T(8,128)(2,1)S(1)} collective-permute-done((bf16[80,2304]{1,0:T(8,128)(2,1)S(1)}, bf16[80,2304]{1,0:T(8,128)(2,1)S(1)}, u32[]{:S(2)}, u32[]{:S(2)}) %collective-permute-start.14) | collective-permute-done | bytes 368672 | tf_op jit(solution)/shard_map/ppermute | solution.py:29
  445.1 5.7 fusion.3
  458.9 5.6 fusion.69
  464.6 4.8 collective-permute-start.24
  477.7 8.1 collective-permute-done.24
  488.8 9.0 collective-permute-done.25
  502.2 26.3 %collective-permute-done.19 = bf16[80,2304]{1,0:T(8,128)(2,1)S(1)} collective-permute-done((bf16[80,2304]{1,0:T(8,128)(2,1)S(1)}, bf16[80,2304]{1,0:T(8,128)(2,1)S(1)}, u32[]{:S(2)}, u32[]{:S(2)}) %collective-permute-start.19) | collective-permute-done | bytes 368672 | tf_op jit(solution)/shard_map/ppermute | solution.py:29
  544.5 16.9 %collective-permute-done.28 = bf16[80,2304]{1,0:T(8,128)(2,1)S(1)} collective-permute-done((bf16[80,2304]{1,0:T(8,128)(2,1)S(1)}, bf16[80,2304]{1,0:T(8,128)(2,1)S(1)}, u32[]{:S(2)}, u32[]{:S(2)}) %collective-permute-start.28) | collective-permute-done | bytes 368672 | tf_op jit(solution)/shard_map/ppermute | solution.py:29
  572.5 23.1 %shard_map.154 = (f32[320,1152]{1,0:T(8,128)}, bf16[8,4,80,1152]{3,2,1,0:T(8,128)(2,1)}) custom-call(s32[1]{0:T(128)} %bitcast.1.row_ref, s32[320,4]{1,0:T(8,128)} %copy.164.query_ref, s32[4,2,640]{2,1,0:T(2,128)} %pad_add_fusion.key_ref, bf16[320,1152]{1,0:T(8,128)(2,1)} %copy.165.q_ref, bf16[8,4,80,1152]{3,2,1,0:T(8,128)(2,1)} %bitcast.196, ...), custom_call_target="tpu_custom_call" | custom-call | tf_op jit(solution)/shard_map/pallas_call | solution.py:274
  595.5 5.8 fusion.62
  605.7 5.2 all-to-all-start.5
  611.0 5.7 add_convert_fusion
  616.7 5.7 copy.194
  622.3 6.7 all-to-all-done.5
  651.3 22.5 %all-to-all-done.8 = bf16[4,288,1440]{2,1,0:T(8,128)(2,1)S(1)} async-done(((bf16[4,288,1440]{2,1,0:T(8,128)(2,1)}), bf16[4,288,1440]{2,1,0:T(8,128)(2,1)S(1)}, u32[]{:S(2)}, u32[]{:S(2)}) %all-to-all-start.8) | async-done | bytes 3317792 | tf_op jit(solution)/shard_map/all_to_all | solution.py:66
  673.8 5.2 all-to-all-start.1
  679.0 5.3 convolution_convert_fusion.1
  692.0 20.0 %all-to-all-done.1 = bf16[4,320,1152]{2,1,0:T(8,128)(2,1)} async-done(((bf16[4,320,1152]{2,1,0:T(8,128)(2,1)}), bf16[4,320,1152]{2,1,0:T(8,128)(2,1)}, u32[]{:S(2)}, u32[]{:S(2)}) %all-to-all-start.1) | async-done | bytes 2949152 | tf_op jit(solution)/shard_map/all_to_all | solution.py:419
  742.6 6.3 add_convert_fusion.1
  748.9 5.7 copy.192
  762.6 5.0 all-to-all-start.7
  786.0 20.8 %all-to-all-done.7 = bf16[4,288,1440]{2,1,0:T(8,128)(2,1)} async-done(((bf16[4,288,1440]{2,1,0:T(8,128)(2,1)}), bf16[4,288,1440]{2,1,0:T(8,128)(2,1)}, u32[]{:S(2)}, u32[]{:S(2)}) %all-to-all-start.7) | async-done | bytes 3317792 | tf_op jit(solution)/shard_map/all_to_all | solution.py:66
  806.8 4.9 all-to-all-start.2
  815.0 5.6 fusion.71
  828.9 5.0 all-to-all-start.3
  851.1 6.5 all-to-all-start.4
  857.5 15.7 %collective-permute-done.32 = bf16[80,2304]{1,0:T(8,128)(2,1)} collective-permute-done((bf16[80,2304]{1,0:T(8,128)(2,1)}, bf16[80,2304]{1,0:T(8,128)(2,1)}, u32[]{:S(2)}, u32[]{:S(2)}) %collective-permute-start.32) | collective-permute-done | bytes 368672 | tf_op jit(solution)/shard_map/ppermute | solution.py:29
  891.3 11.1 %collective-permute-start.44 = (bf16[288,1440]{1,0:T(8,128)(2,1)}, bf16[288,1440]{1,0:T(8,128)(2,1)}, u32[]{:S(2)}, u32[]{:S(2)}) collective-permute-start(bf16[288,1440]{1,0:T(8,128)(2,1)} %reduce_sum.191), channel_id=1, source_target_pairs={{0,0},{1,16},{2,8},{3,24},{8,2},{9,18},{10,10},{11,26},{16,1},{17,... | collective-permute-start | bytes 2488328 | tf_op jit(solution)/shard_map/ppermute | solution.py:76
  914.2 18.3 %collective-permute-start.48 = (f32[2,2304]{1,0:T(2,128)S(1)}, f32[2,2304]{1,0:T(2,128)S(1)}, u32[]{:S(2)}, u32[]{:S(2)}) collective-permute-start(f32[2,2304]{1,0:T(2,128)S(1)} %add.309), channel_id=1, source_target_pairs={{0,8},{8,0},{16,24},{24,16},{1,9},{9,1},{17,25},{25,17},{2,10},{10... | collective-permute-start | bytes 55304 | tf_op jit(solution)/shard_map/ppermute | solution.py:443
  932.5 28.3 %collective-permute-done.48 = f32[2,2304]{1,0:T(2,128)S(1)} collective-permute-done((f32[2,2304]{1,0:T(2,128)S(1)}, f32[2,2304]{1,0:T(2,128)S(1)}, u32[]{:S(2)}, u32[]{:S(2)}) %collective-permute-start.48) | collective-permute-done | bytes 18464 | tf_op jit(solution)/shard_map/ppermute | solution.py:443
  967.6 26.3 %collective-permute-start.37 = (bf16[3,288,576]{2,1,0:T(8,128)(2,1)}, bf16[3,288,576]{2,1,0:T(8,128)(2,1)}, u32[]{:S(2)}, u32[]{:S(2)}) collective-permute-start(bf16[3,288,576]{2,1,0:T(8,128)(2,1)} %pad_maximum_fusion.4), channel_id=1, source_target_pairs={{0,0},{1,16},{2,8},{3,24},{8,2},{9,18},{10,10},{11,26},{16,1},{17,... | collective-permute-start | bytes 2985992 | tf_op jit(solution)/shard_map/ppermute | solution.py:76
  1004.7 26.6 %collective-permute-done.37 = bf16[3,288,576]{2,1,0:T(8,128)(2,1)} collective-permute-done((bf16[3,288,576]{2,1,0:T(8,128)(2,1)}, bf16[3,288,576]{2,1,0:T(8,128)(2,1)}, u32[]{:S(2)}, u32[]{:S(2)}) %collective-permute-start.37) | collective-permute-done | bytes 995360 | tf_op jit(solution)/shard_map/ppermute | solution.py:76
  (430 shorter events, 363.8 us)
Async XLA Ops:
  7.2 205.2 %all-gather.5.cloned.1.call-start = ((), (), s32[]{:S(2)}) async-start(), calls=%async_computation.9 | async-start | bytes 9953280 | tf_op jit(solution)/shard_map/all_gather | solution.py:342
  7.2 42.6 %collective-permute-start.7 = (bf16[3,288,576]{2,1,0:T(8,128)(2,1)}, bf16[3,288,576]{2,1,0:T(8,128)(2,1)S(1)}, u32[]{:S(2)}, u32[]{:S(2)}) collective-permute-start(bf16[3,288,576]{2,1,0:T(8,128)(2,1)} %param.11), channel_id=1, source_target_pairs={{0,0},{1,16},{2,8},{3,24},{8,2},{9,18},{10,10},{11,26},{16,1},{17,... | collective-permute-start | bytes 2985992 | tf_op jit(solution)/shard_map/ppermute | solution.py:76
  50.8 323.4 %all-gather.7.cloned.1.call-start = ((), (), s32[]{:S(2)}) async-start(), calls=%async_computation.10 | async-start | bytes 3317760 | tf_op jit(solution)/shard_map/all_gather | solution.py:344
  53.5 27.9 %collective-permute-start.5 = (bf16[80,2304]{1,0:T(8,128)(2,1)S(1)}, bf16[80,2304]{1,0:T(8,128)(2,1)S(1)}, u32[]{:S(2)}, u32[]{:S(2)}) collective-permute-start(bf16[80,2304]{1,0:T(8,128)(2,1)S(1)} %reshape.533), channel_id=1, source_target_pairs={{0,16},{8,24},{16,0},{24,8},{1,17},{9,25},{17,1},{25,9},{2,18},{10... | collective-permute-start | bytes 1105928 | tf_op jit(solution)/shard_map/ppermute | solution.py:29
  53.6 27.9 %collective-permute-start.6 = (bf16[80,2304]{1,0:T(8,128)(2,1)S(1)}, bf16[80,2304]{1,0:T(8,128)(2,1)S(1)}, u32[]{:S(2)}, u32[]{:S(2)}) collective-permute-start(bf16[80,2304]{1,0:T(8,128)(2,1)S(1)} %reshape.533), channel_id=1, source_target_pairs={{0,24},{8,16},{16,8},{24,0},{1,25},{9,17},{17,9},{25,1},{2,26},{10... | collective-permute-start | bytes 1105928 | tf_op jit(solution)/shard_map/ppermute | solution.py:29
  82.3 69.0 %collective-permute-start.9 = (bf16[576,288]{0,1:T(8,128)(2,1)}, bf16[576,288]{0,1:T(8,128)(2,1)}, u32[]{:S(2)}, u32[]{:S(2)}) collective-permute-start(bf16[576,288]{0,1:T(8,128)(2,1)} %param.12), channel_id=1, source_target_pairs={{0,0},{1,16},{2,8},{3,24},{8,2},{9,18},{10,10},{11,26},{16,1},{17,... | collective-permute-start | bytes 995336 | tf_op jit(solution)/shard_map/ppermute | solution.py:76
  151.3 268.0 %all-gather.11.cloned.1.call-start = ((), (), s32[]{:S(2)}) async-start(), calls=%async_computation.12 | async-start | bytes 7962624 | tf_op jit(solution)/shard_map/all_gather | solution.py:348
  151.4 30.9 %collective-permute-start.16 = (bf16[2,288,1440]{2,1,0:T(8,128)(2,1)}, bf16[2,288,1440]{2,1,0:T(8,128)(2,1)}, u32[]{:S(2)}, u32[]{:S(2)}) collective-permute-start(bf16[2,288,1440]{2,1,0:T(8,128)(2,1)} %param.13), channel_id=1, source_target_pairs={{0,0},{1,16},{2,8},{3,24},{8,2},{9,18},{10,10},{11,26},{16,1},{17,... | collective-permute-start | bytes 4976648 | tf_op jit(solution)/shard_map/ppermute | solution.py:76
  198.6 246.5 %all-gather.9.cloned.1.call-start = ((), (), s32[]{:S(2)}) async-start(), calls=%async_computation.11 | async-start | bytes 15925248 | tf_op jit(solution)/shard_map/all_gather | solution.py:346
  240.3 47.4 %all-to-all-start = ((bf16[4,320,1152]{2,1,0:T(8,128)(2,1)}), bf16[4,320,1152]{2,1,0:T(8,128)(2,1)S(1)}, u32[]{:S(2)}, u32[]{:S(2)}) async-start(bf16[4,320,1152]{2,1,0:T(8,128)(2,1)} %broadcast_in_dim.28), calls=%async_computation | async-start | bytes 5898240 | tf_op jit(solution)/shard_map/all_to_all | solution.py:381
  287.7 63.3 %collective-permute-start.8 = (bf16[4,320,1152]{2,1,0:T(8,128)(2,1)S(1)}, bf16[4,320,1152]{2,1,0:T(8,128)(2,1)}, u32[]{:S(2)}, u32[]{:S(2)}) collective-permute-start(bf16[4,320,1152]{2,1,0:T(8,128)(2,1)S(1)} %all-to-all-done), channel_id=1, source_target_pairs={{0,1},{1,0},{2,3},{3,2},{4,5},{5,4},{6,7},{7,6},{8,9},{9,8},{10,11... | collective-permute-start | bytes 8847368 | tf_op jit(solution)/shard_map/ppermute | solution.py:33
  317.6 28.4 %collective-permute-start.22 = (bf16[80,2304]{1,0:T(8,128)(2,1)}, bf16[80,2304]{1,0:T(8,128)(2,1)S(1)}, u32[]{:S(2)}, u32[]{:S(2)}) collective-permute-start(bf16[80,2304]{1,0:T(8,128)(2,1)} %multiply_convert_fusion.5), channel_id=1, source_target_pairs={{0,16},{8,24},{16,0},{24,8},{1,17},{9,25},{17,1},{25,9},{2,18},{10... | collective-permute-start | bytes 1105928 | tf_op jit(solution)/shard_map/ppermute | solution.py:29
  321.8 62.6 %collective-permute-start.23 = (bf16[80,2304]{1,0:T(8,128)(2,1)}, bf16[80,2304]{1,0:T(8,128)(2,1)}, u32[]{:S(2)}, u32[]{:S(2)}) collective-permute-start(bf16[80,2304]{1,0:T(8,128)(2,1)} %multiply_convert_fusion.5), channel_id=1, source_target_pairs={{0,24},{8,16},{16,8},{24,0},{1,25},{9,17},{17,9},{25,1},{2,26},{10... | collective-permute-start | bytes 1105928 | tf_op jit(solution)/shard_map/ppermute | solution.py:29
  380.0 28.6 %collective-permute-start.11 = (bf16[80,2304]{1,0:T(8,128)(2,1)}, bf16[80,2304]{1,0:T(8,128)(2,1)S(1)}, u32[]{:S(2)}, u32[]{:S(2)}) collective-permute-start(bf16[80,2304]{1,0:T(8,128)(2,1)} %get-tuple-element.57), channel_id=1, source_target_pairs={{0,16},{8,24},{16,0},{24,8},{1,17},{9,25},{17,1},{25,9},{2,18},{10... | collective-permute-start | bytes 1105928 | tf_op jit(solution)/shard_map/ppermute | solution.py:29
  383.1 25.5 %collective-permute-start.12 = (bf16[80,2304]{1,0:T(8,128)(2,1)}, bf16[80,2304]{1,0:T(8,128)(2,1)}, u32[]{:S(2)}, u32[]{:S(2)}) collective-permute-start(bf16[80,2304]{1,0:T(8,128)(2,1)} %get-tuple-element.56), channel_id=1, source_target_pairs={{0,24},{8,16},{16,8},{24,0},{1,25},{9,17},{17,9},{25,1},{2,26},{10... | collective-permute-start | bytes 1105928 | tf_op jit(solution)/shard_map/ppermute | solution.py:29
  416.8 28.2 %collective-permute-start.14 = (bf16[80,2304]{1,0:T(8,128)(2,1)S(1)}, bf16[80,2304]{1,0:T(8,128)(2,1)S(1)}, u32[]{:S(2)}, u32[]{:S(2)}) collective-permute-start(bf16[80,2304]{1,0:T(8,128)(2,1)S(1)} %multiply_convert_fusion.6), channel_id=1, source_target_pairs={{0,16},{8,24},{16,0},{24,8},{1,17},{9,25},{17,1},{25,9},{2,18},{10... | collective-permute-start | bytes 1105928 | tf_op jit(solution)/shard_map/ppermute | solution.py:29
  417.8 27.3 %collective-permute-start.15 = (bf16[80,2304]{1,0:T(8,128)(2,1)S(1)}, bf16[80,2304]{1,0:T(8,128)(2,1)S(1)}, u32[]{:S(2)}, u32[]{:S(2)}) collective-permute-start(bf16[80,2304]{1,0:T(8,128)(2,1)S(1)} %multiply_convert_fusion.6), channel_id=1, source_target_pairs={{0,24},{8,16},{16,8},{24,0},{1,25},{9,17},{17,9},{25,1},{2,26},{10... | collective-permute-start | bytes 1105928 | tf_op jit(solution)/shard_map/ppermute | solution.py:29
  469.5 28.3 %collective-permute-start.25 = (bf16[80,2304]{1,0:T(8,128)(2,1)S(1)}, bf16[80,2304]{1,0:T(8,128)(2,1)S(1)}, u32[]{:S(2)}, u32[]{:S(2)}) collective-permute-start(bf16[80,2304]{1,0:T(8,128)(2,1)S(1)} %get-tuple-element.51), channel_id=1, source_target_pairs={{0,16},{8,24},{16,0},{24,8},{1,17},{9,25},{17,1},{25,9},{2,18},{10... | collective-permute-start | bytes 1105928 | tf_op jit(solution)/shard_map/ppermute | solution.py:29
  470.4 27.3 %collective-permute-start.26 = (bf16[80,2304]{1,0:T(8,128)(2,1)S(1)}, bf16[80,2304]{1,0:T(8,128)(2,1)S(1)}, u32[]{:S(2)}, u32[]{:S(2)}) collective-permute-start(bf16[80,2304]{1,0:T(8,128)(2,1)S(1)} %get-tuple-element.50), channel_id=1, source_target_pairs={{0,24},{8,16},{16,8},{24,0},{1,25},{9,17},{17,9},{25,1},{2,26},{10... | collective-permute-start | bytes 1105928 | tf_op jit(solution)/shard_map/ppermute | solution.py:29
  474.7 27.5 %collective-permute-start.18 = (bf16[80,2304]{1,0:T(8,128)(2,1)S(1)}, bf16[80,2304]{1,0:T(8,128)(2,1)S(1)}, u32[]{:S(2)}, u32[]{:S(2)}) collective-permute-start(bf16[80,2304]{1,0:T(8,128)(2,1)S(1)} %get-tuple-element.52), channel_id=1, source_target_pairs={{0,8},{8,0},{16,24},{24,16},{1,9},{9,1},{17,25},{25,17},{2,10},{10... | collective-permute-start | bytes 1105928 | tf_op jit(solution)/shard_map/ppermute | solution.py:29
  475.8 52.7 %collective-permute-start.19 = (bf16[80,2304]{1,0:T(8,128)(2,1)S(1)}, bf16[80,2304]{1,0:T(8,128)(2,1)S(1)}, u32[]{:S(2)}, u32[]{:S(2)}) collective-permute-start(bf16[80,2304]{1,0:T(8,128)(2,1)S(1)} %get-tuple-element.54), channel_id=1, source_target_pairs={{0,16},{8,24},{16,0},{24,8},{1,17},{9,25},{17,1},{25,9},{2,18},{10... | collective-permute-start | bytes 1105928 | tf_op jit(solution)/shard_map/ppermute | solution.py:29
  485.8 42.8 %collective-permute-start.20 = (bf16[80,2304]{1,0:T(8,128)(2,1)S(1)}, bf16[80,2304]{1,0:T(8,128)(2,1)S(1)}, u32[]{:S(2)}, u32[]{:S(2)}) collective-permute-start(bf16[80,2304]{1,0:T(8,128)(2,1)S(1)} %get-tuple-element.53), channel_id=1, source_target_pairs={{0,24},{8,16},{16,8},{24,0},{1,25},{9,17},{17,9},{25,1},{2,26},{10... | collective-permute-start | bytes 1105928 | tf_op jit(solution)/shard_map/ppermute | solution.py:29
  534.6 26.7 %collective-permute-start.28 = (bf16[80,2304]{1,0:T(8,128)(2,1)S(1)}, bf16[80,2304]{1,0:T(8,128)(2,1)S(1)}, u32[]{:S(2)}, u32[]{:S(2)}) collective-permute-start(bf16[80,2304]{1,0:T(8,128)(2,1)S(1)} %get-tuple-element.24), channel_id=1, source_target_pairs={{0,16},{8,24},{16,0},{24,8},{1,17},{9,25},{17,1},{25,9},{2,18},{10... | collective-permute-start | bytes 1105928 | tf_op jit(solution)/shard_map/ppermute | solution.py:29
  535.6 25.8 %collective-permute-start.29 = (bf16[80,2304]{1,0:T(8,128)(2,1)S(1)}, bf16[80,2304]{1,0:T(8,128)(2,1)S(1)}, u32[]{:S(2)}, u32[]{:S(2)}) collective-permute-start(bf16[80,2304]{1,0:T(8,128)(2,1)S(1)} %get-tuple-element.24), channel_id=1, source_target_pairs={{0,24},{8,16},{16,8},{24,0},{1,25},{9,17},{17,9},{25,1},{2,26},{10... | collective-permute-start | bytes 1105928 | tf_op jit(solution)/shard_map/ppermute | solution.py:29
  540.8 70.1 %collective-permute-start.43 = (bf16[1152,1440]{0,1:T(8,128)(2,1)}, bf16[1152,1440]{0,1:T(8,128)(2,1)}, u32[]{:S(2)}, u32[]{:S(2)}) collective-permute-start(bf16[1152,1440]{0,1:T(8,128)(2,1)} %convolution_convert_fusion), channel_id=1, source_target_pairs={{0,1},{1,0},{2,3},{3,2},{4,5},{5,4},{6,7},{7,6},{8,9},{9,8},{10,11... | collective-permute-start | bytes 9953288 | tf_op jit(solution)/shard_map/ppermute | solution.py:33
  569.3 32.4 %collective-permute-start.38 = (bf16[1152,576]{0,1:T(8,128)(2,1)}, bf16[1152,576]{0,1:T(8,128)(2,1)}, u32[]{:S(2)}, u32[]{:S(2)}) collective-permute-start(bf16[1152,576]{0,1:T(8,128)(2,1)} %convolution_convert_fusion.3), channel_id=1, source_target_pairs={{0,1},{1,0},{2,3},{3,2},{4,5},{5,4},{6,7},{7,6},{8,9},{9,8},{10,11... | collective-permute-start | bytes 3981320 | tf_op jit(solution)/shard_map/ppermute | solution.py:33
  601.3 45.8 %collective-permute-start.30 = (bf16[4,320,1152]{2,1,0:T(8,128)(2,1)}, bf16[4,320,1152]{2,1,0:T(8,128)(2,1)}, u32[]{:S(2)}, u32[]{:S(2)}) collective-permute-start(bf16[4,320,1152]{2,1,0:T(8,128)(2,1)} %bitcast.42), channel_id=1, source_target_pairs={{0,1},{1,0},{2,3},{3,2},{4,5},{5,4},{6,7},{7,6},{8,9},{9,8},{10,11... | collective-permute-start | bytes 8847368 | tf_op jit(solution)/shard_map/ppermute | solution.py:33
  605.7 23.3 %all-to-all-start.5 = ((bf16[4,288,576]{2,1,0:T(8,128)(2,1)}), bf16[4,288,576]{2,1,0:T(8,128)(2,1)S(1)}, u32[]{:S(2)}, u32[]{:S(2)}) async-start(bf16[4,288,576]{2,1,0:T(8,128)(2,1)} %bitcast.62), calls=%async_computation.5 | async-start | bytes 2949120 | tf_op jit(solution)/shard_map/all_to_all | solution.py:66
  630.1 43.6 %all-to-all-start.8 = ((bf16[4,288,1440]{2,1,0:T(8,128)(2,1)}), bf16[4,288,1440]{2,1,0:T(8,128)(2,1)S(1)}, u32[]{:S(2)}, u32[]{:S(2)}) async-start(bf16[4,288,1440]{2,1,0:T(8,128)(2,1)} %bitcast.199), calls=%async_computation.8 | async-start | bytes 7077888 | tf_op jit(solution)/shard_map/all_to_all | solution.py:66
  647.0 37.3 %collective-permute-start.40 = (bf16[1152,1440]{0,1:T(8,128)(2,1)}, bf16[1152,1440]{0,1:T(8,128)(2,1)}, u32[]{:S(2)}, u32[]{:S(2)}) collective-permute-start(bf16[1152,1440]{0,1:T(8,128)(2,1)} %convolution_convert_fusion.2), channel_id=1, source_target_pairs={{0,1},{1,0},{2,3},{3,2},{4,5},{5,4},{6,7},{7,6},{8,9},{9,8},{10,11... | collective-permute-start | bytes 9953288 | tf_op jit(solution)/shard_map/ppermute | solution.py:33
  673.8 38.2 %all-to-all-start.1 = ((bf16[4,320,1152]{2,1,0:T(8,128)(2,1)}), bf16[4,320,1152]{2,1,0:T(8,128)(2,1)}, u32[]{:S(2)}, u32[]{:S(2)}) async-start(bf16[4,320,1152]{2,1,0:T(8,128)(2,1)} %fusion.4), calls=%async_computation.1 | async-start | bytes 5898240 | tf_op jit(solution)/shard_map/all_to_all | solution.py:419
  684.4 58.3 %collective-permute-start.41 = (bf16[1152,1440]{0,1:T(8,128)(2,1)}, bf16[1152,1440]{0,1:T(8,128)(2,1)}, u32[]{:S(2)}, u32[]{:S(2)}) collective-permute-start(bf16[1152,1440]{0,1:T(8,128)(2,1)} %convolution_convert_fusion.1), channel_id=1, source_target_pairs={{0,1},{1,0},{2,3},{3,2},{4,5},{5,4},{6,7},{7,6},{8,9},{9,8},{10,11... | collective-permute-start | bytes 9953288 | tf_op jit(solution)/shard_map/ppermute | solution.py:33
  712.0 48.8 %all-to-all-start.6 = ((bf16[4,288,1440]{2,1,0:T(8,128)(2,1)}), bf16[4,288,1440]{2,1,0:T(8,128)(2,1)S(1)}, u32[]{:S(2)}, u32[]{:S(2)}) async-start(bf16[4,288,1440]{2,1,0:T(8,128)(2,1)} %bitcast.198), calls=%async_computation.6 | async-start | bytes 7077888 | tf_op jit(solution)/shard_map/all_to_all | solution.py:66
  762.6 44.3 %all-to-all-start.7 = ((bf16[4,288,1440]{2,1,0:T(8,128)(2,1)}), bf16[4,288,1440]{2,1,0:T(8,128)(2,1)}, u32[]{:S(2)}, u32[]{:S(2)}) async-start(bf16[4,288,1440]{2,1,0:T(8,128)(2,1)} %bitcast.197), calls=%async_computation.7 | async-start | bytes 7077888 | tf_op jit(solution)/shard_map/all_to_all | solution.py:66
  775.6 45.0 %collective-permute-start.35 = (bf16[1152,576]{0,1:T(8,128)(2,1)}, bf16[1152,576]{0,1:T(8,128)(2,1)}, u32[]{:S(2)}, u32[]{:S(2)}) collective-permute-start(bf16[1152,576]{0,1:T(8,128)(2,1)} %convolution_convert_fusion.5), channel_id=1, source_target_pairs={{0,1},{1,0},{2,3},{3,2},{4,5},{5,4},{6,7},{7,6},{8,9},{9,8},{10,11... | collective-permute-start | bytes 3981320 | tf_op jit(solution)/shard_map/ppermute | solution.py:33
  778.1 68.8 %collective-permute-start.36 = (bf16[1152,576]{0,1:T(8,128)(2,1)}, bf16[1152,576]{0,1:T(8,128)(2,1)}, u32[]{:S(2)}, u32[]{:S(2)}) collective-permute-start(bf16[1152,576]{0,1:T(8,128)(2,1)} %convolution_convert_fusion.4), channel_id=1, source_target_pairs={{0,1},{1,0},{2,3},{3,2},{4,5},{5,4},{6,7},{7,6},{8,9},{9,8},{10,11... | collective-permute-start | bytes 3981320 | tf_op jit(solution)/shard_map/ppermute | solution.py:33
  806.8 22.0 %all-to-all-start.2 = ((bf16[4,288,576]{2,1,0:T(8,128)(2,1)}), bf16[4,288,576]{2,1,0:T(8,128)(2,1)}, u32[]{:S(2)}, u32[]{:S(2)}) async-start(bf16[4,288,576]{2,1,0:T(8,128)(2,1)} %bitcast.223), calls=%async_computation.2 | async-start | bytes 2949120 | tf_op jit(solution)/shard_map/all_to_all | solution.py:66
  828.9 22.2 %all-to-all-start.3 = ((bf16[4,288,576]{2,1,0:T(8,128)(2,1)}), bf16[4,288,576]{2,1,0:T(8,128)(2,1)}, u32[]{:S(2)}, u32[]{:S(2)}) async-start(bf16[4,288,576]{2,1,0:T(8,128)(2,1)} %bitcast.222), calls=%async_computation.3 | async-start | bytes 2949120 | tf_op jit(solution)/shard_map/all_to_all | solution.py:66
  836.2 21.4 %collective-permute-start.31 = (bf16[80,2304]{1,0:T(8,128)(2,1)}, bf16[80,2304]{1,0:T(8,128)(2,1)S(1)}, u32[]{:S(2)}, u32[]{:S(2)}) collective-permute-start(bf16[80,2304]{1,0:T(8,128)(2,1)} %get-tuple-element.46), channel_id=1, source_target_pairs={{0,8},{8,0},{16,24},{24,16},{1,9},{9,1},{17,25},{25,17},{2,10},{10... | collective-permute-start | bytes 1105928 | tf_op jit(solution)/shard_map/ppermute | solution.py:29
  840.8 32.5 %collective-permute-start.32 = (bf16[80,2304]{1,0:T(8,128)(2,1)}, bf16[80,2304]{1,0:T(8,128)(2,1)}, u32[]{:S(2)}, u32[]{:S(2)}) collective-permute-start(bf16[80,2304]{1,0:T(8,128)(2,1)} %get-tuple-element.48), channel_id=1, source_target_pairs={{0,16},{8,24},{16,0},{24,8},{1,17},{9,25},{17,1},{25,9},{2,18},{10... | collective-permute-start | bytes 1105928 | tf_op jit(solution)/shard_map/ppermute | solution.py:29
  842.0 31.3 %collective-permute-start.33 = (bf16[80,2304]{1,0:T(8,128)(2,1)}, bf16[80,2304]{1,0:T(8,128)(2,1)}, u32[]{:S(2)}, u32[]{:S(2)}) collective-permute-start(bf16[80,2304]{1,0:T(8,128)(2,1)} %get-tuple-element.47), channel_id=1, source_target_pairs={{0,24},{8,16},{16,8},{24,0},{1,25},{9,17},{17,9},{25,1},{2,26},{10... | collective-permute-start | bytes 1105928 | tf_op jit(solution)/shard_map/ppermute | solution.py:29
  844.6 43.1 %collective-permute-start.39 = (bf16[288,576]{1,0:T(8,128)(2,1)}, bf16[288,576]{1,0:T(8,128)(2,1)}, u32[]{:S(2)}, u32[]{:S(2)}) collective-permute-start(bf16[288,576]{1,0:T(8,128)(2,1)} %reduce_sum.188), channel_id=1, source_target_pairs={{0,0},{1,16},{2,8},{3,24},{8,2},{9,18},{10,10},{11,26},{16,1},{17,... | collective-permute-start | bytes 995336 | tf_op jit(solution)/shard_map/ppermute | solution.py:76
  851.1 113.6 %all-to-all-start.4 = ((bf16[4,288,576]{2,1,0:T(8,128)(2,1)}), bf16[4,288,576]{2,1,0:T(8,128)(2,1)}, u32[]{:S(2)}, u32[]{:S(2)}) async-start(bf16[4,288,576]{2,1,0:T(8,128)(2,1)} %bitcast.57), calls=%async_computation.4 | async-start | bytes 2949120 | tf_op jit(solution)/shard_map/all_to_all | solution.py:66
  891.3 107.1 %collective-permute-start.44 = (bf16[288,1440]{1,0:T(8,128)(2,1)}, bf16[288,1440]{1,0:T(8,128)(2,1)}, u32[]{:S(2)}, u32[]{:S(2)}) collective-permute-start(bf16[288,1440]{1,0:T(8,128)(2,1)} %reduce_sum.191), channel_id=1, source_target_pairs={{0,0},{1,16},{2,8},{3,24},{8,2},{9,18},{10,10},{11,26},{16,1},{17,... | collective-permute-start | bytes 2488328 | tf_op jit(solution)/shard_map/ppermute | solution.py:76
  912.2 88.7 %collective-permute-start.42 = (bf16[2,288,1440]{2,1,0:T(8,128)(2,1)}, bf16[2,288,1440]{2,1,0:T(8,128)(2,1)}, u32[]{:S(2)}, u32[]{:S(2)}) collective-permute-start(bf16[2,288,1440]{2,1,0:T(8,128)(2,1)} %pad_maximum_fusion.1), channel_id=1, source_target_pairs={{0,0},{1,16},{2,8},{3,24},{8,2},{9,18},{10,10},{11,26},{16,1},{17,... | collective-permute-start | bytes 4976648 | tf_op jit(solution)/shard_map/ppermute | solution.py:76
  914.2 46.7 %collective-permute-start.48 = (f32[2,2304]{1,0:T(2,128)S(1)}, f32[2,2304]{1,0:T(2,128)S(1)}, u32[]{:S(2)}, u32[]{:S(2)}) collective-permute-start(f32[2,2304]{1,0:T(2,128)S(1)} %add.309), channel_id=1, source_target_pairs={{0,8},{8,0},{16,24},{24,16},{1,9},{9,1},{17,25},{25,17},{2,10},{10... | collective-permute-start | bytes 55304 | tf_op jit(solution)/shard_map/ppermute | solution.py:443
  960.8 36.8 %collective-permute-start.49 = (f32[2,2304]{1,0:T(2,128)S(1)}, f32[2,2304]{1,0:T(2,128)S(1)}, u32[]{:S(2)}, u32[]{:S(2)}) collective-permute-start(f32[2,2304]{1,0:T(2,128)S(1)} %add.310), channel_id=1, source_target_pairs={{0,16},{8,24},{16,0},{24,8},{1,17},{9,25},{17,1},{25,9},{2,18},{10... | collective-permute-start | bytes 55304 | tf_op jit(solution)/shard_map/ppermute | solution.py:443
  967.6 63.7 %collective-permute-start.37 = (bf16[3,288,576]{2,1,0:T(8,128)(2,1)}, bf16[3,288,576]{2,1,0:T(8,128)(2,1)}, u32[]{:S(2)}, u32[]{:S(2)}) collective-permute-start(bf16[3,288,576]{2,1,0:T(8,128)(2,1)} %pad_maximum_fusion.4), channel_id=1, source_target_pairs={{0,0},{1,16},{2,8},{3,24},{8,2},{9,18},{10,10},{11,26},{16,1},{17,... | collective-permute-start | bytes 2985992 | tf_op jit(solution)/shard_map/ppermute | solution.py:76
  (85 other events, 2243.1 us)
Sparse Core Ops, SparseCore 0:
  51.0 76.3 all-gather.4
  151.4 56.2 all-gather.6
  209.7 56.3 all-gather.10
  267.8 96.8 all-gather.8

commit v2 on v1

--- a/solution.py
+++ b/solution.py
@@ -16,8 +16,8 @@
 f32 = jnp.float32
 bf16 = jnp.bfloat16
 
-PLANE = ("pb", "tx", "tc")
-CHIPS = ("pb", "tx")
+PLANE = ("tc", "tx", "pb")
+CHIPS = ("tx", "pb")
 ROW = "za"
 
 
@@ -33,47 +33,84 @@
     return lax.ppermute(array, "tc", [(0, 1), (1, 0)])
 
 
-def row_gather(rows):
-    count = lax.axis_size(ROW)
-    return jnp.concatenate([rows] + [send_row(rows, k) for k in range(1, count)], axis=0)
-
-
-def row_scatter(partial):
+def after(array, *done):
+    return lax.optimization_barrier((array,) + done)[0]
+
+
+def row_send(rows):
+    return [rows] + [send_row(rows, k) for k in range(1, lax.axis_size(ROW))]
+
+
+def row_split(partial):
     count = lax.axis_size(ROW)
     height = partial.shape[0] // count
-    total = partial[:height]
-    for k in range(1, count):
-        total = total + send_row(partial[k * height : (k + 1) * height].astype(bf16), k).astype(f32)
+    parts = [partial[k * height : (k + 1) * height] for k in range(count)]
+    return [parts[0]] + [send_row(parts[k].astype(bf16), k) for k in range(1, count)]
+
+
+def row_sum(parts):
+    total = parts[0]
+    for part in parts[1:]:
+        total = total + part.astype(f32)
     return total
 
 
-def after(array, done):
-    return lax.optimization_barrier((array, done))[0]
-
-
-def plane_scatter(left, right):
-    core = lax.axis_index("tc")
+def halves(array, cut):
+    return [array[:, :cut], array[:, cut:]]
+
+
+def turn(parts, back=False):
+    rows, shares = lax.axis_size(ROW), lax.axis_size("tx") * lax.axis_size("tc")
+
+    def move(part, twist):
+        pairs = [
+            (z * shares + t, (t ^ twist) * shares + z % 2 * (shares // 2) + z // 2)
+            for z in range(rows)
+            for t in range(shares)
+        ]
+        if back:
+            pairs = [(j, i) for i, j in pairs]
+        return lax.ppermute(part, (ROW, "tx", "tc"), pairs)
+
+    return [move(parts[0], 0), move(parts[1], shares // 2)]
+
+
+def columns(parts):
+    return jnp.concatenate(parts, axis=1)
+
+
+def rows_of(parts):
+    return jnp.concatenate(parts, axis=0)
+
+
+def fence(*values):
+    return lax.optimization_barrier(values)
+
+
+def plane_gather(piece):
+    return lax.all_gather(piece, PLANE, axis=0, tiled=True)
+
+
+def with_twin(left):
+    half = left.shape[1] // 2
+    first = lax.axis_index("tc") == 0
+    mine = jnp.where(first, left[:, :half], left[:, half:])
+    other = jnp.where(first, left[:, half:], left[:, :half])
+    return rows_of([mine, swap_core(other)])
+
+
+def pair_sum(left, right):
     chips = lax.axis_size("pb") * lax.axis_size("tx")
-    blocks = left.reshape(left.shape[0], chips, 2, -1)
-
-    def half(which):
-        part = lax.dynamic_index_in_dim(blocks, which, 2, keepdims=False)
-        return dot(part.reshape(left.shape[0], -1), right, ((0,), (0,)))
-
-    other = swap_core(half(1 - core).astype(bf16))
-    total = (half(core) + other.astype(f32)).astype(bf16)
-    total = total.reshape(chips, -1, total.shape[1])
-    total = lax.all_to_all(total, CHIPS, 0, 0, tiled=True)
-    return jnp.sum(total.astype(f32), axis=0).astype(bf16)
-
-
-def turn(array):
-    pairs = []
-    for z in range(4):
-        for tx in range(2):
-            for tc in range(2):
-                pairs.append((z * 4 + tx * 2 + tc, (tc * 2 + tx) * 4 + (z % 2) * 2 + z // 2))
-    return lax.ppermute(array, ("za", "tx", "tc"), pairs)
+    total = dot(rows_of([right, swap_core(right)]), left, ((0,), (0,))).astype(bf16).T
+    return total.reshape(chips, -1, total.shape[1])
+
+
+def exchange(blocks):
+    return lax.all_to_all(blocks, CHIPS, 0, 0, tiled=True)
+
+
+def chip_sum(received):
+    return jnp.sum(received.astype(f32), axis=0).astype(bf16)
 
 
 def lineage(segments, parents):
@@ -256,6 +293,12 @@
     return heads, rows, keys, fixed, bias, params
 
 
+def work(queries, kv, products):
+    return pl.CostEstimate(
+        flops=products * kv.size * 8000, bytes_accessed=4 * kv.size, transcendentals=0
+    )
+
+
 def attend(row, query_info, key_info, queries, kv):
     heads, rows, keys, fixed, bias, params = attention_specs(queries, kv, query_info, key_info)
     return pl.pallas_call(
@@ -266,6 +309,7 @@
         out_shape=jax.ShapeDtypeStruct(queries.shape, f32),
         scratch_shapes=[bias],
         compiler_params=params,
+        cost_estimate=work(queries, kv, 2),
     )(row, query_info, key_info, queries, kv)
 
 
@@ -282,6 +326,7 @@
         ],
         scratch_shapes=[bias],
         compiler_params=params,
+        cost_estimate=work(queries, kv, 5),
     )(row, query_info, key_info, queries, kv, saved, grad)
 
 
@@ -304,14 +349,6 @@
     own, width = block_input.shape
     piece = width // plane
 
-    def to_plane(array):
-        blocks = array.reshape(-1, c_n, x_n, b_n, piece)
-        return blocks.transpose(0, 3, 2, 1, 4).reshape(array.shape)
-
-    def from_plane(array):
-        blocks = array.reshape(-1, b_n, x_n, c_n, piece)
-        return blocks.transpose(0, 3, 2, 1, 4).reshape(array.shape)
-
     def untangle(array, axis, index):
         count = array.shape[axis]
         for bit in range(count.bit_length() - 1):
@@ -321,34 +358,42 @@
             array = jnp.where((index >> bit) & 1 == 1, flipped, array)
         return array
 
+    features = w_qkv.shape[2]
+    heads = features // HD
+    near = (heads + 1) // 2
+    units = w_down.shape[0]
+    near_units = min(units, (units // 2 + 127) // 128 * 128)
+    w_kv = side_by_side(w_qkv[1], w_qkv[2])
+
+    low = 32
     small = jnp.concatenate(
-        [norm_gains.astype(f32).reshape(-1), tok_seg.astype(f32), tok_pos.astype(f32)]
-    )
-    small = jnp.stack([small] + [send_row(small, k) for k in range(1, rows_n)])
-    across_b = [
+        [norm_gains.reshape(-1)] + [t.astype(bf16) for t in (tok_seg, tok_pos // low, tok_pos % low)]
+    )
+    small = jnp.pad(small, (0, width - small.shape[0]))
+    small = [small] + [
         lax.ppermute(small, "pb", [(i, i ^ k) for i in range(b_n)]) for k in range(1, b_n)
     ]
-    small = jnp.stack([small] + across_b, axis=1)
+    kv_full = plane_gather(columns(turn(halves(w_kv, near * 2 * HD))))
+    q_full = plane_gather(columns(turn(halves(w_qkv[0], near * HD))))
+    x_own = block_input
+    x_parts = row_send(jnp.concatenate([x_own, jnp.stack(small)], axis=0))
+    x_parts, out_halves, gate_halves, up_halves, down_halves = fence(
+        x_parts,
+        halves(w_out.T, near * HD),
+        halves(w_gate_up[0], near_units),
+        halves(w_gate_up[1], near_units),
+        halves(w_down.T, near_units),
+    )
+    out_moved = turn(out_halves)
+    gate_moved = turn(gate_halves)
+    small = jnp.stack([part[own:] for part in x_parts])
     gains = small[..., : 2 * norm_gains.shape[1]].reshape(rows_n, b_n, 2, -1)
     group = tok_seg.shape[0]
-    seg_all = small[..., -2 * group : -group].astype(jnp.int32)
-    pos_all = small[..., -group:].astype(jnp.int32)
-    x_own = to_plane(block_input)
-    x_group = row_gather(x_own)
+    small = small[..., gains.shape[3] * 2 :][..., : 3 * group].astype(jnp.int32)
+    seg_all = small[..., :group]
+    pos_all = small[..., group : 2 * group] * low + small[..., 2 * group :]
     gains = untangle(untangle(gains, 0, z), 1, b).transpose(2, 0, 1, 3).reshape(2, width)
-    gains = to_plane(gains)
-
-    qkv_moved = turn(w_qkv)
-    qkv_full = lax.all_gather(qkv_moved, PLANE, axis=1, tiled=True)
-    out_moved = turn(after(w_out, x_group))
-    out_full = lax.all_gather(out_moved, PLANE, axis=1, tiled=True)
-    gate_up_moved = turn(after(w_gate_up, x_group))
-    gate_up_full = lax.all_gather(gate_up_moved, PLANE, axis=1, tiled=True)
-    down_moved = turn(after(w_down, gate_up_moved))
-    down_full = lax.all_gather(down_moved, PLANE, axis=1, tiled=True)
-
-    cot_own = to_plane(cotangent).astype(f32)
-    grad_branch_f = row_gather(after((depth_scale * cot_own).astype(bf16), down_moved))
+    gains = gains.astype(f32)
 
     pos_all = untangle(pos_all, 1, b).reshape(rows_n, b_n, x_n, c_n, own)
     seg_all = untangle(untangle(seg_all, 0, z), 1, b).reshape(pos_all.shape)
@@ -360,7 +405,7 @@
         return lax.dynamic_slice_in_dim(array, c, 1, 3).reshape(-1)
 
     def for_keys(array):
-        array = untangle(array, 3, c).transpose(0, 3, 1, 2, 4)
+        array = untangle(array, 3, c).transpose(0, 3, 2, 1, 4)
         return array.reshape(-1, 8 * own)
 
     own_seg, own_index, pos_group = for_group(seg_all), for_group(index_all), for_group(pos_all)
@@ -369,75 +414,128 @@
     key_info = jnp.stack([for_keys(seg_all), for_keys(index_all)], axis=1)
     row = z.astype(jnp.int32).reshape(1)
 
-    rows_a = x_group.astype(f32)
+    cosine, sine_table = rope_tables(pos_group)
+    cot_own = cotangent.astype(f32)
+    branch_f = (depth_scale * cot_own).astype(bf16)
+    rows_a = rows_of([part[:own] for part in x_parts]).astype(f32)
     normed_a = ((rows_a * inverse_rms(rows_a)) * gains[0]).astype(bf16)
-    cosine, sine_table = rope_tables(pos_group)
-    queries = (rotate(dot(normed_a, qkv_full[0]), cosine, sine_table)).astype(bf16) * bf16(HD**-0.5)
-    keys = rotate(dot(normed_a, qkv_full[1]), cosine, sine_table).astype(bf16)
-    values = dot(normed_a, qkv_full[2]).astype(bf16)
-    queries = side_by_side(queries, None)
-    kv = side_by_side(keys, values)
+    group = rows_n * own
+    mine = dot(normed_a, kv_full).reshape(group, heads, 2, HD)
+    keys = rotate(mine[:, :, 0].reshape(group, -1), cosine, sine_table).astype(bf16)
+    mine = side_by_side(keys, mine[:, :, 1].reshape(group, -1).astype(bf16))
+    mine, out_moved, gate_moved, up_halves, down_halves, branch_f = fence(
+        mine, out_moved, gate_moved, up_halves, down_halves, branch_f
+    )
+    out_full = plane_gather(columns(out_moved))
+    gate_full = plane_gather(columns(gate_moved))
+    up_moved = turn(up_halves)
+    down_moved = turn(down_halves)
     chips = b_n * x_n
-    kv = lax.all_to_all(jnp.broadcast_to(kv[None], (chips,) + kv.shape), CHIPS, 0, 0, tiled=True)
+    kv = exchange(jnp.broadcast_to(mine[None], (chips,) + mine.shape))
+    queries = rotate(dot(after(normed_a, mine), q_full), cosine, sine_table)
+    queries = side_by_side(queries.astype(bf16) * bf16(HD**-0.5), None)
+    kv, up_moved, down_moved, queries, query_info, key_info, branch_f = fence(
+        kv, up_moved, down_moved, queries, query_info, key_info, branch_f
+    )
+    up_full = plane_gather(columns(up_moved))
+    down_full = plane_gather(columns(down_moved))
+    f_parts = row_send(branch_f)
     kv = jnp.concatenate([kv, swap_core(kv)], axis=0).reshape(plane, rows_n, own, -1)
     saved = attend(row, query_info, key_info, queries, kv)
-    attended = saved.reshape(rows_n * own, -1, 2, HD)[:, :, 1].reshape(rows_n * own, -1).astype(bf16)
-    mid = x_own.astype(f32) + depth_scale * row_scatter(dot(attended, out_full))
+    attended = saved.reshape(group, heads, 2, HD)[:, :, 1].reshape(group, -1).astype(bf16)
+    mid_part = dot(attended, out_full, ((1,), (1,)))
+    parts = row_split(mid_part)
+    parts, f_parts = fence(parts, f_parts)
+    mid = x_own.astype(f32) + depth_scale * row_sum(parts)
     inv_f = inverse_rms(mid)
     unit_f = mid * inv_f
-    normed_f = row_gather((unit_f * gains[1]).astype(bf16))
-    gate = dot(normed_f, gate_up_full[0])
-    up = dot(normed_f, gate_up_full[1])
+    normed_f = rows_of(row_send((unit_f * gains[1]).astype(bf16)))
+    grad_branch_f = rows_of(f_parts)
+    gate = dot(normed_f, gate_full)
+    up = dot(normed_f, up_full)
     sig = jax.nn.sigmoid(gate)
     silu = gate * sig
     hidden = (silu * up).astype(bf16)
-    output = mid + depth_scale * row_scatter(dot(hidden, down_full))
-
-    grad_hidden = dot(grad_branch_f, down_full, ((1,), (1,)))
+    gf_twin = with_twin(grad_branch_f)
+    nf_twin = with_twin(normed_f)
+    grad_hidden = dot(grad_branch_f, down_full)
     grad_gate = (grad_hidden * up * sig * (1.0 + gate * (1.0 - sig))).astype(bf16)
     grad_up = (grad_hidden * silu).astype(bf16)
-    grad_normed_f = row_scatter(
-        dot(grad_gate, gate_up_full[0], ((1,), (1,))) + dot(grad_up, gate_up_full[1], ((1,), (1,)))
-    )
+    normed_part = dot(grad_gate, gate_full, ((1,), (1,))) + dot(grad_up, up_full, ((1,), (1,)))
+    down_pair = pair_sum(gf_twin, hidden)
+    normed_part, down_pair, hidden, grad_gate, grad_up, nf_twin = fence(
+        normed_part, down_pair, hidden, grad_gate, grad_up, nf_twin
+    )
+
+    parts = row_split(normed_part)
+    down_sum = exchange(down_pair)
+    gate_pair = pair_sum(nf_twin, grad_gate)
+    up_pair = pair_sum(nf_twin, grad_up)
+    parts, down_sum, gate_pair, up_pair = fence(parts, down_sum, gate_pair, up_pair)
+    grad_normed_f = row_sum(parts)
     gain_f = jnp.sum(grad_normed_f * unit_f, axis=0)
     grad_mid = cot_own + norm_back(grad_normed_f * gains[1], unit_f, inv_f)
-    grad_branch_a = row_gather((depth_scale * grad_mid).astype(bf16))
-
-    grad_gate_up = jnp.stack([plane_scatter(normed_f, g) for g in (grad_gate, grad_up)])
-    grad_down = plane_scatter(grad_branch_f, hidden)
-    grad_out = plane_scatter(grad_branch_a, attended)
-    grad_gate_up = turn(grad_gate_up).astype(f32)
-    grad_down = turn(grad_down).astype(f32).T
-    grad_out = turn(grad_out).astype(f32).T
-
-    grad_attended = dot(grad_branch_a, out_full, ((1,), (1,))).astype(bf16)
+    branch_a = (depth_scale * grad_mid).astype(bf16)
+
+    parts = row_send(branch_a)
+    gate_sum = exchange(gate_pair)
+    down_sum = chip_sum(down_sum)
+    parts, gate_sum, down_sum, up_pair = fence(parts, gate_sum, down_sum, up_pair)
+    grad_branch_a = rows_of(parts)
+    up_sum = exchange(up_pair)
+    down_back = turn(halves(down_sum, near_units), True)
+    gate_back = turn(halves(chip_sum(gate_sum), near_units), True)
+    grad_attended = dot(grad_branch_a, out_full).astype(bf16)
     grad_q, grad_kv = attend_back(
         row, query_info, key_info, queries, kv, saved, side_by_side(None, grad_attended)
     )
-    grad_kv = grad_kv.reshape(2, chips, rows_n * own, -1)
+    grad_q, grad_kv, up_sum, down_back, gate_back, hidden = fence(
+        grad_q, grad_kv, up_sum, down_back, gate_back, hidden
+    )
+
+    output_part = dot(hidden, down_full, ((1,), (1,)))
+    grad_kv = grad_kv.reshape(2, chips, group, -1)
     grad_kv = (grad_kv[0].astype(f32) + swap_core(grad_kv[1]).astype(f32)).astype(bf16)
-    grad_kv = lax.all_to_all(grad_kv, CHIPS, 0, 0, tiled=True)
-    grad_kv = jnp.sum(grad_kv.astype(f32), axis=0).reshape(rows_n * own, -1, 2, HD)
-    flat = (rows_n * own, w_qkv.shape[2])
-    grad_q = grad_q.reshape(rows_n * own, -1, 2, HD)[:, :, 0].reshape(flat) * HD**-0.5
+    grad_kv, output_part = fence(grad_kv, output_part)
+    grad_kv = exchange(grad_kv)
+    output_parts = row_split(output_part)
+    grad_q = grad_q.reshape(group, heads, 2, HD)[:, :, 0].reshape(group, -1) * HD**-0.5
     grad_q = rotate(grad_q, cosine, -sine_table).astype(bf16)
-    grad_k = rotate(grad_kv[:, :, 0].reshape(flat), cosine, -sine_table).astype(bf16)
-    grad_v = grad_kv[:, :, 1].reshape(flat).astype(bf16)
-    grad_normed_a = row_scatter(
-        dot(grad_q, qkv_full[0], ((1,), (1,)))
-        + dot(grad_k, qkv_full[1], ((1,), (1,)))
-        + dot(grad_v, qkv_full[2], ((1,), (1,)))
-    )
+    q_pair = pair_sum(with_twin(normed_a), grad_q)
+    out_pair = pair_sum(with_twin(grad_branch_a), attended)
+    up_sum = chip_sum(up_sum)
+    grad_kv, q_pair, out_pair, up_sum = fence(grad_kv, q_pair, out_pair, up_sum)
+    grad_kv = jnp.sum(grad_kv.astype(f32), axis=0).reshape(group, heads, 2, HD)
+    grad_k = rotate(grad_kv[:, :, 0].reshape(group, -1), cosine, -sine_table).astype(bf16)
+    grad_kv = side_by_side(grad_k, grad_kv[:, :, 1].reshape(group, -1).astype(bf16))
+    normed_part = dot(grad_q, q_full, ((1,), (1,))) + dot(grad_kv, kv_full, ((1,), (1,)))
+    grad_kv, normed_part, output_parts = fence(grad_kv, normed_part, output_parts)
+    two_sum = exchange(jnp.concatenate([q_pair, out_pair], axis=2))
+    parts = row_split(normed_part)
+    kv_pair = pair_sum(with_twin(normed_a), grad_kv)
+    up_back = turn(halves(up_sum, near_units), True)
+    kv_pair, two_sum, parts = fence(kv_pair, two_sum, parts)
+    kv_sum = exchange(kv_pair)
+    two_sum = chip_sum(two_sum)
+    q_back = turn(halves(two_sum[:, :features], near * HD), True)
+    out_back = turn(halves(two_sum[:, features:], near * HD), True)
+    grad_normed_a = row_sum(parts)
+    kv_back = turn(halves(chip_sum(kv_sum), near * 2 * HD), True)
+    output = mid + depth_scale * row_sum(output_parts)
+
+    grad_gate_up = jnp.stack([columns(gate_back), columns(up_back)]).astype(f32)
+    grad_down = columns(down_back).astype(f32).T
+    grad_out = columns(out_back).astype(f32).T
+    grad_w_kv = columns(kv_back).reshape(piece, heads, 2, HD)
     grad_qkv = jnp.stack(
-        [plane_scatter(normed_a, g) for g in (grad_q, grad_k, grad_v)]
-    )
-    grad_qkv = turn(grad_qkv).astype(f32)
+        [columns(q_back)] + [grad_w_kv[:, :, n].reshape(piece, features) for n in range(2)]
+    ).astype(f32)
     rows_own = x_own.astype(f32)
     inv_a = inverse_rms(rows_own)
     unit_a = rows_own * inv_a
     gain_a = jnp.sum(grad_normed_a * unit_a, axis=0)
     grad_input = grad_mid + norm_back(grad_normed_a * gains[0], unit_a, inv_a)
-    gain_sum = from_plane(jnp.stack([gain_a, gain_f]))
+    gain_sum = jnp.stack([gain_a, gain_f])
     for axis, count in (("tc", c_n), ("tx", x_n), ("pb", b_n), ("za", rows_n)):
         for bit in range(count.bit_length() - 1):
             gain_sum = gain_sum + lax.ppermute(
@@ -446,7 +544,7 @@
     part = width // (rows_n * plane)
     place = ((z * b_n + b) * x_n + x) * c_n + c
     grad_gains = lax.dynamic_slice_in_dim(gain_sum, place * part, part, 1)
-    return (from_plane(output), from_plane(grad_input), grad_qkv, grad_out, grad_gate_up, grad_down, grad_gains)
+    return (output, grad_input, grad_qkv, grad_out, grad_gate_up, grad_down, grad_gains)
 
 
 def solution(mesh):

time: 1060 us -> 832 us (0.78)
  the two profiles are of different devices: /device:TPU:2 before, /device:TPU:1 now
where the time goes in v2:
time: 832 us; the launch traced here: 824 us
  waiting for transfers between devices  294 us (35%)
  starting transfers between devices  207 us (25%)
  matrix products  103 us (12%)
  local copies, waits for them, and re-layouts  85.6 us (10%)
  other arithmetic  78.9 us (9%)
  Pallas kernels  39.3 us (5%)
  between operations  15.9 us (2%)
    ppermute x24, waiting for transfers between devices, move(): return lax.ppermute(part, (ROW, 'tx', 'tc'), pairs)  124 us
    dot_general x18, matrix products, dot(): return lax.dot_general(a, b, (dims, ((), ())), preferred_element_type=f32)  103 us
    ppermute x24, waiting for transfers between devices, send_row(): lax.ppermute(array, ROW, [(i, i ^ distance) for i in range(lax.axis_size(...  87 us
    ppermute x24, starting transfers between devices, move(): return lax.ppermute(part, (ROW, 'tx', 'tc'), pairs)  82.3 us
    ppermute x24, starting transfers between devices, send_row(): lax.ppermute(array, ROW, [(i, i ^ distance) for i in range(lax.axis_size(...  66 us
    all_to_all x7, waiting for transfers between devices, exchange(): return lax.all_to_all(blocks, CHIPS, 0, 0, tiled=True)  40.9 us
    all_to_all x7, starting transfers between devices, exchange(): return lax.all_to_all(blocks, CHIPS, 0, 0, tiled=True)  30.8 us
    ppermute x5, waiting for transfers between devices, on_device(): lax.ppermute(gain_sum, axis, [(i, i ^ 1 << bit) for i in range(count)])  26.6 us
  transfers between devices with their start and end apart: 79, of which 29 were waited for; matrix products, arithmetic and copies ran while one was open for 28% of the time, Pallas kernels for 5%

profile of v2, /device:TPU:1, one launch (start us, length us, event | category | flops | bytes accessed | tf_op | source)
XLA Modules:
  0.0 823.9 jit_solution(5761245705146570503)
XLA Ops:
  16.6 18.6 %collective-permute-done.5 = bf16[288,512]{0,1:T(8,128)(2,1)S(1)} collective-permute-done((bf16[288,512]{0,1:T(8,128)(2,1)S(1)}, bf16[288,512]{0,1:T(8,128)(2,1)S(1)}, u32[]{:S(2)}, u32[]{:S(2)}) %collective-permute-start.5) | collective-permute-done | bytes 294944 | tf_op jit(solution)/shard_map/ppermute | solution.py:73
  39.5 6.3 collective-permute-start.14
  64.9 16.6 %collective-permute-done.2 = bf16[82,2304]{1,0:T(8,128)(2,1)S(1)} collective-permute-done((bf16[82,2304]{1,0:T(8,128)(2,1)S(1)}, bf16[82,2304]{1,0:T(8,128)(2,1)S(1)}, u32[]{:S(2)}, u32[]{:S(2)}) %collective-permute-start.2) | collective-permute-done | bytes 377888 | tf_op jit(solution)/shard_map/ppermute | solution.py:29
  85.6 12.6 %collective-permute-start.6 = (bf16[288,320]{1,0:T(8,128)(2,1)}, bf16[288,320]{1,0:T(8,128)(2,1)}, u32[]{:S(2)}, u32[]{:S(2)}) collective-permute-start(bf16[288,320]{1,0:T(8,128)(2,1)} %slice.385), channel_id=1, source_target_pairs={{0,0},{1,8},{2,16},{3,24},{8,2},{9,10},{10,18},{11,26},{16,1},{17,... | collective-permute-start | bytes 552968 | tf_op jit(solution)/shard_map/ppermute | solution.py:73
  106.4 6.0 fusion.69
  112.9 12.6 %collective-permute-done.9 = bf16[288,672]{1,0:T(8,128)(2,1)} collective-permute-done((bf16[288,672]{1,0:T(8,128)(2,1)}, bf16[288,672]{1,0:T(8,128)(2,1)}, u32[]{:S(2)}, u32[]{:S(2)}) %collective-permute-start.9) | collective-permute-done | bytes 387104 | tf_op jit(solution)/shard_map/ppermute | solution.py:73
  153.0 20.4 %collective-permute-done.11 = bf16[288,672]{1,0:T(8,128)(2,1)} collective-permute-done((bf16[288,672]{1,0:T(8,128)(2,1)}, bf16[288,672]{1,0:T(8,128)(2,1)}, u32[]{:S(2)}, u32[]{:S(2)}) %collective-permute-start.11) | collective-permute-done | bytes 387104 | tf_op jit(solution)/shard_map/ppermute | solution.py:73
  173.5 9.3 %collective-permute-done.13 = bf16[288,672]{1,0:T(8,128)(2,1)} collective-permute-done((bf16[288,672]{1,0:T(8,128)(2,1)}, bf16[288,672]{1,0:T(8,128)(2,1)}, u32[]{:S(2)}, u32[]{:S(2)}) %collective-permute-start.13) | collective-permute-done | bytes 387104 | tf_op jit(solution)/shard_map/ppermute | solution.py:73
  182.7 12.4 %all-to-all-done = bf16[4,320,1152]{2,1,0:T(8,128)(2,1)S(1)} async-done(((bf16[4,320,1152]{2,1,0:T(8,128)(2,1)}), bf16[4,320,1152]{2,1,0:T(8,128)(2,1)S(1)}, u32[]{:S(2)}, u32[]{:S(2)}) %all-to-all-start) | async-done | bytes 2949152 | tf_op jit(solution)/shard_map/all_to_all | solution.py:109
  215.6 16.2 %shard_map.153.out_ref = f32[320,1152]{1,0:T(8,128)} custom-call(s32[1]{0:T(128)} %bitcast.row_ref, s32[320,4]{1,0:T(8,128)} %copy.95.query_ref, s32[4,2,640]{2,1,0:T(2,128)} %pad_add_fusion.key_ref, bf16[320,1152]{1,0:T(8,128)(2,1)} %copy.96.q_ref, bf16[8,4,80,1152]{3,2,1,0:T(8,128)(2,1)} %bitcast.139), custom_call_target="tpu_custom_call" | custom-call | flops 47185920000 | bytes 11796480 | tf_op jit(solution)/shard_map/pallas_call | solution.py:304
  243.1 12.5 %collective-permute-done.17 = bf16[80,2304]{1,0:T(8,128)(2,1)} collective-permute-done((bf16[80,2304]{1,0:T(8,128)(2,1)}, bf16[80,2304]{1,0:T(8,128)(2,1)}, u32[]{:S(2)}, u32[]{:S(2)}) %collective-permute-start.17) | collective-permute-done | bytes 368672 | tf_op jit(solution)/shard_map/ppermute | solution.py:29
  255.6 9.7 %collective-permute-done.19 = bf16[80,2304]{1,0:T(8,128)(2,1)} collective-permute-done((bf16[80,2304]{1,0:T(8,128)(2,1)}, bf16[80,2304]{1,0:T(8,128)(2,1)}, u32[]{:S(2)}, u32[]{:S(2)}) %collective-permute-start.19) | collective-permute-done | bytes 368672 | tf_op jit(solution)/shard_map/ppermute | solution.py:29
  269.5 16.1 %collective-permute-start.24 = (bf16[80,2304]{1,0:T(8,128)(2,1)S(1)}, bf16[80,2304]{1,0:T(8,128)(2,1)S(1)}, u32[]{:S(2)}, u32[]{:S(2)}) collective-permute-start(bf16[80,2304]{1,0:T(8,128)(2,1)S(1)} %multiply_convert_fusion.4), channel_id=1, source_target_pairs={{0,16},{8,24},{16,0},{24,8},{1,17},{9,25},{17,1},{25,9},{2,18},{10... | collective-permute-start | bytes 1105928 | tf_op jit(solution)/shard_map/ppermute | solution.py:29
  287.7 21.2 %collective-permute-done.24 = bf16[80,2304]{1,0:T(8,128)(2,1)S(1)} collective-permute-done((bf16[80,2304]{1,0:T(8,128)(2,1)S(1)}, bf16[80,2304]{1,0:T(8,128)(2,1)S(1)}, u32[]{:S(2)}, u32[]{:S(2)}) %collective-permute-start.24) | collective-permute-done | bytes 368672 | tf_op jit(solution)/shard_map/ppermute | solution.py:29
  315.4 6.9 fusion.58
  322.2 7.9 fusion.71
  330.1 16.1 %all-gather.15.cloned.1.call-done = bf16[2304,1440]{1,0:T(8,128)(2,1)} async-done(((bf16[288,1440]{1,0:T(8,128)(2,1)}), bf16[2304,1440]{1,0:T(8,128)(2,1)}) %all-gather.15.cloned.1.call-update) | async-done | bytes 6635536 | tf_op jit(solution)/shard_map/all_gather | solution.py:91
  346.2 8.5 %multiply_convert_fusion = (bf16[320,1440]{1,0:T(8,128)(2,1)S(1)}, bf16[320,1440]{1,0:T(8,128)(2,1)}, bf16[320,1440]{1,0:T(8,128)(2,1)}) fusion(f32[320,1440]{1,0:T(8,128)} %fusion.58, f32[320,1440]{1,0:T(8,128)} %fusion.71, bf16[2304,1440]{1,0:T(8,128)(2,1)} %all-gather.15.cloned.1.call-done, bf16[80,2304]{1,0:T(8,128)(2,1)S(1)} %collective-permute-done.25, ...), kind=kOutput, calls=%fused_computation.27 | convolution fusion | flops 2136176640 | bytes 14561280 | tf_op jit(solution)/shard_map/dot_general | solution.py:25
  355.0 5.9 fusion.72
  361.0 13.6 %convolution_add_fusion.1 = f32[320,2304]{1,0:T(8,128)} fusion(f32[320,2304]{1,0:T(8,128)S(1)} %fusion.72, bf16[320,1440]{1,0:T(8,128)(2,1)} %get-tuple-element.139, bf16[2304,1440]{1,0:T(8,128)(2,1)S(1)} %copy-done.52), kind=kOutput, calls=%fused_computation.9 | convolution fusion | flops 2124103680 | bytes 13455360 | tf_op jit(solution)/shard_map/dot_general | solution.py:25
  374.6 5.8 convolution_convert_fusion.3
  380.4 5.7 copy.98
  398.1 5.9 convolution_convert_fusion.2
  404.0 5.7 copy.99
  409.7 6.2 convolution_convert_fusion.1
  415.9 5.7 copy.100
  422.4 8.8 %all-to-all-done.1 = bf16[4,288,1440]{2,1,0:T(8,128)(2,1)} async-done(((bf16[4,288,1440]{2,1,0:T(8,128)(2,1)}), bf16[4,288,1440]{2,1,0:T(8,128)(2,1)}, u32[]{:S(2)}, u32[]{:S(2)}) %all-to-all-start.1) | async-done | bytes 3317792 | tf_op jit(solution)/shard_map/all_to_all | solution.py:109
  444.7 9.4 %collective-permute-done.34 = bf16[80,2304]{1,0:T(8,128)(2,1)S(1)} collective-permute-done((bf16[80,2304]{1,0:T(8,128)(2,1)S(1)}, bf16[80,2304]{1,0:T(8,128)(2,1)S(1)}, u32[]{:S(2)}, u32[]{:S(2)}) %collective-permute-start.34) | collective-permute-done | bytes 368672 | tf_op jit(solution)/shard_map/ppermute | solution.py:29
  454.1 10.7 %collective-permute-done.36 = bf16[80,2304]{1,0:T(8,128)(2,1)S(1)} collective-permute-done((bf16[80,2304]{1,0:T(8,128)(2,1)S(1)}, bf16[80,2304]{1,0:T(8,128)(2,1)S(1)}, u32[]{:S(2)}, u32[]{:S(2)}) %collective-permute-start.36) | collective-permute-done | bytes 368672 | tf_op jit(solution)/shard_map/ppermute | solution.py:29
  464.8 11.5 %all-to-all-done.2 = bf16[4,288,1440]{2,1,0:T(8,128)(2,1)} async-done(((bf16[4,288,1440]{2,1,0:T(8,128)(2,1)}), bf16[4,288,1440]{2,1,0:T(8,128)(2,1)}, u32[]{:S(2)}, u32[]{:S(2)}) %all-to-all-start.2) | async-done | bytes 3317792 | tf_op jit(solution)/shard_map/all_to_all | solution.py:109
  490.8 5.5 collective-permute-start.37
  500.9 23.0 %shard_map.154 = (f32[320,1152]{1,0:T(8,128)}, bf16[8,4,80,1152]{3,2,1,0:T(8,128)(2,1)}) custom-call(s32[1]{0:T(128)} %bitcast.row_ref, s32[320,4]{1,0:T(8,128)} %copy.95.query_ref, s32[4,2,640]{2,1,0:T(2,128)} %pad_add_fusion.key_ref, bf16[320,1152]{1,0:T(8,128)(2,1)} %copy.96.q_ref, bf16[8,4,80,1152]{3,2,1,0:T(8,128)(2,1)} %bitcast.140, ...), custom_call_target="tpu_custom_call" | custom-call | flops 117964800000 | bytes 11796480 | tf_op jit(solution)/shard_map/pallas_call | solution.py:318
  523.9 13.0 %collective-permute-done.40 = bf16[288,672]{1,0:T(8,128)(2,1)S(1)} collective-permute-done((bf16[288,672]{1,0:T(8,128)(2,1)}, bf16[288,672]{1,0:T(8,128)(2,1)S(1)}, u32[]{:S(2)}, u32[]{:S(2)}) %collective-permute-start.40) | collective-permute-done | bytes 387104 | tf_op jit(solution)/shard_map/ppermute | solution.py:73
  540.3 8.9 %collective-permute-done.39 = bf16[288,768]{1,0:T(8,128)(2,1)} collective-permute-done((bf16[288,768]{1,0:T(8,128)(2,1)}, bf16[288,768]{1,0:T(8,128)(2,1)}, u32[]{:S(2)}, u32[]{:S(2)}) %collective-permute-start.39) | collective-permute-done | bytes 442400 | tf_op jit(solution)/shard_map/ppermute | solution.py:73
  549.2 7.1 all-to-all-done.3
  556.2 5.7 fusion.60
  561.9 13.3 %collective-permute-start.41 = (bf16[4,320,1152]{2,1,0:T(8,128)(2,1)}, bf16[4,320,1152]{2,1,0:T(8,128)(2,1)}, u32[]{:S(2)}, u32[]{:S(2)}) collective-permute-start(bf16[4,320,1152]{2,1,0:T(8,128)(2,1)} %bitcast.40), channel_id=1, source_target_pairs={{0,1},{1,0},{2,3},{3,2},{4,5},{5,4},{6,7},{7,6},{8,9},{9,8},{10,11... | collective-permute-start | bytes 8847368 | tf_op jit(solution)/shard_map/ppermute | solution.py:33
  580.4 7.3 fusion.73
  645.6 5.2 fusion.74
  660.8 9.5 %collective-permute-start.60 = (bf16[288,672]{1,0:T(8,128)(2,1)S(1)}, bf16[288,672]{1,0:T(8,128)(2,1)S(1)}, u32[]{:S(2)}, u32[]{:S(2)}) collective-permute-start(bf16[288,672]{1,0:T(8,128)(2,1)S(1)} %slice.384), channel_id=1, source_target_pairs={{16,0},{24,1},{0,2},{8,3},{18,8},{26,9},{2,10},{10,11},{17,16},{25... | collective-permute-start | bytes 1161224 | tf_op jit(solution)/shard_map/ppermute | solution.py:73
  675.6 22.0 %collective-permute-start.52 = (bf16[80,2304]{1,0:T(8,128)(2,1)}, bf16[80,2304]{1,0:T(8,128)(2,1)S(1)}, u32[]{:S(2)}, u32[]{:S(2)}) collective-permute-start(bf16[80,2304]{1,0:T(8,128)(2,1)} %get-tuple-element.207), channel_id=1, source_target_pairs={{0,24},{8,16},{16,8},{24,0},{1,25},{9,17},{17,9},{25,1},{2,26},{10... | collective-permute-start | bytes 1105928 | tf_op jit(solution)/shard_map/ppermute | solution.py:29
  697.6 16.1 %collective-permute-done.59 = bf16[288,768]{1,0:T(8,128)(2,1)S(1)} collective-permute-done((bf16[288,768]{1,0:T(8,128)(2,1)S(1)}, bf16[288,768]{1,0:T(8,128)(2,1)S(1)}, u32[]{:S(2)}, u32[]{:S(2)}) %collective-permute-start.59) | collective-permute-done | bytes 442400 | tf_op jit(solution)/shard_map/ppermute | solution.py:73
  716.0 5.8 convolution_convert_fusion
  735.0 26.0 %collective-permute-done.62 = f32[2,2304]{1,0:T(2,128)S(1)} collective-permute-done((f32[2,2304]{1,0:T(2,128)S(1)}, f32[2,2304]{1,0:T(2,128)S(1)}, u32[]{:S(2)}, u32[]{:S(2)}) %collective-permute-start.62) | collective-permute-done | bytes 18464 | tf_op jit(solution)/shard_map/ppermute | solution.py:541
  764.5 5.7 collective-permute-start.54
  783.6 6.8 collective-permute-start.57
  791.2 13.4 %collective-permute-done.53 = bf16[288,320]{1,0:T(8,128)(2,1)} collective-permute-done((bf16[288,320]{1,0:T(8,128)(2,1)}, bf16[288,320]{1,0:T(8,128)(2,1)}, u32[]{:S(2)}, u32[]{:S(2)}) %collective-permute-start.53) | collective-permute-done | bytes 184352 | tf_op jit(solution)/shard_map/ppermute | solution.py:73
  805.7 6.6 collective-permute-done.57
  (447 shorter events, 282.3 us)
Async XLA Ops:
  7.2 99.3 %all-gather.7.cloned.1.call-start = ((), (), s32[]{:S(2)}) async-start(), calls=%async_computation.7 | async-start | bytes 5971968 | tf_op jit(solution)/shard_map/all_gather | solution.py:91
  9.2 27.2 %collective-permute-start.4 = (bf16[288,640]{0,1:T(8,128)(2,1)S(1)}, bf16[288,640]{0,1:T(8,128)(2,1)S(1)}, u32[]{:S(2)}, u32[]{:S(2)}) collective-permute-start(bf16[288,640]{0,1:T(8,128)(2,1)S(1)} %slice.394), channel_id=1, source_target_pairs={{0,0},{1,8},{2,16},{3,24},{8,2},{9,10},{10,18},{11,26},{16,1},{17,... | collective-permute-start | bytes 1105928 | tf_op jit(solution)/shard_map/ppermute | solution.py:73
  37.7 110.2 %all-gather.9.cloned.1.call-start = ((), (), s32[]{:S(2)}) async-start(), calls=%async_computation.8 | async-start | bytes 3317760 | tf_op jit(solution)/shard_map/all_gather | solution.py:91
  47.8 33.7 %collective-permute-start.2 = (bf16[82,2304]{1,0:T(8,128)(2,1)S(1)}, bf16[82,2304]{1,0:T(8,128)(2,1)S(1)}, u32[]{:S(2)}, u32[]{:S(2)}) collective-permute-start(bf16[82,2304]{1,0:T(8,128)(2,1)S(1)} %pad_maximum_fusion.17), channel_id=1, source_target_pairs={{0,16},{8,24},{16,0},{24,8},{1,17},{9,25},{17,1},{25,9},{2,18},{10... | collective-permute-start | bytes 1133576 | tf_op jit(solution)/shard_map/ppermute | solution.py:29
  49.0 32.5 %collective-permute-start.3 = (bf16[82,2304]{1,0:T(8,128)(2,1)S(1)}, bf16[82,2304]{1,0:T(8,128)(2,1)}, u32[]{:S(2)}, u32[]{:S(2)}) collective-permute-start(bf16[82,2304]{1,0:T(8,128)(2,1)S(1)} %pad_maximum_fusion.17), channel_id=1, source_target_pairs={{0,24},{8,16},{16,8},{24,0},{1,25},{9,17},{17,9},{25,1},{2,26},{10... | collective-permute-start | bytes 1133576 | tf_op jit(solution)/shard_map/ppermute | solution.py:29
  60.0 174.9 %all-gather.11.cloned.1.call-start = ((), (), s32[]{:S(2)}) async-start(), calls=%async_computation.9 | async-start | bytes 3317760 | tf_op jit(solution)/shard_map/all_gather | solution.py:91
  85.6 27.3 %collective-permute-start.6 = (bf16[288,320]{1,0:T(8,128)(2,1)}, bf16[288,320]{1,0:T(8,128)(2,1)}, u32[]{:S(2)}, u32[]{:S(2)}) collective-permute-start(bf16[288,320]{1,0:T(8,128)(2,1)} %slice.385), channel_id=1, source_target_pairs={{0,0},{1,8},{2,16},{3,24},{8,2},{9,10},{10,18},{11,26},{16,1},{17,... | collective-permute-start | bytes 552968 | tf_op jit(solution)/shard_map/ppermute | solution.py:73
  98.3 27.2 %collective-permute-start.8 = (bf16[288,768]{1,0:T(8,128)(2,1)}, bf16[288,768]{1,0:T(8,128)(2,1)}, u32[]{:S(2)}, u32[]{:S(2)}) collective-permute-start(bf16[288,768]{1,0:T(8,128)(2,1)} %slice.387), channel_id=1, source_target_pairs={{0,0},{1,8},{2,16},{3,24},{8,2},{9,10},{10,18},{11,26},{16,1},{17,... | collective-permute-start | bytes 1327112 | tf_op jit(solution)/shard_map/ppermute | solution.py:73
  127.4 188.0 %all-gather.17.cloned.1.call-start = ((), (), s32[]{:S(2)}) async-start(), calls=%async_computation.12 | async-start | bytes 7962624 | tf_op jit(solution)/shard_map/all_gather | solution.py:91
  132.4 62.7 %all-to-all-start = ((bf16[4,320,1152]{2,1,0:T(8,128)(2,1)}), bf16[4,320,1152]{2,1,0:T(8,128)(2,1)S(1)}, u32[]{:S(2)}, u32[]{:S(2)}) async-start(bf16[4,320,1152]{2,1,0:T(8,128)(2,1)} %broadcast_in_dim.22), calls=%async_computation | async-start | bytes 5898240 | tf_op jit(solution)/shard_map/all_to_all | solution.py:109
  136.3 186.0 %all-gather.13.cloned.1.call-start = ((), (), s32[]{:S(2)}) async-start(), calls=%async_computation.10 | async-start | bytes 7962624 | tf_op jit(solution)/shard_map/all_gather | solution.py:91
  138.0 44.7 %collective-permute-start.10 = (bf16[288,768]{1,0:T(8,128)(2,1)}, bf16[288,768]{1,0:T(8,128)(2,1)}, u32[]{:S(2)}, u32[]{:S(2)}) collective-permute-start(bf16[288,768]{1,0:T(8,128)(2,1)} %slice.389), channel_id=1, source_target_pairs={{0,0},{1,8},{2,16},{3,24},{8,2},{9,10},{10,18},{11,26},{16,1},{17,... | collective-permute-start | bytes 1327112 | tf_op jit(solution)/shard_map/ppermute | solution.py:73
  139.9 33.5 %collective-permute-start.11 = (bf16[288,672]{1,0:T(8,128)(2,1)}, bf16[288,672]{1,0:T(8,128)(2,1)}, u32[]{:S(2)}, u32[]{:S(2)}) collective-permute-start(bf16[288,672]{1,0:T(8,128)(2,1)} %slice.390), channel_id=1, source_target_pairs={{0,16},{1,24},{2,0},{3,8},{8,18},{9,26},{10,2},{11,10},{16,17},{17... | collective-permute-start | bytes 1161224 | tf_op jit(solution)/shard_map/ppermute | solution.py:73
  144.6 38.1 %collective-permute-start.12 = (bf16[288,768]{1,0:T(8,128)(2,1)}, bf16[288,768]{1,0:T(8,128)(2,1)}, u32[]{:S(2)}, u32[]{:S(2)}) collective-permute-start(bf16[288,768]{1,0:T(8,128)(2,1)} %slice.391), channel_id=1, source_target_pairs={{0,0},{1,8},{2,16},{3,24},{8,2},{9,10},{10,18},{11,26},{16,1},{17,... | collective-permute-start | bytes 1327112 | tf_op jit(solution)/shard_map/ppermute | solution.py:73
  146.5 36.2 %collective-permute-start.13 = (bf16[288,672]{1,0:T(8,128)(2,1)}, bf16[288,672]{1,0:T(8,128)(2,1)}, u32[]{:S(2)}, u32[]{:S(2)}) collective-permute-start(bf16[288,672]{1,0:T(8,128)(2,1)} %slice.392), channel_id=1, source_target_pairs={{0,16},{1,24},{2,0},{3,8},{8,18},{9,26},{10,2},{11,10},{16,17},{17... | collective-permute-start | bytes 1161224 | tf_op jit(solution)/shard_map/ppermute | solution.py:73
  197.3 148.9 %all-gather.15.cloned.1.call-start = ((), (), s32[]{:S(2)}) async-start(), calls=%async_computation.11 | async-start | bytes 7962624 | tf_op jit(solution)/shard_map/all_gather | solution.py:91
  200.3 40.8 %collective-permute-start.20 = (bf16[80,2304]{1,0:T(8,128)(2,1)}, bf16[80,2304]{1,0:T(8,128)(2,1)}, u32[]{:S(2)}, u32[]{:S(2)}) collective-permute-start(bf16[80,2304]{1,0:T(8,128)(2,1)} %fusion.28), channel_id=1, source_target_pairs={{0,8},{8,0},{16,24},{24,16},{1,9},{9,1},{17,25},{25,17},{2,10},{10... | collective-permute-start | bytes 1105928 | tf_op jit(solution)/shard_map/ppermute | solution.py:29
  203.4 39.7 %collective-permute-start.21 = (bf16[80,2304]{1,0:T(8,128)(2,1)}, bf16[80,2304]{1,0:T(8,128)(2,1)}, u32[]{:S(2)}, u32[]{:S(2)}) collective-permute-start(bf16[80,2304]{1,0:T(8,128)(2,1)} %fusion.28), channel_id=1, source_target_pairs={{0,16},{8,24},{16,0},{24,8},{1,17},{9,25},{17,1},{25,9},{2,18},{10... | collective-permute-start | bytes 1105928 | tf_op jit(solution)/shard_map/ppermute | solution.py:29
  203.4 39.7 %collective-permute-start.22 = (bf16[80,2304]{1,0:T(8,128)(2,1)}, bf16[80,2304]{1,0:T(8,128)(2,1)}, u32[]{:S(2)}, u32[]{:S(2)}) collective-permute-start(bf16[80,2304]{1,0:T(8,128)(2,1)} %fusion.28), channel_id=1, source_target_pairs={{0,24},{8,16},{16,8},{24,0},{1,25},{9,17},{17,9},{25,1},{2,26},{10... | collective-permute-start | bytes 1105928 | tf_op jit(solution)/shard_map/ppermute | solution.py:29
  269.5 39.4 %collective-permute-start.24 = (bf16[80,2304]{1,0:T(8,128)(2,1)S(1)}, bf16[80,2304]{1,0:T(8,128)(2,1)S(1)}, u32[]{:S(2)}, u32[]{:S(2)}) collective-permute-start(bf16[80,2304]{1,0:T(8,128)(2,1)S(1)} %multiply_convert_fusion.4), channel_id=1, source_target_pairs={{0,16},{8,24},{16,0},{24,8},{1,17},{9,25},{17,1},{25,9},{2,18},{10... | collective-permute-start | bytes 1105928 | tf_op jit(solution)/shard_map/ppermute | solution.py:29
  314.1 60.5 %collective-permute-start.26 = (bf16[320,1152]{1,0:T(8,128)(2,1)}, bf16[320,1152]{1,0:T(8,128)(2,1)}, u32[]{:S(2)}, u32[]{:S(2)}) collective-permute-start(bf16[320,1152]{1,0:T(8,128)(2,1)} %get-tuple-element.223), channel_id=1, source_target_pairs={{0,1},{1,0},{2,3},{3,2},{4,5},{5,4},{6,7},{7,6},{8,9},{9,8},{10,11... | collective-permute-start | bytes 2211848 | tf_op jit(solution)/shard_map/ppermute | solution.py:33
  386.1 45.0 %all-to-all-start.1 = ((bf16[4,288,1440]{2,1,0:T(8,128)(2,1)}), bf16[4,288,1440]{2,1,0:T(8,128)(2,1)}, u32[]{:S(2)}, u32[]{:S(2)}) async-start(bf16[4,288,1440]{2,1,0:T(8,128)(2,1)} %bitcast.138), calls=%async_computation.1 | async-start | bytes 7077888 | tf_op jit(solution)/shard_map/all_to_all | solution.py:109
  394.5 27.1 %collective-permute-start.29 = (bf16[80,2304]{1,0:T(8,128)(2,1)}, bf16[80,2304]{1,0:T(8,128)(2,1)S(1)}, u32[]{:S(2)}, u32[]{:S(2)}) collective-permute-start(bf16[80,2304]{1,0:T(8,128)(2,1)} %get-tuple-element.219), channel_id=1, source_target_pairs={{0,8},{8,0},{16,24},{24,16},{1,9},{9,1},{17,25},{25,17},{2,10},{10... | collective-permute-start | bytes 1105928 | tf_op jit(solution)/shard_map/ppermute | solution.py:29
  395.7 25.9 %collective-permute-start.30 = (bf16[80,2304]{1,0:T(8,128)(2,1)}, bf16[80,2304]{1,0:T(8,128)(2,1)S(1)}, u32[]{:S(2)}, u32[]{:S(2)}) collective-permute-start(bf16[80,2304]{1,0:T(8,128)(2,1)} %get-tuple-element.218), channel_id=1, source_target_pairs={{0,16},{8,24},{16,0},{24,8},{1,17},{9,25},{17,1},{25,9},{2,18},{10... | collective-permute-start | bytes 1105928 | tf_op jit(solution)/shard_map/ppermute | solution.py:29
  431.1 45.1 %all-to-all-start.2 = ((bf16[4,288,1440]{2,1,0:T(8,128)(2,1)}), bf16[4,288,1440]{2,1,0:T(8,128)(2,1)}, u32[]{:S(2)}, u32[]{:S(2)}) async-start(bf16[4,288,1440]{2,1,0:T(8,128)(2,1)} %bitcast.137), calls=%async_computation.2 | async-start | bytes 7077888 | tf_op jit(solution)/shard_map/all_to_all | solution.py:109
  487.1 69.1 %all-to-all-start.3 = ((bf16[4,288,1440]{2,1,0:T(8,128)(2,1)}), bf16[4,288,1440]{2,1,0:T(8,128)(2,1)S(1)}, u32[]{:S(2)}, u32[]{:S(2)}) async-start(bf16[4,288,1440]{2,1,0:T(8,128)(2,1)} %bitcast.136), calls=%async_computation.3 | async-start | bytes 7077888 | tf_op jit(solution)/shard_map/all_to_all | solution.py:109
  490.8 48.7 %collective-permute-start.37 = (bf16[288,768]{1,0:T(8,128)(2,1)}, bf16[288,768]{1,0:T(8,128)(2,1)S(1)}, u32[]{:S(2)}, u32[]{:S(2)}) collective-permute-start(bf16[288,768]{1,0:T(8,128)(2,1)} %slice.350), channel_id=1, source_target_pairs={{0,0},{8,1},{16,2},{24,3},{2,8},{10,9},{18,10},{26,11},{1,16},{9,1... | collective-permute-start | bytes 1327112 | tf_op jit(solution)/shard_map/ppermute | solution.py:73
  496.4 27.5 %collective-permute-start.38 = (bf16[288,672]{1,0:T(8,128)(2,1)}, bf16[288,672]{1,0:T(8,128)(2,1)S(1)}, u32[]{:S(2)}, u32[]{:S(2)}) collective-permute-start(bf16[288,672]{1,0:T(8,128)(2,1)} %slice.351), channel_id=1, source_target_pairs={{16,0},{24,1},{0,2},{8,3},{18,8},{26,9},{2,10},{10,11},{17,16},{25... | collective-permute-start | bytes 1161224 | tf_op jit(solution)/shard_map/ppermute | solution.py:73
  498.4 50.8 %collective-permute-start.39 = (bf16[288,768]{1,0:T(8,128)(2,1)}, bf16[288,768]{1,0:T(8,128)(2,1)}, u32[]{:S(2)}, u32[]{:S(2)}) collective-permute-start(bf16[288,768]{1,0:T(8,128)(2,1)} %slice.420), channel_id=1, source_target_pairs={{0,0},{8,1},{16,2},{24,3},{2,8},{10,9},{18,10},{26,11},{1,16},{9,1... | collective-permute-start | bytes 1327112 | tf_op jit(solution)/shard_map/ppermute | solution.py:73
  500.3 36.7 %collective-permute-start.40 = (bf16[288,672]{1,0:T(8,128)(2,1)}, bf16[288,672]{1,0:T(8,128)(2,1)S(1)}, u32[]{:S(2)}, u32[]{:S(2)}) collective-permute-start(bf16[288,672]{1,0:T(8,128)(2,1)} %slice.421), channel_id=1, source_target_pairs={{16,0},{24,1},{0,2},{8,3},{18,8},{26,9},{2,10},{10,11},{17,16},{25... | collective-permute-start | bytes 1161224 | tf_op jit(solution)/shard_map/ppermute | solution.py:73
  561.9 25.8 %collective-permute-start.41 = (bf16[4,320,1152]{2,1,0:T(8,128)(2,1)}, bf16[4,320,1152]{2,1,0:T(8,128)(2,1)}, u32[]{:S(2)}, u32[]{:S(2)}) collective-permute-start(bf16[4,320,1152]{2,1,0:T(8,128)(2,1)} %bitcast.40), channel_id=1, source_target_pairs={{0,1},{1,0},{2,3},{3,2},{4,5},{5,4},{6,7},{7,6},{8,9},{9,8},{10,11... | collective-permute-start | bytes 8847368 | tf_op jit(solution)/shard_map/ppermute | solution.py:33
  577.9 38.5 %collective-permute-start.42 = (bf16[320,1152]{1,0:T(8,128)(2,1)}, bf16[320,1152]{1,0:T(8,128)(2,1)}, u32[]{:S(2)}, u32[]{:S(2)}) collective-permute-start(bf16[320,1152]{1,0:T(8,128)(2,1)} %get-tuple-element.216), channel_id=1, source_target_pairs={{0,1},{1,0},{2,3},{3,2},{4,5},{5,4},{6,7},{7,6},{8,9},{9,8},{10,11... | collective-permute-start | bytes 2211848 | tf_op jit(solution)/shard_map/ppermute | solution.py:33
  591.8 39.7 %all-to-all-start.4 = ((bf16[4,320,1152]{2,1,0:T(8,128)(2,1)}), bf16[4,320,1152]{2,1,0:T(8,128)(2,1)}, u32[]{:S(2)}, u32[]{:S(2)}) async-start(bf16[4,320,1152]{2,1,0:T(8,128)(2,1)} %fusion), calls=%async_computation.4 | async-start | bytes 5898240 | tf_op jit(solution)/shard_map/all_to_all | solution.py:109
  625.3 28.1 %collective-permute-start.46 = (bf16[80,2304]{1,0:T(8,128)(2,1)}, bf16[80,2304]{1,0:T(8,128)(2,1)S(1)}, u32[]{:S(2)}, u32[]{:S(2)}) collective-permute-start(bf16[80,2304]{1,0:T(8,128)(2,1)} %get-tuple-element.212), channel_id=1, source_target_pairs={{0,8},{8,0},{16,24},{24,16},{1,9},{9,1},{17,25},{25,17},{2,10},{10... | collective-permute-start | bytes 1105928 | tf_op jit(solution)/shard_map/ppermute | solution.py:29
  626.8 26.6 %collective-permute-start.47 = (bf16[80,2304]{1,0:T(8,128)(2,1)}, bf16[80,2304]{1,0:T(8,128)(2,1)}, u32[]{:S(2)}, u32[]{:S(2)}) collective-permute-start(bf16[80,2304]{1,0:T(8,128)(2,1)} %get-tuple-element.211), channel_id=1, source_target_pairs={{0,16},{8,24},{16,0},{24,8},{1,17},{9,25},{17,1},{25,9},{2,18},{10... | collective-permute-start | bytes 1105928 | tf_op jit(solution)/shard_map/ppermute | solution.py:29
  640.8 81.1 %all-to-all-start.5 = ((bf16[4,288,1152]{2,1,0:T(8,128)(2,1)}), bf16[4,288,1152]{2,1,0:T(8,128)(2,1)}, u32[]{:S(2)}, u32[]{:S(2)}) async-start(bf16[4,288,1152]{2,1,0:T(8,128)(2,1)} %pad_maximum_fusion.1), calls=%async_computation.5 | async-start | bytes 5308416 | tf_op jit(solution)/shard_map/all_to_all | solution.py:109
  658.5 55.3 %collective-permute-start.49 = (bf16[320,1152]{1,0:T(8,128)(2,1)}, bf16[320,1152]{1,0:T(8,128)(2,1)}, u32[]{:S(2)}, u32[]{:S(2)}) collective-permute-start(bf16[320,1152]{1,0:T(8,128)(2,1)} %copy.111), channel_id=1, source_target_pairs={{0,1},{1,0},{2,3},{3,2},{4,5},{5,4},{6,7},{7,6},{8,9},{9,8},{10,11... | collective-permute-start | bytes 2211848 | tf_op jit(solution)/shard_map/ppermute | solution.py:33
  670.2 43.5 %collective-permute-start.59 = (bf16[288,768]{1,0:T(8,128)(2,1)S(1)}, bf16[288,768]{1,0:T(8,128)(2,1)S(1)}, u32[]{:S(2)}, u32[]{:S(2)}) collective-permute-start(bf16[288,768]{1,0:T(8,128)(2,1)S(1)} %slice.383), channel_id=1, source_target_pairs={{0,0},{8,1},{16,2},{24,3},{2,8},{10,9},{18,10},{26,11},{1,16},{9,1... | collective-permute-start | bytes 1327112 | tf_op jit(solution)/shard_map/ppermute | solution.py:73
  673.2 48.6 %collective-permute-start.50 = (bf16[80,2304]{1,0:T(8,128)(2,1)}, bf16[80,2304]{1,0:T(8,128)(2,1)}, u32[]{:S(2)}, u32[]{:S(2)}) collective-permute-start(bf16[80,2304]{1,0:T(8,128)(2,1)} %get-tuple-element.209), channel_id=1, source_target_pairs={{0,8},{8,0},{16,24},{24,16},{1,9},{9,1},{17,25},{25,17},{2,10},{10... | collective-permute-start | bytes 1105928 | tf_op jit(solution)/shard_map/ppermute | solution.py:29
  673.6 48.2 %collective-permute-start.51 = (bf16[80,2304]{1,0:T(8,128)(2,1)}, bf16[80,2304]{1,0:T(8,128)(2,1)}, u32[]{:S(2)}, u32[]{:S(2)}) collective-permute-start(bf16[80,2304]{1,0:T(8,128)(2,1)} %get-tuple-element.208), channel_id=1, source_target_pairs={{0,16},{8,24},{16,0},{24,8},{1,17},{9,25},{17,1},{25,9},{2,18},{10... | collective-permute-start | bytes 1105928 | tf_op jit(solution)/shard_map/ppermute | solution.py:29
  675.6 46.2 %collective-permute-start.52 = (bf16[80,2304]{1,0:T(8,128)(2,1)}, bf16[80,2304]{1,0:T(8,128)(2,1)S(1)}, u32[]{:S(2)}, u32[]{:S(2)}) collective-permute-start(bf16[80,2304]{1,0:T(8,128)(2,1)} %get-tuple-element.207), channel_id=1, source_target_pairs={{0,24},{8,16},{16,8},{24,0},{1,25},{9,17},{17,9},{25,1},{2,26},{10... | collective-permute-start | bytes 1105928 | tf_op jit(solution)/shard_map/ppermute | solution.py:29
  726.5 46.3 %all-to-all-start.6 = ((bf16[4,288,1152]{2,1,0:T(8,128)(2,1)}), bf16[4,288,1152]{2,1,0:T(8,128)(2,1)S(1)}, u32[]{:S(2)}, u32[]{:S(2)}) async-start(bf16[4,288,1152]{2,1,0:T(8,128)(2,1)} %bitcast.155), calls=%async_computation.6 | async-start | bytes 5308416 | tf_op jit(solution)/shard_map/all_to_all | solution.py:109
  732.7 28.3 %collective-permute-start.62 = (f32[2,2304]{1,0:T(2,128)S(1)}, f32[2,2304]{1,0:T(2,128)S(1)}, u32[]{:S(2)}, u32[]{:S(2)}) collective-permute-start(f32[2,2304]{1,0:T(2,128)S(1)} %fusion.57), channel_id=1, source_target_pairs={{0,2},{2,0},{1,3},{3,1},{4,6},{6,4},{5,7},{7,5},{8,10},{10,8},{9,1... | collective-permute-start | bytes 55304 | tf_op jit(solution)/shard_map/ppermute | solution.py:541
  764.5 25.9 %collective-permute-start.54 = (bf16[288,256]{1,0:T(8,128)(2,1)}, bf16[288,256]{1,0:T(8,128)(2,1)}, u32[]{:S(2)}, u32[]{:S(2)}) collective-permute-start(bf16[288,256]{1,0:T(8,128)(2,1)} %get-tuple-element.245), channel_id=1, source_target_pairs={{16,0},{24,1},{0,2},{8,3},{18,8},{26,9},{2,10},{10,11},{17,16},{25... | collective-permute-start | bytes 442376 | tf_op jit(solution)/shard_map/ppermute | solution.py:73
  770.2 34.4 %collective-permute-start.53 = (bf16[288,320]{1,0:T(8,128)(2,1)}, bf16[288,320]{1,0:T(8,128)(2,1)}, u32[]{:S(2)}, u32[]{:S(2)}) collective-permute-start(bf16[288,320]{1,0:T(8,128)(2,1)} %get-tuple-element.243), channel_id=1, source_target_pairs={{0,0},{8,1},{16,2},{24,3},{2,8},{10,9},{18,10},{26,11},{1,16},{9,1... | collective-permute-start | bytes 552968 | tf_op jit(solution)/shard_map/ppermute | solution.py:73
  772.4 33.4 %collective-permute-start.58 = (bf16[288,256]{1,0:T(8,128)(2,1)}, bf16[288,256]{1,0:T(8,128)(2,1)}, u32[]{:S(2)}, u32[]{:S(2)}) collective-permute-start(bf16[288,256]{1,0:T(8,128)(2,1)} %get-tuple-element.244), channel_id=1, source_target_pairs={{16,0},{24,1},{0,2},{8,3},{18,8},{26,9},{2,10},{10,11},{17,16},{25... | collective-permute-start | bytes 442376 | tf_op jit(solution)/shard_map/ppermute | solution.py:73
  775.2 39.1 %collective-permute-start.55 = (bf16[288,640]{1,0:T(8,128)(2,1)S(1)}, bf16[288,640]{1,0:T(8,128)(2,1)S(1)}, u32[]{:S(2)}, u32[]{:S(2)}) collective-permute-start(bf16[288,640]{1,0:T(8,128)(2,1)S(1)} %slice.441), channel_id=1, source_target_pairs={{0,0},{8,1},{16,2},{24,3},{2,8},{10,9},{18,10},{26,11},{1,16},{9,1... | collective-permute-start | bytes 1105928 | tf_op jit(solution)/shard_map/ppermute | solution.py:73
  783.6 28.8 %collective-permute-start.57 = (bf16[288,320]{1,0:T(8,128)(2,1)S(1)}, bf16[288,320]{1,0:T(8,128)(2,1)S(1)}, u32[]{:S(2)}, u32[]{:S(2)}) collective-permute-start(bf16[288,320]{1,0:T(8,128)(2,1)S(1)} %copy-done.40), channel_id=1, source_target_pairs={{0,0},{8,1},{16,2},{24,3},{2,8},{10,9},{18,10},{26,11},{1,16},{9,1... | collective-permute-start | bytes 552968 | tf_op jit(solution)/shard_map/ppermute | solution.py:73
  (88 other events, 1544.4 us)
Sparse Core Ops, SparseCore 0:
  37.8 43.0 all-gather.6
  83.4 40.5 all-gather.8
  127.5 62.9 all-gather.10
  192.2 52.1 all-gather.16
  246.7 48.8 all-gather.12
  297.4 48.7 all-gather.14

commit v3 on v2

--- a/solution.py
+++ b/solution.py
@@ -55,8 +55,20 @@
     return total
 
 
-def halves(array, cut):
-    return [array[:, :cut], array[:, cut:]]
+def bundle(arrays, cuts):
+    return [
+        columns([a[:, :cut] for a, cut in zip(arrays, cuts)]),
+        columns([a[:, cut:] for a, cut in zip(arrays, cuts)]),
+    ]
+
+
+def unbundle(parts, widths, cuts):
+    arrays, first, second = [], 0, 0
+    for wide, cut in zip(widths, cuts):
+        rest = wide - cut
+        arrays.append(columns([parts[0][:, first : first + cut], parts[1][:, second : second + rest]]))
+        first, second = first + cut, second + rest
+    return arrays
 
 
 def turn(parts, back=False):
@@ -91,18 +103,43 @@
     return lax.all_gather(piece, PLANE, axis=0, tiled=True)
 
 
+def core_halves(array):
+    half = array.shape[1] // 2
+    first = lax.axis_index("tc") == 0
+    left, right = array[:, :half], array[:, half:]
+    return jnp.where(first, left, right), jnp.where(first, right, left)
+
+
 def with_twin(left):
-    half = left.shape[1] // 2
-    first = lax.axis_index("tc") == 0
-    mine = jnp.where(first, left[:, :half], left[:, half:])
-    other = jnp.where(first, left[:, half:], left[:, :half])
-    return rows_of([mine, swap_core(other)])
+    mine, other = core_halves(left)
+    return [mine, swap_core(other)]
+
+
+def pair_kernel(left_ref, left_far_ref, right_ref, right_far_ref, out_ref):
+    total = dot(left_ref[...], right_ref[...], ((0,), (0,)))
+    total += dot(left_far_ref[...], right_far_ref[...], ((0,), (0,)))
+    out_ref[...] = total.astype(bf16)
 
 
 def pair_sum(left, right):
     chips = lax.axis_size("pb") * lax.axis_size("tx")
-    total = dot(rows_of([right, swap_core(right)]), left, ((0,), (0,))).astype(bf16).T
-    return total.reshape(chips, -1, total.shape[1])
+    tokens, rows = left[0].shape
+    wide = right.shape[1]
+    tile = 384 if rows % 384 == 0 else rows
+    lefts = pl.BlockSpec((tokens, tile), lambda i: (0, i))
+    rights = pl.BlockSpec((tokens, wide), lambda i: (0, 0))
+    total = pl.pallas_call(
+        pair_kernel,
+        grid=(rows // tile,),
+        in_specs=[lefts, lefts, rights, rights],
+        out_specs=pl.BlockSpec((tile, wide), lambda i: (i, 0)),
+        out_shape=jax.ShapeDtypeStruct((rows, wide), bf16),
+        compiler_params=pltpu.CompilerParams(vmem_limit_bytes=40 * 2**20),
+        cost_estimate=pl.CostEstimate(
+            flops=4 * tokens * rows * wide, bytes_accessed=2 * rows * wide, transcendentals=0
+        ),
+    )(*left, right, swap_core(right))
+    return total.reshape(chips, -1, wide)
 
 
 def exchange(blocks):
@@ -184,10 +221,9 @@
     )
 
 
-def keys_of(kv_ref, row, quarter, part, spans):
-    count = kv_ref.shape[0] // spans
-    block = kv_ref[pl.ds(part * count, count), quarter ^ row]
-    return block.reshape(-1, 2 * HD)
+def span_of(refs, row, quarter, part, count):
+    where = (pl.ds(part * count, count), quarter ^ row)
+    return rows_of([ref[where].reshape(-1, 2 * HD) for ref in refs])
 
 
 def lower(top, change, skip):
@@ -196,16 +232,17 @@
     return jnp.concatenate([top[:skip], change(top[skip:])], axis=0)
 
 
-def attend_kernel(row_ref, query_ref, key_ref, q_ref, kv_ref, out_ref, bias_ref):
-    chunks, height = kv_ref.shape[1:3]
+def attend_kernel(row_ref, query_ref, key_ref, q_ref, near_ref, far_ref, out_ref, bias_ref):
+    chips, chunks, height = near_ref.shape[:3]
     spans = key_ref.shape[0] // chunks
+    count = chips // spans
     row = row_ref[0]
     fill_bias(query_ref, key_ref, bias_ref)
     q = in_token_order(q_ref, row, chunks)
 
     def span(part, carry):
         peak, total, mixed = carry
-        keys = [keys_of(kv_ref, row, n, part, spans) for n in range(chunks)]
+        keys = [span_of((near_ref, far_ref), row, n, part, count) for n in range(chunks)]
         scores = [
             dot(q[n * height :], keys[n], ((1,), (1,))) + bias_ref[n * spans + part, n * height :, :]
             for n in range(chunks)
@@ -240,11 +277,22 @@
 
 
 def attend_back_kernel(
-    row_ref, query_ref, key_ref, q_ref, kv_ref, out_ref, grad_ref, grad_q_ref, grad_kv_ref, bias_ref
+    row_ref,
+    query_ref,
+    key_ref,
+    q_ref,
+    near_ref,
+    far_ref,
+    out_ref,
+    grad_ref,
+    grad_q_ref,
+    grad_near_ref,
+    grad_far_ref,
+    bias_ref,
 ):
-    chunks, height = kv_ref.shape[1:3]
+    chips, chunks, height = near_ref.shape[:3]
     spans = key_ref.shape[0] // chunks
-    count = kv_ref.shape[0] // spans
+    count = chips // spans
     row = row_ref[0]
     fill_bias(query_ref, key_ref, bias_ref)
     q = in_token_order(q_ref, row, chunks)
@@ -256,7 +304,7 @@
     def span(part, grad_q):
         for n in range(chunks):
             skip = n * height
-            keys = keys_of(kv_ref, row, n, part, spans)
+            keys = span_of((near_ref, far_ref), row, n, part, count)
             scores = dot(q[skip:], keys, ((1,), (1,))) + bias_ref[n * spans + part, skip:, :]
             probs = jnp.exp(scores - log_total[skip:])
             grad_probs = dot(grad[skip:], keys, ((1,), (1,)))
@@ -264,9 +312,10 @@
             added = dot(grad_scores, q[skip:], ((0,), (0,))) + dot(
                 probs.astype(bf16), grad[skip:], ((0,), (0,))
             )
-            grad_kv_ref[pl.ds(part * count, count), n ^ row] = added.astype(bf16).reshape(
-                count, height, 2 * HD
-            )
+            added = added.astype(bf16).reshape(2, count, height, 2 * HD)
+            where = (pl.ds(part * count, count), n ^ row)
+            grad_near_ref[where] = added[0]
+            grad_far_ref[where] = added[1]
             more = dot(grad_scores, keys)
             grad_q = lower(grad_q, lambda v: v + more, skip)
         return grad_q
@@ -282,7 +331,7 @@
 def attention_specs(queries, kv, query_info, key_info):
     heads = queries.shape[1] // (2 * HD)
     rows = pl.BlockSpec((queries.shape[0], 2 * HD), lambda h: (0, h))
-    keys = pl.BlockSpec(kv.shape[:3] + (2 * HD,), lambda h: (0, 0, 0, h))
+    keys = pl.BlockSpec(kv[0].shape[:3] + (2 * HD,), lambda h: (0, 0, 0, h))
     fixed = [
         pl.BlockSpec(memory_space=pltpu.SMEM),
         pl.BlockSpec(query_info.shape, lambda h: (0, 0)),
@@ -293,9 +342,9 @@
     return heads, rows, keys, fixed, bias, params
 
 
-def work(queries, kv, products):
+def work(kv, products):
     return pl.CostEstimate(
-        flops=products * kv.size * 8000, bytes_accessed=4 * kv.size, transcendentals=0
+        flops=products * kv[0].size * 16000, bytes_accessed=8 * kv[0].size, transcendentals=0
     )
 
 
@@ -304,13 +353,13 @@
     return pl.pallas_call(
         attend_kernel,
         grid=(heads,),
-        in_specs=fixed + [rows, keys],
+        in_specs=fixed + [rows, keys, keys],
         out_specs=rows,
         out_shape=jax.ShapeDtypeStruct(queries.shape, f32),
         scratch_shapes=[bias],
         compiler_params=params,
-        cost_estimate=work(queries, kv, 2),
-    )(row, query_info, key_info, queries, kv)
+        cost_estimate=work(kv, 2),
+    )(row, query_info, key_info, queries, *kv)
 
 
 def attend_back(row, query_info, key_info, queries, kv, saved, grad):
@@ -318,16 +367,14 @@
     return pl.pallas_call(
         attend_back_kernel,
         grid=(heads,),
-        in_specs=fixed + [rows, keys, rows, rows],
-        out_specs=[rows, keys],
-        out_shape=[
-            jax.ShapeDtypeStruct(queries.shape, f32),
-            jax.ShapeDtypeStruct(kv.shape, bf16),
-        ],
+        in_specs=fixed + [rows, keys, keys, rows, rows],
+        out_specs=[rows, keys, keys],
+        out_shape=[jax.ShapeDtypeStruct(queries.shape, f32)]
+        + [jax.ShapeDtypeStruct(t.shape, bf16) for t in kv],
         scratch_shapes=[bias],
         compiler_params=params,
-        cost_estimate=work(queries, kv, 5),
-    )(row, query_info, key_info, queries, kv, saved, grad)
+        cost_estimate=work(kv, 5),
+    )(row, query_info, key_info, queries, *kv, saved, grad)
 
 
 def on_device(
@@ -369,24 +416,20 @@
     small = jnp.concatenate(
         [norm_gains.reshape(-1)] + [t.astype(bf16) for t in (tok_seg, tok_pos // low, tok_pos % low)]
     )
-    small = jnp.pad(small, (0, width - small.shape[0]))
+    small = jnp.pad(small, (0, width - small.shape[0]))[None]
+    x_own = block_input
+    x_parts = row_send(rows_of([x_own, small]))
+    kv_full = plane_gather(*unbundle(turn(bundle([w_kv], [near * 2 * HD])), [2 * features], [near * 2 * HD]))
+    q_full = plane_gather(*unbundle(turn(bundle([w_qkv[0]], [near * HD])), [features], [near * HD]))
+    first = bundle([w_gate_up[0], w_gate_up[1], w_out.T], [near_units, near_units, near * HD])
+    second = bundle([w_down.T], [near_units])
+    x_parts, first, second = fence(x_parts, first, second)
+    first = turn(first)
+    small = rows_of([part[own:] for part in x_parts])
     small = [small] + [
         lax.ppermute(small, "pb", [(i, i ^ k) for i in range(b_n)]) for k in range(1, b_n)
     ]
-    kv_full = plane_gather(columns(turn(halves(w_kv, near * 2 * HD))))
-    q_full = plane_gather(columns(turn(halves(w_qkv[0], near * HD))))
-    x_own = block_input
-    x_parts = row_send(jnp.concatenate([x_own, jnp.stack(small)], axis=0))
-    x_parts, out_halves, gate_halves, up_halves, down_halves = fence(
-        x_parts,
-        halves(w_out.T, near * HD),
-        halves(w_gate_up[0], near_units),
-        halves(w_gate_up[1], near_units),
-        halves(w_down.T, near_units),
-    )
-    out_moved = turn(out_halves)
-    gate_moved = turn(gate_halves)
-    small = jnp.stack([part[own:] for part in x_parts])
+    small = jnp.stack(small, axis=1)
     gains = small[..., : 2 * norm_gains.shape[1]].reshape(rows_n, b_n, 2, -1)
     group = tok_seg.shape[0]
     small = small[..., gains.shape[3] * 2 :][..., : 3 * group].astype(jnp.int32)
@@ -405,8 +448,8 @@
         return lax.dynamic_slice_in_dim(array, c, 1, 3).reshape(-1)
 
     def for_keys(array):
-        array = untangle(array, 3, c).transpose(0, 3, 2, 1, 4)
-        return array.reshape(-1, 8 * own)
+        array = untangle(array, 3, c).transpose(0, 3, 2, 1, 4).reshape(rows_n, 2, -1, 4, own)
+        return array.transpose(0, 2, 1, 3, 4).reshape(-1, 8 * own)
 
     own_seg, own_index, pos_group = for_group(seg_all), for_group(index_all), for_group(pos_all)
     parent_seg, grand_seg = lineage(own_seg, seg_parent)
@@ -423,29 +466,30 @@
     mine = dot(normed_a, kv_full).reshape(group, heads, 2, HD)
     keys = rotate(mine[:, :, 0].reshape(group, -1), cosine, sine_table).astype(bf16)
     mine = side_by_side(keys, mine[:, :, 1].reshape(group, -1).astype(bf16))
-    mine, out_moved, gate_moved, up_halves, down_halves, branch_f = fence(
-        mine, out_moved, gate_moved, up_halves, down_halves, branch_f
-    )
-    out_full = plane_gather(columns(out_moved))
-    gate_full = plane_gather(columns(gate_moved))
-    up_moved = turn(up_halves)
-    down_moved = turn(down_halves)
+    mine, second, branch_f, query_info, key_info = fence(
+        mine, second, branch_f, query_info, key_info
+    )
+    gate_moved, up_moved, out_moved = unbundle(
+        after(first, mine), [units, units, features], [near_units, near_units, near * HD]
+    )
+    out_full, gate_full, up_full = plane_gather(out_moved), plane_gather(gate_moved), plane_gather(up_moved)
+    second = turn(second)
+    f_parts = row_send(branch_f)
     chips = b_n * x_n
     kv = exchange(jnp.broadcast_to(mine[None], (chips,) + mine.shape))
     queries = rotate(dot(after(normed_a, mine), q_full), cosine, sine_table)
     queries = side_by_side(queries.astype(bf16) * bf16(HD**-0.5), None)
-    kv, up_moved, down_moved, queries, query_info, key_info, branch_f = fence(
-        kv, up_moved, down_moved, queries, query_info, key_info, branch_f
-    )
-    up_full = plane_gather(columns(up_moved))
-    down_full = plane_gather(columns(down_moved))
-    f_parts = row_send(branch_f)
-    kv = jnp.concatenate([kv, swap_core(kv)], axis=0).reshape(plane, rows_n, own, -1)
+    kv, second, queries, f_parts = fence(kv, second, queries, f_parts)
+    (down_moved,) = unbundle(second, [units], [near_units])
+    kv = [t.reshape(chips, rows_n, own, -1) for t in (kv, swap_core(kv))]
     saved = attend(row, query_info, key_info, queries, kv)
     attended = saved.reshape(group, heads, 2, HD)[:, :, 1].reshape(group, -1).astype(bf16)
     mid_part = dot(attended, out_full, ((1,), (1,)))
     parts = row_split(mid_part)
-    parts, f_parts = fence(parts, f_parts)
+    down_near = exchange(jnp.broadcast_to(down_moved[None], (chips,) + down_moved.shape))
+    parts, down_near = fence(parts, down_near)
+    down_near = down_near.reshape(-1, units)
+    down_full = rows_of([down_near, swap_core(down_near)])
     mid = x_own.astype(f32) + depth_scale * row_sum(parts)
     inv_f = inverse_rms(mid)
     unit_f = mid * inv_f
@@ -458,7 +502,7 @@
     hidden = (silu * up).astype(bf16)
     gf_twin = with_twin(grad_branch_f)
     nf_twin = with_twin(normed_f)
-    grad_hidden = dot(grad_branch_f, down_full)
+    grad_hidden = dot(columns(core_halves(grad_branch_f)), down_full)
     grad_gate = (grad_hidden * up * sig * (1.0 + gate * (1.0 - sig))).astype(bf16)
     grad_up = (grad_hidden * silu).astype(bf16)
     normed_part = dot(grad_gate, gate_full, ((1,), (1,))) + dot(grad_up, up_full, ((1,), (1,)))
@@ -480,55 +524,65 @@
     parts = row_send(branch_a)
     gate_sum = exchange(gate_pair)
     down_sum = chip_sum(down_sum)
-    parts, gate_sum, down_sum, up_pair = fence(parts, gate_sum, down_sum, up_pair)
+    output_part = dot(after(hidden, branch_a), down_full, ((1,), (1,)))
+    na_twin = with_twin(after(normed_a, branch_a))
+    attended = after(attended, branch_a)
+    parts, gate_sum, down_sum, up_pair, output_part, na_twin, attended = fence(
+        parts, gate_sum, down_sum, up_pair, output_part, na_twin, attended
+    )
+    two_back = bundle([down_sum, chip_sum(gate_sum)], [near_units, near_units])
     grad_branch_a = rows_of(parts)
     up_sum = exchange(up_pair)
-    down_back = turn(halves(down_sum, near_units), True)
-    gate_back = turn(halves(chip_sum(gate_sum), near_units), True)
+    output_parts = row_split(output_part)
     grad_attended = dot(grad_branch_a, out_full).astype(bf16)
-    grad_q, grad_kv = attend_back(
+    grad_q, *grad_kv = attend_back(
         row, query_info, key_info, queries, kv, saved, side_by_side(None, grad_attended)
     )
-    grad_q, grad_kv, up_sum, down_back, gate_back, hidden = fence(
-        grad_q, grad_kv, up_sum, down_back, gate_back, hidden
-    )
-
-    output_part = dot(hidden, down_full, ((1,), (1,)))
-    grad_kv = grad_kv.reshape(2, chips, group, -1)
+    grad_q, grad_kv, up_sum, output_parts = fence(grad_q, grad_kv, up_sum, output_parts)
+
     grad_kv = (grad_kv[0].astype(f32) + swap_core(grad_kv[1]).astype(f32)).astype(bf16)
-    grad_kv, output_part = fence(grad_kv, output_part)
+    grad_kv = grad_kv.reshape(chips, group, -1)
+    grad_kv, grad_q, up_sum, two_back, grad_branch_a = fence(
+        grad_kv, grad_q, up_sum, two_back, grad_branch_a
+    )
     grad_kv = exchange(grad_kv)
-    output_parts = row_split(output_part)
+    two_back = turn(two_back, True)
+    up_back = bundle([chip_sum(up_sum)], [near_units])
     grad_q = grad_q.reshape(group, heads, 2, HD)[:, :, 0].reshape(group, -1) * HD**-0.5
     grad_q = rotate(grad_q, cosine, -sine_table).astype(bf16)
-    q_pair = pair_sum(with_twin(normed_a), grad_q)
+    q_pair = pair_sum(na_twin, grad_q)
     out_pair = pair_sum(with_twin(grad_branch_a), attended)
-    up_sum = chip_sum(up_sum)
-    grad_kv, q_pair, out_pair, up_sum = fence(grad_kv, q_pair, out_pair, up_sum)
+    two_pair = jnp.concatenate([q_pair, out_pair], axis=2)
+    grad_kv, two_pair = fence(grad_kv, two_pair)
+    two_sum = exchange(two_pair)
     grad_kv = jnp.sum(grad_kv.astype(f32), axis=0).reshape(group, heads, 2, HD)
     grad_k = rotate(grad_kv[:, :, 0].reshape(group, -1), cosine, -sine_table).astype(bf16)
     grad_kv = side_by_side(grad_k, grad_kv[:, :, 1].reshape(group, -1).astype(bf16))
     normed_part = dot(grad_q, q_full, ((1,), (1,))) + dot(grad_kv, kv_full, ((1,), (1,)))
-    grad_kv, normed_part, output_parts = fence(grad_kv, normed_part, output_parts)
-    two_sum = exchange(jnp.concatenate([q_pair, out_pair], axis=2))
+    grad_kv, normed_part, two_back, up_back = fence(grad_kv, normed_part, two_back, up_back)
     parts = row_split(normed_part)
-    kv_pair = pair_sum(with_twin(normed_a), grad_kv)
-    up_back = turn(halves(up_sum, near_units), True)
-    kv_pair, two_sum, parts = fence(kv_pair, two_sum, parts)
+    kv_pair = pair_sum(na_twin, grad_kv)
+    kv_pair, two_sum = fence(kv_pair, two_sum)
     kv_sum = exchange(kv_pair)
     two_sum = chip_sum(two_sum)
-    q_back = turn(halves(two_sum[:, :features], near * HD), True)
-    out_back = turn(halves(two_sum[:, features:], near * HD), True)
+    parts, two_sum, up_back = fence(parts, two_sum, up_back)
+    up_back = turn(up_back, True)
     grad_normed_a = row_sum(parts)
-    kv_back = turn(halves(chip_sum(kv_sum), near * 2 * HD), True)
-    output = mid + depth_scale * row_sum(output_parts)
-
-    grad_gate_up = jnp.stack([columns(gate_back), columns(up_back)]).astype(f32)
-    grad_down = columns(down_back).astype(f32).T
-    grad_out = columns(out_back).astype(f32).T
-    grad_w_kv = columns(kv_back).reshape(piece, heads, 2, HD)
+    output = mid + depth_scale * columns(core_halves(row_sum(output_parts)))
+    kv_sum, up_back = fence(kv_sum, up_back)
+    last_cuts = [near * 2 * HD, near * HD, near * HD]
+    last_back = bundle([chip_sum(kv_sum), two_sum[:, :features], two_sum[:, features:]], last_cuts)
+    last_back = turn(last_back, True)
+
+    grad_w_down, grad_w_gate = unbundle(two_back, [units, units], [near_units, near_units])
+    (grad_w_up,) = unbundle(up_back, [units], [near_units])
+    grad_w_kv, grad_w_q, grad_w_out = unbundle(last_back, [2 * features, features, features], last_cuts)
+    grad_gate_up = jnp.stack([grad_w_gate, grad_w_up]).astype(f32)
+    grad_down = grad_w_down.astype(f32).T
+    grad_out = grad_w_out.astype(f32).T
+    grad_w_kv = grad_w_kv.reshape(piece, heads, 2, HD)
     grad_qkv = jnp.stack(
-        [columns(q_back)] + [grad_w_kv[:, :, n].reshape(piece, features) for n in range(2)]
+        [grad_w_q] + [grad_w_kv[:, :, n].reshape(piece, features) for n in range(2)]
     ).astype(f32)
     rows_own = x_own.astype(f32)
     inv_a = inverse_rms(rows_own)

time: 832 us -> 781 us (0.939)
  matrix products: 103 us -> 58.8 us
  starting transfers between devices: 207 us -> 165 us
  Pallas kernels: 39.3 us -> 69.8 us
  local copies, waits for them, and re-layouts: 85.6 us -> 94.5 us
    dot_general x18 -> x12, matrix products: 103 us -> 58.8 us  [dot(): return lax.dot_general(a, b, (dims, ((), ())), preferred_element_type=f32)]
    ppermute x24, starting transfers between devices: 66 us -> 33.7 us  [send_row(): lax.ppermute(array, ROW, [(i, i ^ distance) for i in range(lax.axis_size(...]
    pallas_call x0 -> x6, Pallas kernels: none -> 30.5 us  [pair_sum(): pl.pallas_call(pair_kernel, grid=(rows // tile,), in_specs=[lefts, lefts,...]
    ppermute x24 -> x14, starting transfers between devices: 82.3 us -> 52.5 us  [move(): return lax.ppermute(part, (ROW, 'tx', 'tc'), pairs)]
    all_to_all x7 -> x8, waiting for transfers between devices: 40.9 us -> 69.9 us  [exchange(): return lax.all_to_all(blocks, CHIPS, 0, 0, tiled=True)]
    convert_element_type x5 -> x1, local copies, waits for them, and re-layouts: 20.9 us -> 1.23 us  [on_device(): grad_q = rotate(grad_q, cosine, -sine_table).astype(bf16)]
    all_gather x6 -> x5, waiting for transfers between devices: 16.1 us -> 0.03 us  [plane_gather(): return lax.all_gather(piece, PLANE, axis=0, tiled=True)]
    ppermute x24, waiting for transfers between devices: 87 us -> 72.2 us  [send_row(): lax.ppermute(array, ROW, [(i, i ^ distance) for i in range(lax.axis_size(...]
  transfers between devices with their start and end apart: 79 -> 70, of which waited for: 29 -> 26; matrix products, arithmetic and copies ran while one was open for 28% -> 27% of each run, Pallas kernels for 5% -> 9%
where the time goes in v3:
time: 781 us; the launch traced here: 769 us
  waiting for transfers between devices  286 us (37%)
  starting transfers between devices  165 us (21%)
  local copies, waits for them, and re-layouts  94.5 us (12%)
  other arithmetic  79 us (10%)
  Pallas kernels  69.8 us (9%)
  matrix products  58.8 us (8%)
  between operations  16.1 us (2%)
    ppermute x14, waiting for transfers between devices, move(): return lax.ppermute(part, (ROW, 'tx', 'tc'), pairs)  125 us
    ppermute x24, waiting for transfers between devices, send_row(): lax.ppermute(array, ROW, [(i, i ^ distance) for i in range(lax.axis_size(...  72.2 us
    all_to_all x8, waiting for transfers between devices, exchange(): return lax.all_to_all(blocks, CHIPS, 0, 0, tiled=True)  69.9 us
    dot_general x12, matrix products, dot(): return lax.dot_general(a, b, (dims, ((), ())), preferred_element_type=f32)  58.8 us
    ppermute x14, starting transfers between devices, move(): return lax.ppermute(part, (ROW, 'tx', 'tc'), pairs)  52.5 us
    all_to_all x8, starting transfers between devices, exchange(): return lax.all_to_all(blocks, CHIPS, 0, 0, tiled=True)  36.8 us
    ppermute x24, starting transfers between devices, send_row(): lax.ppermute(array, ROW, [(i, i ^ distance) for i in range(lax.axis_size(...  33.7 us
    pallas_call x6, Pallas kernels, pair_sum(): pl.pallas_call(pair_kernel, grid=(rows // tile,), in_specs=[lefts, lefts,...  30.5 us
  transfers between devices with their start and end apart: 70, of which 26 were waited for; matrix products, arithmetic and copies ran while one was open for 27% of the time, Pallas kernels for 9%

profile of v3, /device:TPU:1, one launch (start us, length us, event | category | flops | bytes accessed | tf_op | source)
XLA Modules:
  0.0 768.6 jit_solution(15580534214084870511)
XLA Ops:
  9.2 4.6 collective-permute-start.4
  16.6 18.5 %collective-permute-done.5 = bf16[288,512]{0,1:T(8,128)(2,1)S(1)} collective-permute-done((bf16[288,512]{0,1:T(8,128)(2,1)S(1)}, bf16[288,512]{0,1:T(8,128)(2,1)S(1)}, u32[]{:S(2)}, u32[]{:S(2)}) %collective-permute-start.5) | collective-permute-done | bytes 294944 | tf_op jit(solution)/shard_map/ppermute | solution.py:85
  44.5 5.9 collective-permute-start.8
  58.3 27.2 %collective-permute-done.9 = bf16[288,256]{1,0:T(8,128)(2,1)} collective-permute-done((bf16[288,256]{1,0:T(8,128)(2,1)}, bf16[288,256]{1,0:T(8,128)(2,1)}, u32[]{:S(2)}, u32[]{:S(2)}) %collective-permute-start.9) | collective-permute-done | bytes 147488 | tf_op jit(solution)/shard_map/ppermute | solution.py:85
  104.1 6.0 fusion.52
  110.5 33.9 %collective-permute-done.15 = bf16[288,1600]{1,0:T(8,128)(2,1)} collective-permute-done((bf16[288,1600]{1,0:T(8,128)(2,1)}, bf16[288,1600]{1,0:T(8,128)(2,1)}, u32[]{:S(2)}, u32[]{:S(2)}) %collective-permute-start.15) | collective-permute-done | bytes 921632 | tf_op jit(solution)/shard_map/ppermute | solution.py:85
  154.4 4.8 all-to-all-start
  164.8 4.9 collective-permute-start.7
  173.5 6.9 collective-permute-done.10
  180.4 15.7 %collective-permute-done.11 = bf16[80,2304]{1,0:T(8,128)(2,1)} collective-permute-done((bf16[80,2304]{1,0:T(8,128)(2,1)S(1)}, bf16[80,2304]{1,0:T(8,128)(2,1)}, u32[]{:S(2)}, u32[]{:S(2)}) %collective-permute-start.11) | collective-permute-done | bytes 368672 | tf_op jit(solution)/shard_map/ppermute | solution.py:29
  196.1 16.3 %collective-permute-done.7 = bf16[288,672]{1,0:T(8,128)(2,1)} collective-permute-done((bf16[288,672]{1,0:T(8,128)(2,1)}, bf16[288,672]{1,0:T(8,128)(2,1)}, u32[]{:S(2)}, u32[]{:S(2)}) %collective-permute-start.7) | collective-permute-done | bytes 387104 | tf_op jit(solution)/shard_map/ppermute | solution.py:85
  222.9 16.3 %shard_map.153.out_ref = f32[320,1152]{1,0:T(8,128)} custom-call(s32[1]{0:T(128)} %bitcast.row_ref, s32[320,4]{1,0:T(8,128)} %copy.145.query_ref, s32[4,2,640]{2,1,0:T(2,128)} %pad_add_fusion.key_ref, bf16[320,1152]{1,0:T(8,128)(2,1)} %copy.146.q_ref, bf16[4,4,80,1152]{3,2,1,0:T(8,128)(2,1)} %bitcast.25.near_ref, bf16[4,4,80,1152]{3,2,1,0:T(8,128)(2,1)} %bitcast.26.far_ref), custom_call_target="tpu_custom_call" | custom-call | flops 47185920000 | bytes 11796480 | tf_op jit(solution)/shard_map/pallas_call | solution.py:353
  256.6 16.8 %all-to-all-done.1 = bf16[4,288,1440]{2,1,0:T(8,128)(2,1)S(1)} async-done(((bf16[4,288,1440]{2,1,0:T(8,128)(2,1)}), bf16[4,288,1440]{2,1,0:T(8,128)(2,1)S(1)}, u32[]{:S(2)}, u32[]{:S(2)}) %all-to-all-start.1) | async-done | bytes 3317792 | tf_op jit(solution)/shard_map/all_to_all | solution.py:146
  291.2 7.3 collective-permute-start.21
  302.4 24.1 %collective-permute-done.21 = bf16[80,2304]{1,0:T(8,128)(2,1)S(1)} collective-permute-done((bf16[80,2304]{1,0:T(8,128)(2,1)S(1)}, bf16[80,2304]{1,0:T(8,128)(2,1)S(1)}, u32[]{:S(2)}, u32[]{:S(2)}) %collective-permute-start.21) | collective-permute-done | bytes 368672 | tf_op jit(solution)/shard_map/ppermute | solution.py:29
  328.0 6.1 copy.149
  334.1 7.1 fusion.1
  341.3 6.7 fusion.35
  348.0 7.7 %multiply_convert_fusion = (bf16[320,1440]{1,0:T(8,128)(2,1)S(1)}, bf16[320,1440]{1,0:T(8,128)(2,1)S(1)}, bf16[320,1440]{1,0:T(8,128)(2,1)S(1)}) fusion(f32[320,1440]{1,0:T(8,128)} %fusion.35, f32[320,1440]{1,0:T(8,128)} %fusion.1, bf16[2304,1440]{1,0:T(8,128)(2,1)} %all-gather.12.cloned.1.call-done, bf16[80,2304]{1,0:T(8,128)(2,1)} %copy-done.55, ...), kind=kOutput, calls=%fused_computation.13 | convolution fusion | flops 2136176640 | bytes 14561280 | tf_op jit(solution)/shard_map/dot_general | solution.py:25
  358.5 7.2 convolution_add_fusion.1
  365.6 6.4 shard_map.154
  372.0 4.9 all-to-all-start.2
  383.2 6.3 shard_map.155
  389.5 6.3 shard_map.156
  395.9 10.5 %collective-permute-done.27 = bf16[80,2304]{1,0:T(8,128)(2,1)} collective-permute-done((bf16[80,2304]{1,0:T(8,128)(2,1)S(1)}, bf16[80,2304]{1,0:T(8,128)(2,1)}, u32[]{:S(2)}, u32[]{:S(2)}) %collective-permute-start.27) | collective-permute-done | bytes 368672 | tf_op jit(solution)/shard_map/ppermute | solution.py:29
  406.4 11.1 %all-to-all-done.2 = bf16[4,288,1440]{2,1,0:T(8,128)(2,1)} async-done(((bf16[4,288,1440]{2,1,0:T(8,128)(2,1)}), bf16[4,288,1440]{2,1,0:T(8,128)(2,1)}, u32[]{:S(2)}, u32[]{:S(2)}) %all-to-all-start.2) | async-done | bytes 3317792 | tf_op jit(solution)/shard_map/all_to_all | solution.py:146
  417.5 4.9 all-to-all-start.3
  430.9 6.1 fusion
  437.0 3.8 reduce_sum.158
  440.8 8.9 %collective-permute-done.33 = bf16[80,2304]{1,0:T(8,128)(2,1)} collective-permute-done((bf16[80,2304]{1,0:T(8,128)(2,1)S(1)}, bf16[80,2304]{1,0:T(8,128)(2,1)}, u32[]{:S(2)}, u32[]{:S(2)}) %collective-permute-start.33) | collective-permute-done | bytes 368672 | tf_op jit(solution)/shard_map/ppermute | solution.py:29
  449.7 12.6 %all-to-all-done.3 = bf16[4,288,1440]{2,1,0:T(8,128)(2,1)} async-done(((bf16[4,288,1440]{2,1,0:T(8,128)(2,1)}), bf16[4,288,1440]{2,1,0:T(8,128)(2,1)}, u32[]{:S(2)}, u32[]{:S(2)}) %all-to-all-start.3) | async-done | bytes 3317792 | tf_op jit(solution)/shard_map/all_to_all | solution.py:146
  470.4 4.9 all-to-all-start.4
  481.0 23.1 %shard_map.157 = (f32[320,1152]{1,0:T(8,128)}, bf16[4,4,80,1152]{3,2,1,0:T(8,128)(2,1)}, bf16[4,4,80,1152]{3,2,1,0:T(8,128)(2,1)}) custom-call(s32[1]{0:T(128)} %bitcast.row_ref, s32[320,4]{1,0:T(8,128)} %copy.145.query_ref, s32[4,2,640]{2,1,0:T(2,128)} %pad_add_fusion.key_ref, bf16[320,1152]{1,0:T(8,128)(2,1)} %copy.146.q_ref, ...), custom_call_target="tpu_custom_call" | custom-call | flops 117964800000 | bytes 11796480 | tf_op jit(solution)/shard_map/pallas_call | solution.py:367
  504.2 11.2 %all-to-all-done.4 = bf16[4,288,1440]{2,1,0:T(8,128)(2,1)} async-done(((bf16[4,288,1440]{2,1,0:T(8,128)(2,1)}), bf16[4,288,1440]{2,1,0:T(8,128)(2,1)}, u32[]{:S(2)}, u32[]{:S(2)}) %all-to-all-start.4) | async-done | bytes 3317792 | tf_op jit(solution)/shard_map/all_to_all | solution.py:146
  531.2 4.2 add_convert_fusion
  535.5 4.8 all-to-all-start.5
  572.7 18.2 %all-to-all-done.5 = bf16[4,320,1152]{2,1,0:T(8,128)(2,1)} async-done(((bf16[4,320,1152]{2,1,0:T(8,128)(2,1)}), bf16[4,320,1152]{2,1,0:T(8,128)(2,1)}, u32[]{:S(2)}, u32[]{:S(2)}) %all-to-all-start.5) | async-done | bytes 2949152 | tf_op jit(solution)/shard_map/all_to_all | solution.py:146
  598.3 5.0 all-to-all-start.6
  603.5 5.2 fusion.55
  618.3 15.8 %collective-permute-start.47 = (bf16[320,1152]{1,0:T(8,128)(2,1)S(1)}, bf16[320,1152]{1,0:T(8,128)(2,1)S(1)}, u32[]{:S(2)}, u32[]{:S(2)}) collective-permute-start(bf16[320,1152]{1,0:T(8,128)(2,1)S(1)} %copy.163.right_ref), channel_id=1, source_target_pairs={{0,1},{1,0},{2,3},{3,2},{4,5},{5,4},{6,7},{7,6},{8,9},{9,8},{10,11... | collective-permute-start | bytes 2211848 | tf_op jit(solution)/shard_map/ppermute | solution.py:33
  638.9 4.6 shard_map.160
  650.7 6.7 collective-permute-start.53
  657.4 3.8 all-to-all-start.7
  661.2 9.2 %collective-permute-start.48 = (bf16[288,768]{1,0:T(8,128)(2,1)}, bf16[288,768]{1,0:T(8,128)(2,1)}, u32[]{:S(2)}, u32[]{:S(2)}) collective-permute-start(bf16[288,768]{1,0:T(8,128)(2,1)} %slice.486), channel_id=1, source_target_pairs={{0,0},{8,1},{16,2},{24,3},{2,8},{10,9},{18,10},{26,11},{1,16},{9,1... | collective-permute-start | bytes 1327112 | tf_op jit(solution)/shard_map/ppermute | solution.py:85
  676.4 15.6 %collective-permute-done.54 = f32[2,2304]{1,0:T(2,128)S(1)} collective-permute-done((f32[2,2304]{1,0:T(2,128)S(1)}, f32[2,2304]{1,0:T(2,128)S(1)}, u32[]{:S(2)}, u32[]{:S(2)}) %collective-permute-start.54) | collective-permute-done | bytes 18464 | tf_op jit(solution)/shard_map/ppermute | solution.py:595
  695.0 6.7 collective-permute-start.56
  707.3 14.2 %collective-permute-start.51 = (bf16[288,1024]{1,0:T(8,128)(2,1)}, bf16[288,1024]{1,0:T(8,128)(2,1)}, u32[]{:S(2)}, u32[]{:S(2)}) collective-permute-start(bf16[288,1024]{1,0:T(8,128)(2,1)} %pad_maximum_fusion.17), channel_id=1, source_target_pairs={{16,0},{24,1},{0,2},{8,3},{18,8},{26,9},{2,10},{10,11},{17,16},{25... | collective-permute-start | bytes 1769480 | tf_op jit(solution)/shard_map/ppermute | solution.py:85
  731.7 24.8 %collective-permute-done.50 = bf16[288,1280]{1,0:T(8,128)(2,1)S(1)} collective-permute-done((bf16[288,1280]{1,0:T(8,128)(2,1)S(1)}, bf16[288,1280]{1,0:T(8,128)(2,1)S(1)}, u32[]{:S(2)}, u32[]{:S(2)}) %collective-permute-start.50) | collective-permute-done | bytes 737312 | tf_op jit(solution)/shard_map/ppermute | solution.py:85
  (492 shorter events, 249.0 us)
Async XLA Ops:
  7.2 97.0 %all-gather.6.cloned.1.call-start = ((), (), s32[]{:S(2)}) async-start(), calls=%async_computation.8 | async-start | bytes 5971968 | tf_op jit(solution)/shard_map/all_gather | solution.py:103
  9.2 27.2 %collective-permute-start.4 = (bf16[288,640]{0,1:T(8,128)(2,1)S(1)}, bf16[288,640]{0,1:T(8,128)(2,1)S(1)}, u32[]{:S(2)}, u32[]{:S(2)}) collective-permute-start(bf16[288,640]{0,1:T(8,128)(2,1)S(1)} %slice.446), channel_id=1, source_target_pairs={{0,0},{1,8},{2,16},{3,24},{8,2},{9,10},{10,18},{11,26},{16,1},{17,... | collective-permute-start | bytes 1105928 | tf_op jit(solution)/shard_map/ppermute | solution.py:85
  37.7 132.0 %all-gather.8.cloned.1.call-start = ((), (), s32[]{:S(2)}) async-start(), calls=%async_computation.9 | async-start | bytes 3317760 | tf_op jit(solution)/shard_map/all_gather | solution.py:103
  39.3 48.5 %collective-permute-start = (bf16[81,2304]{1,0:T(8,128)(2,1)}, bf16[81,2304]{1,0:T(8,128)(2,1)}, u32[]{:S(2)}, u32[]{:S(2)}) collective-permute-start(bf16[81,2304]{1,0:T(8,128)(2,1)} %constant_dynamic-update-slice_fusion), channel_id=1, source_target_pairs={{0,8},{8,0},{16,24},{24,16},{1,9},{9,1},{17,25},{25,17},{2,10},{10... | collective-permute-start | bytes 1119752 | tf_op jit(solution)/shard_map/ppermute | solution.py:29
  39.3 48.5 %collective-permute-start.1 = (bf16[81,2304]{1,0:T(8,128)(2,1)}, bf16[81,2304]{1,0:T(8,128)(2,1)}, u32[]{:S(2)}, u32[]{:S(2)}) collective-permute-start(bf16[81,2304]{1,0:T(8,128)(2,1)} %constant_dynamic-update-slice_fusion), channel_id=1, source_target_pairs={{0,16},{8,24},{16,0},{24,8},{1,17},{9,25},{17,1},{25,9},{2,18},{10... | collective-permute-start | bytes 1119752 | tf_op jit(solution)/shard_map/ppermute | solution.py:29
  39.4 48.5 %collective-permute-start.2 = (bf16[81,2304]{1,0:T(8,128)(2,1)}, bf16[81,2304]{1,0:T(8,128)(2,1)}, u32[]{:S(2)}, u32[]{:S(2)}) collective-permute-start(bf16[81,2304]{1,0:T(8,128)(2,1)} %constant_dynamic-update-slice_fusion), channel_id=1, source_target_pairs={{0,24},{8,16},{16,8},{24,0},{1,25},{9,17},{17,9},{25,1},{2,26},{10... | collective-permute-start | bytes 1119752 | tf_op jit(solution)/shard_map/ppermute | solution.py:29
  43.7 41.9 %collective-permute-start.9 = (bf16[288,256]{1,0:T(8,128)(2,1)}, bf16[288,256]{1,0:T(8,128)(2,1)}, u32[]{:S(2)}, u32[]{:S(2)}) collective-permute-start(bf16[288,256]{1,0:T(8,128)(2,1)} %slice.456), channel_id=1, source_target_pairs={{0,16},{1,24},{2,0},{3,8},{8,18},{9,26},{10,2},{11,10},{16,17},{17... | collective-permute-start | bytes 442376 | tf_op jit(solution)/shard_map/ppermute | solution.py:85
  44.5 41.3 %collective-permute-start.8 = (bf16[288,320]{1,0:T(8,128)(2,1)}, bf16[288,320]{1,0:T(8,128)(2,1)}, u32[]{:S(2)}, u32[]{:S(2)}) collective-permute-start(bf16[288,320]{1,0:T(8,128)(2,1)} %slice.455), channel_id=1, source_target_pairs={{0,0},{1,8},{2,16},{3,24},{8,2},{9,10},{10,18},{11,26},{16,1},{17,... | collective-permute-start | bytes 552968 | tf_op jit(solution)/shard_map/ppermute | solution.py:85
  87.8 157.8 %all-gather.10.cloned.1.call-start = ((), (), s32[]{:S(2)}) async-start(), calls=%async_computation.10 | async-start | bytes 3317760 | tf_op jit(solution)/shard_map/all_gather | solution.py:103
  96.9 47.6 %collective-permute-start.14 = (bf16[288,1856]{1,0:T(8,128)(2,1)}, bf16[288,1856]{1,0:T(8,128)(2,1)}, u32[]{:S(2)}, u32[]{:S(2)}) collective-permute-start(bf16[288,1856]{1,0:T(8,128)(2,1)} %pad_maximum_fusion.6), channel_id=1, source_target_pairs={{0,0},{1,8},{2,16},{3,24},{8,2},{9,10},{10,18},{11,26},{16,1},{17,... | collective-permute-start | bytes 3207176 | tf_op jit(solution)/shard_map/ppermute | solution.py:85
  98.8 45.6 %collective-permute-start.15 = (bf16[288,1600]{1,0:T(8,128)(2,1)}, bf16[288,1600]{1,0:T(8,128)(2,1)}, u32[]{:S(2)}, u32[]{:S(2)}) collective-permute-start(bf16[288,1600]{1,0:T(8,128)(2,1)} %concatenate.119), channel_id=1, source_target_pairs={{0,16},{1,24},{2,0},{3,8},{8,18},{9,26},{10,2},{11,10},{16,17},{17... | collective-permute-start | bytes 2764808 | tf_op jit(solution)/shard_map/ppermute | solution.py:85
  147.4 193.9 %all-gather.14.cloned.1.call-start = ((), (), s32[]{:S(2)}) async-start(), calls=%async_computation.12 | async-start | bytes 7962624 | tf_op jit(solution)/shard_map/all_gather | solution.py:103
  154.4 58.0 %all-to-all-start = ((bf16[4,320,1152]{2,1,0:T(8,128)(2,1)}), bf16[4,320,1152]{2,1,0:T(8,128)(2,1)}, u32[]{:S(2)}, u32[]{:S(2)}) async-start(bf16[4,320,1152]{2,1,0:T(8,128)(2,1)} %broadcast_in_dim.30), calls=%async_computation | async-start | bytes 5898240 | tf_op jit(solution)/shard_map/all_to_all | solution.py:146
  159.2 188.8 %all-gather.12.cloned.1.call-start = ((), (), s32[]{:S(2)}) async-start(), calls=%async_computation.11 | async-start | bytes 7962624 | tf_op jit(solution)/shard_map/all_gather | solution.py:103
  159.3 36.8 %collective-permute-start.11 = (bf16[80,2304]{1,0:T(8,128)(2,1)S(1)}, bf16[80,2304]{1,0:T(8,128)(2,1)}, u32[]{:S(2)}, u32[]{:S(2)}) collective-permute-start(bf16[80,2304]{1,0:T(8,128)(2,1)S(1)} %copy-done.32), channel_id=1, source_target_pairs={{0,16},{8,24},{16,0},{24,8},{1,17},{9,25},{17,1},{25,9},{2,18},{10... | collective-permute-start | bytes 1105928 | tf_op jit(solution)/shard_map/ppermute | solution.py:29
  159.4 36.7 %collective-permute-start.12 = (bf16[80,2304]{1,0:T(8,128)(2,1)S(1)}, bf16[80,2304]{1,0:T(8,128)(2,1)}, u32[]{:S(2)}, u32[]{:S(2)}) collective-permute-start(bf16[80,2304]{1,0:T(8,128)(2,1)S(1)} %copy-done.32), channel_id=1, source_target_pairs={{0,24},{8,16},{16,8},{24,0},{1,25},{9,17},{17,9},{25,1},{2,26},{10... | collective-permute-start | bytes 1105928 | tf_op jit(solution)/shard_map/ppermute | solution.py:29
  162.9 49.6 %collective-permute-start.6 = (bf16[288,768]{1,0:T(8,128)(2,1)}, bf16[288,768]{1,0:T(8,128)(2,1)}, u32[]{:S(2)}, u32[]{:S(2)}) collective-permute-start(bf16[288,768]{1,0:T(8,128)(2,1)} %slice.443), channel_id=1, source_target_pairs={{0,0},{1,8},{2,16},{3,24},{8,2},{9,10},{10,18},{11,26},{16,1},{17,... | collective-permute-start | bytes 1327112 | tf_op jit(solution)/shard_map/ppermute | solution.py:85
  164.8 47.6 %collective-permute-start.7 = (bf16[288,672]{1,0:T(8,128)(2,1)}, bf16[288,672]{1,0:T(8,128)(2,1)}, u32[]{:S(2)}, u32[]{:S(2)}) collective-permute-start(bf16[288,672]{1,0:T(8,128)(2,1)} %slice.444), channel_id=1, source_target_pairs={{0,16},{1,24},{2,0},{3,8},{8,18},{9,26},{10,2},{11,10},{16,17},{17... | collective-permute-start | bytes 1161224 | tf_op jit(solution)/shard_map/ppermute | solution.py:85
  219.2 54.2 %all-to-all-start.1 = ((bf16[4,288,1440]{2,1,0:T(8,128)(2,1)}), bf16[4,288,1440]{2,1,0:T(8,128)(2,1)S(1)}, u32[]{:S(2)}, u32[]{:S(2)}) async-start(bf16[4,288,1440]{2,1,0:T(8,128)(2,1)} %broadcast_in_dim.31), calls=%async_computation.1 | async-start | bytes 7077888 | tf_op jit(solution)/shard_map/all_to_all | solution.py:146
  250.0 23.4 %collective-permute-start.16 = (bf16[80,2304]{1,0:T(8,128)(2,1)}, bf16[80,2304]{1,0:T(8,128)(2,1)}, u32[]{:S(2)}, u32[]{:S(2)}) collective-permute-start(bf16[80,2304]{1,0:T(8,128)(2,1)} %get-tuple-element.257), channel_id=1, source_target_pairs={{0,8},{8,0},{16,24},{24,16},{1,9},{9,1},{17,25},{25,17},{2,10},{10... | collective-permute-start | bytes 1105928 | tf_op jit(solution)/shard_map/ppermute | solution.py:29
  252.7 24.5 %collective-permute-start.18 = (bf16[80,2304]{1,0:T(8,128)(2,1)}, bf16[80,2304]{1,0:T(8,128)(2,1)}, u32[]{:S(2)}, u32[]{:S(2)}) collective-permute-start(bf16[80,2304]{1,0:T(8,128)(2,1)} %get-tuple-element.255), channel_id=1, source_target_pairs={{0,24},{8,16},{16,8},{24,0},{1,25},{9,17},{17,9},{25,1},{2,26},{10... | collective-permute-start | bytes 1105928 | tf_op jit(solution)/shard_map/ppermute | solution.py:29
  280.8 47.2 %collective-permute-start.19 = (bf16[1152,1440]{0,1:T(8,128)(2,1)}, bf16[1152,1440]{0,1:T(8,128)(2,1)}, u32[]{:S(2)}, u32[]{:S(2)}) collective-permute-start(bf16[1152,1440]{0,1:T(8,128)(2,1)} %copy.148), channel_id=1, source_target_pairs={{0,1},{1,0},{2,3},{3,2},{4,5},{5,4},{6,7},{7,6},{8,9},{9,8},{10,11... | collective-permute-start | bytes 9953288 | tf_op jit(solution)/shard_map/ppermute | solution.py:33
  291.2 35.3 %collective-permute-start.21 = (bf16[80,2304]{1,0:T(8,128)(2,1)S(1)}, bf16[80,2304]{1,0:T(8,128)(2,1)S(1)}, u32[]{:S(2)}, u32[]{:S(2)}) collective-permute-start(bf16[80,2304]{1,0:T(8,128)(2,1)S(1)} %multiply_convert_fusion.4), channel_id=1, source_target_pairs={{0,16},{8,24},{16,0},{24,8},{1,17},{9,25},{17,1},{25,9},{2,18},{10... | collective-permute-start | bytes 1105928 | tf_op jit(solution)/shard_map/ppermute | solution.py:29
  298.5 28.0 %collective-permute-start.20 = (bf16[80,2304]{1,0:T(8,128)(2,1)S(1)}, bf16[80,2304]{1,0:T(8,128)(2,1)S(1)}, u32[]{:S(2)}, u32[]{:S(2)}) collective-permute-start(bf16[80,2304]{1,0:T(8,128)(2,1)S(1)} %multiply_convert_fusion.4), channel_id=1, source_target_pairs={{0,8},{8,0},{16,24},{24,16},{1,9},{9,1},{17,25},{25,17},{2,10},{10... | collective-permute-start | bytes 1105928 | tf_op jit(solution)/shard_map/ppermute | solution.py:29
  299.5 66.1 %collective-permute-start.23 = (bf16[320,1152]{1,0:T(8,128)(2,1)}, bf16[320,1152]{1,0:T(8,128)(2,1)}, u32[]{:S(2)}, u32[]{:S(2)}) collective-permute-start(bf16[320,1152]{1,0:T(8,128)(2,1)} %get-tuple-element.254), channel_id=1, source_target_pairs={{0,1},{1,0},{2,3},{3,2},{4,5},{5,4},{6,7},{7,6},{8,9},{9,8},{10,11... | collective-permute-start | bytes 2211848 | tf_op jit(solution)/shard_map/ppermute | solution.py:33
  327.6 44.4 %collective-permute-start.25 = (bf16[320,1152]{1,0:T(8,128)(2,1)}, bf16[320,1152]{1,0:T(8,128)(2,1)}, u32[]{:S(2)}, u32[]{:S(2)}) collective-permute-start(bf16[320,1152]{1,0:T(8,128)(2,1)} %get-tuple-element.251), channel_id=1, source_target_pairs={{0,1},{1,0},{2,3},{3,2},{4,5},{5,4},{6,7},{7,6},{8,9},{9,8},{10,11... | collective-permute-start | bytes 2211848 | tf_op jit(solution)/shard_map/ppermute | solution.py:33
  372.0 45.5 %all-to-all-start.2 = ((bf16[4,288,1440]{2,1,0:T(8,128)(2,1)}), bf16[4,288,1440]{2,1,0:T(8,128)(2,1)}, u32[]{:S(2)}, u32[]{:S(2)}) async-start(bf16[4,288,1440]{2,1,0:T(8,128)(2,1)} %bitcast.30), calls=%async_computation.2 | async-start | bytes 7077888 | tf_op jit(solution)/shard_map/all_to_all | solution.py:146
  379.6 26.7 %collective-permute-start.27 = (bf16[80,2304]{1,0:T(8,128)(2,1)S(1)}, bf16[80,2304]{1,0:T(8,128)(2,1)}, u32[]{:S(2)}, u32[]{:S(2)}) collective-permute-start(bf16[80,2304]{1,0:T(8,128)(2,1)S(1)} %get-tuple-element.249), channel_id=1, source_target_pairs={{0,16},{8,24},{16,0},{24,8},{1,17},{9,25},{17,1},{25,9},{2,18},{10... | collective-permute-start | bytes 1105928 | tf_op jit(solution)/shard_map/ppermute | solution.py:29
  380.7 25.7 %collective-permute-start.28 = (bf16[80,2304]{1,0:T(8,128)(2,1)S(1)}, bf16[80,2304]{1,0:T(8,128)(2,1)}, u32[]{:S(2)}, u32[]{:S(2)}) collective-permute-start(bf16[80,2304]{1,0:T(8,128)(2,1)S(1)} %get-tuple-element.248), channel_id=1, source_target_pairs={{0,24},{8,16},{16,8},{24,0},{1,25},{9,17},{17,9},{25,1},{2,26},{10... | collective-permute-start | bytes 1105928 | tf_op jit(solution)/shard_map/ppermute | solution.py:29
  417.5 44.8 %all-to-all-start.3 = ((bf16[4,288,1440]{2,1,0:T(8,128)(2,1)}), bf16[4,288,1440]{2,1,0:T(8,128)(2,1)}, u32[]{:S(2)}, u32[]{:S(2)}) async-start(bf16[4,288,1440]{2,1,0:T(8,128)(2,1)} %bitcast.31), calls=%async_computation.3 | async-start | bytes 7077888 | tf_op jit(solution)/shard_map/all_to_all | solution.py:146
  426.1 23.6 %collective-permute-start.33 = (bf16[80,2304]{1,0:T(8,128)(2,1)S(1)}, bf16[80,2304]{1,0:T(8,128)(2,1)}, u32[]{:S(2)}, u32[]{:S(2)}) collective-permute-start(bf16[80,2304]{1,0:T(8,128)(2,1)S(1)} %multiply_convert_fusion.3), channel_id=1, source_target_pairs={{0,24},{8,16},{16,8},{24,0},{1,25},{9,17},{17,9},{25,1},{2,26},{10... | collective-permute-start | bytes 1105928 | tf_op jit(solution)/shard_map/ppermute | solution.py:29
  470.4 45.0 %all-to-all-start.4 = ((bf16[4,288,1440]{2,1,0:T(8,128)(2,1)}), bf16[4,288,1440]{2,1,0:T(8,128)(2,1)}, u32[]{:S(2)}, u32[]{:S(2)}) async-start(bf16[4,288,1440]{2,1,0:T(8,128)(2,1)} %bitcast.32), calls=%async_computation.4 | async-start | bytes 7077888 | tf_op jit(solution)/shard_map/all_to_all | solution.py:146
  477.4 26.7 %collective-permute-start.35 = (bf16[80,2304]{1,0:T(8,128)(2,1)S(1)}, bf16[80,2304]{1,0:T(8,128)(2,1)S(1)}, u32[]{:S(2)}, u32[]{:S(2)}) collective-permute-start(bf16[80,2304]{1,0:T(8,128)(2,1)S(1)} %get-tuple-element.245), channel_id=1, source_target_pairs={{0,8},{8,0},{16,24},{24,16},{1,9},{9,1},{17,25},{25,17},{2,10},{10... | collective-permute-start | bytes 1105928 | tf_op jit(solution)/shard_map/ppermute | solution.py:29
  477.5 26.6 %collective-permute-start.36 = (bf16[80,2304]{1,0:T(8,128)(2,1)S(1)}, bf16[80,2304]{1,0:T(8,128)(2,1)S(1)}, u32[]{:S(2)}, u32[]{:S(2)}) collective-permute-start(bf16[80,2304]{1,0:T(8,128)(2,1)S(1)} %get-tuple-element.244), channel_id=1, source_target_pairs={{0,16},{8,24},{16,0},{24,8},{1,17},{9,25},{17,1},{25,9},{2,18},{10... | collective-permute-start | bytes 1105928 | tf_op jit(solution)/shard_map/ppermute | solution.py:29
  478.9 25.3 %collective-permute-start.37 = (bf16[80,2304]{1,0:T(8,128)(2,1)S(1)}, bf16[80,2304]{1,0:T(8,128)(2,1)S(1)}, u32[]{:S(2)}, u32[]{:S(2)}) collective-permute-start(bf16[80,2304]{1,0:T(8,128)(2,1)S(1)} %get-tuple-element.243), channel_id=1, source_target_pairs={{0,24},{8,16},{16,8},{24,0},{1,25},{9,17},{17,9},{25,1},{2,26},{10... | collective-permute-start | bytes 1105928 | tf_op jit(solution)/shard_map/ppermute | solution.py:29
  526.6 40.3 %collective-permute-start.41 = (bf16[320,576]{1,0:T(8,128)(2,1)S(1)}, bf16[320,576]{1,0:T(8,128)(2,1)S(1)}, u32[]{:S(2)}, u32[]{:S(2)}) collective-permute-start(bf16[320,576]{1,0:T(8,128)(2,1)S(1)} %copy.159.right_ref), channel_id=1, source_target_pairs={{0,1},{1,0},{2,3},{3,2},{4,5},{5,4},{6,7},{7,6},{8,9},{9,8},{10,11... | collective-permute-start | bytes 1105928 | tf_op jit(solution)/shard_map/ppermute | solution.py:33
  535.5 55.4 %all-to-all-start.5 = ((bf16[4,320,1152]{2,1,0:T(8,128)(2,1)}), bf16[4,320,1152]{2,1,0:T(8,128)(2,1)}, u32[]{:S(2)}, u32[]{:S(2)}) async-start(bf16[4,320,1152]{2,1,0:T(8,128)(2,1)} %bitcast.139), calls=%async_computation.5 | async-start | bytes 5898240 | tf_op jit(solution)/shard_map/all_to_all | solution.py:146
  543.5 23.4 %collective-permute-start.40 = (bf16[320,1152]{1,0:T(8,128)(2,1)}, bf16[320,1152]{1,0:T(8,128)(2,1)}, u32[]{:S(2)}, u32[]{:S(2)}) collective-permute-start(bf16[320,1152]{1,0:T(8,128)(2,1)} %get-tuple-element.241), channel_id=1, source_target_pairs={{0,1},{1,0},{2,3},{3,2},{4,5},{5,4},{6,7},{7,6},{8,9},{9,8},{10,11... | collective-permute-start | bytes 2211848 | tf_op jit(solution)/shard_map/ppermute | solution.py:33
  559.8 51.3 %collective-permute-start.42 = (bf16[288,1536]{1,0:T(8,128)(2,1)}, bf16[288,1536]{1,0:T(8,128)(2,1)}, u32[]{:S(2)}, u32[]{:S(2)}) collective-permute-start(bf16[288,1536]{1,0:T(8,128)(2,1)} %pad_maximum_fusion.13), channel_id=1, source_target_pairs={{0,0},{8,1},{16,2},{24,3},{2,8},{10,9},{18,10},{26,11},{1,16},{9,1... | collective-permute-start | bytes 2654216 | tf_op jit(solution)/shard_map/ppermute | solution.py:85
  561.7 48.5 %collective-permute-start.43 = (bf16[288,1344]{1,0:T(8,128)(2,1)}, bf16[288,1344]{1,0:T(8,128)(2,1)}, u32[]{:S(2)}, u32[]{:S(2)}) collective-permute-start(bf16[288,1344]{1,0:T(8,128)(2,1)} %pad_maximum_fusion.16), channel_id=1, source_target_pairs={{16,0},{24,1},{0,2},{8,3},{18,8},{26,9},{2,10},{10,11},{17,16},{25... | collective-permute-start | bytes 2322440 | tf_op jit(solution)/shard_map/ppermute | solution.py:85
  598.3 45.2 %all-to-all-start.6 = ((bf16[4,288,1152]{2,1,0:T(8,128)(2,1)}), bf16[4,288,1152]{2,1,0:T(8,128)(2,1)}, u32[]{:S(2)}, u32[]{:S(2)}) async-start(bf16[4,288,1152]{2,1,0:T(8,128)(2,1)} %pad_maximum_fusion.3), calls=%async_computation.6 | async-start | bytes 5308416 | tf_op jit(solution)/shard_map/all_to_all | solution.py:146
  612.8 34.0 %collective-permute-start.44 = (bf16[80,2304]{1,0:T(8,128)(2,1)}, bf16[80,2304]{1,0:T(8,128)(2,1)}, u32[]{:S(2)}, u32[]{:S(2)}) collective-permute-start(bf16[80,2304]{1,0:T(8,128)(2,1)} %get-tuple-element.240), channel_id=1, source_target_pairs={{0,8},{8,0},{16,24},{24,16},{1,9},{9,1},{17,25},{25,17},{2,10},{10... | collective-permute-start | bytes 1105928 | tf_op jit(solution)/shard_map/ppermute | solution.py:29
  614.7 32.1 %collective-permute-start.45 = (bf16[80,2304]{1,0:T(8,128)(2,1)}, bf16[80,2304]{1,0:T(8,128)(2,1)}, u32[]{:S(2)}, u32[]{:S(2)}) collective-permute-start(bf16[80,2304]{1,0:T(8,128)(2,1)} %get-tuple-element.239), channel_id=1, source_target_pairs={{0,16},{8,24},{16,0},{24,8},{1,17},{9,25},{17,1},{25,9},{2,18},{10... | collective-permute-start | bytes 1105928 | tf_op jit(solution)/shard_map/ppermute | solution.py:29
  616.2 30.6 %collective-permute-start.46 = (bf16[80,2304]{1,0:T(8,128)(2,1)}, bf16[80,2304]{1,0:T(8,128)(2,1)}, u32[]{:S(2)}, u32[]{:S(2)}) collective-permute-start(bf16[80,2304]{1,0:T(8,128)(2,1)} %get-tuple-element.238), channel_id=1, source_target_pairs={{0,24},{8,16},{16,8},{24,0},{1,25},{9,17},{17,9},{25,1},{2,26},{10... | collective-permute-start | bytes 1105928 | tf_op jit(solution)/shard_map/ppermute | solution.py:29
  657.4 47.1 %all-to-all-start.7 = ((bf16[4,288,1152]{2,1,0:T(8,128)(2,1)}), bf16[4,288,1152]{2,1,0:T(8,128)(2,1)S(1)}, u32[]{:S(2)}, u32[]{:S(2)}) async-start(bf16[4,288,1152]{2,1,0:T(8,128)(2,1)} %bitcast.45), calls=%async_computation.7 | async-start | bytes 5308416 | tf_op jit(solution)/shard_map/all_to_all | solution.py:146
  661.2 43.2 %collective-permute-start.48 = (bf16[288,768]{1,0:T(8,128)(2,1)}, bf16[288,768]{1,0:T(8,128)(2,1)}, u32[]{:S(2)}, u32[]{:S(2)}) collective-permute-start(bf16[288,768]{1,0:T(8,128)(2,1)} %slice.486), channel_id=1, source_target_pairs={{0,0},{8,1},{16,2},{24,3},{2,8},{10,9},{18,10},{26,11},{1,16},{9,1... | collective-permute-start | bytes 1327112 | tf_op jit(solution)/shard_map/ppermute | solution.py:85
  670.4 33.3 %collective-permute-start.49 = (bf16[288,672]{1,0:T(8,128)(2,1)}, bf16[288,672]{1,0:T(8,128)(2,1)S(1)}, u32[]{:S(2)}, u32[]{:S(2)}) collective-permute-start(bf16[288,672]{1,0:T(8,128)(2,1)} %slice.487), channel_id=1, source_target_pairs={{16,0},{24,1},{0,2},{8,3},{18,8},{26,9},{2,10},{10,11},{17,16},{25... | collective-permute-start | bytes 1161224 | tf_op jit(solution)/shard_map/ppermute | solution.py:85
  721.9 34.7 %collective-permute-start.50 = (bf16[288,1280]{1,0:T(8,128)(2,1)S(1)}, bf16[288,1280]{1,0:T(8,128)(2,1)S(1)}, u32[]{:S(2)}, u32[]{:S(2)}) collective-permute-start(bf16[288,1280]{1,0:T(8,128)(2,1)S(1)} %concatenate.144), channel_id=1, source_target_pairs={{0,0},{8,1},{16,2},{24,3},{2,8},{10,9},{18,10},{26,11},{1,16},{9,1... | collective-permute-start | bytes 2211848 | tf_op jit(solution)/shard_map/ppermute | solution.py:85
  (100 other events, 1568.2 us)
Sparse Core Ops, SparseCore 0:
  37.8 44.9 all-gather.5
  87.9 53.7 all-gather.7
  147.5 47.5 all-gather.9
  196.8 93.5 all-gather.13
  292.2 48.0 all-gather.11

commit v4 on v3

--- a/solution.py
+++ b/solution.py
@@ -38,14 +38,25 @@
 
 
 def row_send(rows):
-    return [rows] + [send_row(rows, k) for k in range(1, lax.axis_size(ROW))]
+    count = lax.axis_size(ROW)
+    if count != 4:
+        return [rows] + [send_row(rows, k) for k in range(1, count)]
+    side, across = send_row(rows, 1), send_row(rows, 2)
+    return [rows, side, across, send_row(across, 1)]
 
 
 def row_split(partial):
     count = lax.axis_size(ROW)
     height = partial.shape[0] // count
     parts = [partial[k * height : (k + 1) * height] for k in range(count)]
-    return [parts[0]] + [send_row(parts[k].astype(bf16), k) for k in range(1, count)]
+    if count != 4:
+        return [parts[0]] + [send_row(parts[k].astype(bf16), k) for k in range(1, count)]
+    far = send_row(parts[3].astype(bf16), 1)
+    return [
+        parts[0],
+        send_row(parts[1].astype(bf16), 1),
+        send_row((parts[2] + far.astype(f32)).astype(bf16), 2),
+    ]
 
 
 def row_sum(parts):

time: 781 us -> 769 us (0.985)
  starting transfers between devices: 165 us -> 138 us
  waiting for transfers between devices: 286 us -> 297 us
    ppermute x24, waiting for transfers between devices: 72.2 us -> 113 us  [send_row(): lax.ppermute(array, ROW, [(i, i ^ distance) for i in range(lax.axis_size(...]
    ppermute x14, waiting for transfers between devices: 125 us -> 100 us  [move(): return lax.ppermute(part, (ROW, 'tx', 'tc'), pairs)]
    ppermute x13, starting transfers between devices: 25.6 us -> 9.1 us  [swap_core(): return lax.ppermute(array, 'tc', [(0, 1), (1, 0)])]
    all_to_all x8, waiting for transfers between devices: 69.9 us -> 54.7 us  [exchange(): return lax.all_to_all(blocks, CHIPS, 0, 0, tiled=True)]
    ppermute x5, starting transfers between devices: 14.8 us -> 5.08 us  [on_device(): lax.ppermute(gain_sum, axis, [(i, i ^ 1 << bit) for i in range(count)])]
    ppermute x5, waiting for transfers between devices: 18.4 us -> 28 us  [on_device(): lax.ppermute(gain_sum, axis, [(i, i ^ 1 << bit) for i in range(count)])]
    all_to_all x8, starting transfers between devices: 36.8 us -> 45.1 us  [exchange(): return lax.all_to_all(blocks, CHIPS, 0, 0, tiled=True)]
  transfers between devices with their start and end apart: 70 -> 70, of which waited for: 26 -> 31; matrix products, arithmetic and copies ran while one was open for 27% -> 28% of each run, Pallas kernels for 9% -> 9%
where the time goes in v4:
time: 769 us; the launch traced here: 756 us
  waiting for transfers between devices  297 us (39%)
  starting transfers between devices  138 us (18%)
  local copies, waits for them, and re-layouts  92.7 us (12%)
  other arithmetic  85.9 us (11%)
  Pallas kernels  70 us (9%)
  matrix products  56.5 us (7%)
  between operations  15.9 us (2%)
    ppermute x24, waiting for transfers between devices, send_row(): lax.ppermute(array, ROW, [(i, i ^ distance) for i in range(lax.axis_size(...  113 us
    ppermute x14, waiting for transfers between devices, move(): return lax.ppermute(part, (ROW, 'tx', 'tc'), pairs)  100 us
    dot_general x12, matrix products, dot(): return lax.dot_general(a, b, (dims, ((), ())), preferred_element_type=f32)  56.5 us
    all_to_all x8, waiting for transfers between devices, exchange(): return lax.all_to_all(blocks, CHIPS, 0, 0, tiled=True)  54.7 us
    ppermute x14, starting transfers between devices, move(): return lax.ppermute(part, (ROW, 'tx', 'tc'), pairs)  48.8 us
    all_to_all x8, starting transfers between devices, exchange(): return lax.all_to_all(blocks, CHIPS, 0, 0, tiled=True)  45.1 us
    pallas_call x6, Pallas kernels, pair_sum(): pl.pallas_call(pair_kernel, grid=(rows // tile,), in_specs=[lefts, lefts,...  30.6 us
    ppermute x24, starting transfers between devices, send_row(): lax.ppermute(array, ROW, [(i, i ^ distance) for i in range(lax.axis_size(...  28.9 us
  transfers between devices with their start and end apart: 70, of which 31 were waited for; matrix products, arithmetic and copies ran while one was open for 28% of the time, Pallas kernels for 9%

profile of v4, /device:TPU:1, one launch (start us, length us, event | category | flops | bytes accessed | tf_op | source)
XLA Modules:
  0.0 756.2 jit_solution(3604203968087561794)
XLA Ops:
  9.2 4.6 collective-permute-start.4
  16.6 18.5 %collective-permute-done.5 = bf16[288,512]{0,1:T(8,128)(2,1)S(1)} collective-permute-done((bf16[288,512]{0,1:T(8,128)(2,1)S(1)}, bf16[288,512]{0,1:T(8,128)(2,1)S(1)}, u32[]{:S(2)}, u32[]{:S(2)}) %collective-permute-start.5) | collective-permute-done | bytes 294944 | tf_op jit(solution)/shard_map/ppermute | solution.py:96
  42.1 6.7 collective-permute-start.8
  51.1 14.0 %collective-permute-done.1 = bf16[81,2304]{1,0:T(8,128)(2,1)} collective-permute-done((bf16[81,2304]{1,0:T(8,128)(2,1)}, bf16[81,2304]{1,0:T(8,128)(2,1)}, u32[]{:S(2)}, u32[]{:S(2)}) %collective-permute-start.1) | collective-permute-done | bytes 373280 | tf_op jit(solution)/shard_map/ppermute | solution.py:29
  71.5 4.3 collective-permute-done.2
  93.5 6.0 fusion.53
  99.9 31.4 %collective-permute-done.15 = bf16[288,1600]{1,0:T(8,128)(2,1)} collective-permute-done((bf16[288,1600]{1,0:T(8,128)(2,1)}, bf16[288,1600]{1,0:T(8,128)(2,1)}, u32[]{:S(2)}, u32[]{:S(2)}) %collective-permute-start.15) | collective-permute-done | bytes 921632 | tf_op jit(solution)/shard_map/ppermute | solution.py:96
  144.7 4.7 all-to-all-start
  159.9 18.5 %collective-permute-done.11 = bf16[80,2304]{1,0:T(8,128)(2,1)} collective-permute-done((bf16[80,2304]{1,0:T(8,128)(2,1)S(1)}, bf16[80,2304]{1,0:T(8,128)(2,1)}, u32[]{:S(2)}, u32[]{:S(2)}) %collective-permute-start.11) | collective-permute-done | bytes 368672 | tf_op jit(solution)/shard_map/ppermute | solution.py:29
  178.8 10.2 %collective-permute-done.7 = bf16[288,672]{1,0:T(8,128)(2,1)} collective-permute-done((bf16[288,672]{1,0:T(8,128)(2,1)}, bf16[288,672]{1,0:T(8,128)(2,1)}, u32[]{:S(2)}, u32[]{:S(2)}) %collective-permute-start.7) | collective-permute-done | bytes 387104 | tf_op jit(solution)/shard_map/ppermute | solution.py:96
  197.6 4.6 all-to-all-start.1
  202.2 16.3 %shard_map.153.out_ref = f32[320,1152]{1,0:T(8,128)} custom-call(s32[1]{0:T(128)} %bitcast.row_ref, s32[320,4]{1,0:T(8,128)} %copy.145.query_ref, s32[4,2,640]{2,1,0:T(2,128)} %pad_add_fusion.key_ref, bf16[320,1152]{1,0:T(8,128)(2,1)} %copy.146.q_ref, bf16[4,4,80,1152]{3,2,1,0:T(8,128)(2,1)} %bitcast.25.near_ref, bf16[4,4,80,1152]{3,2,1,0:T(8,128)(2,1)} %bitcast.26.far_ref), custom_call_target="tpu_custom_call" | custom-call | flops 47185920000 | bytes 11796480 | tf_op jit(solution)/shard_map/pallas_call | solution.py:364
  224.8 4.9 fusion.52
  230.6 11.7 %collective-permute-start.17 = (bf16[80,2304]{1,0:T(8,128)(2,1)}, bf16[80,2304]{1,0:T(8,128)(2,1)}, u32[]{:S(2)}, u32[]{:S(2)}) collective-permute-start(bf16[80,2304]{1,0:T(8,128)(2,1)} %get-tuple-element.252), channel_id=1, source_target_pairs={{0,8},{8,0},{16,24},{24,16},{1,9},{9,1},{17,25},{25,17},{2,10},{10... | collective-permute-start | bytes 1105928 | tf_op jit(solution)/shard_map/ppermute | solution.py:29
  243.2 8.1 %collective-permute-done.17 = bf16[80,2304]{1,0:T(8,128)(2,1)} collective-permute-done((bf16[80,2304]{1,0:T(8,128)(2,1)}, bf16[80,2304]{1,0:T(8,128)(2,1)}, u32[]{:S(2)}, u32[]{:S(2)}) %collective-permute-start.17) | collective-permute-done | bytes 368672 | tf_op jit(solution)/shard_map/ppermute | solution.py:29
  257.2 4.8 collective-permute-done.16
  262.0 9.6 %collective-permute-done.18 = bf16[80,2304]{1,0:T(8,128)(2,1)} collective-permute-done((bf16[80,2304]{1,0:T(8,128)(2,1)}, bf16[80,2304]{1,0:T(8,128)(2,1)}, u32[]{:S(2)}, u32[]{:S(2)}) %collective-permute-start.18) | collective-permute-done | bytes 368672 | tf_op jit(solution)/shard_map/ppermute | solution.py:29
  284.8 13.2 %collective-permute-done.21 = bf16[80,2304]{1,0:T(8,128)(2,1)S(1)} collective-permute-done((bf16[80,2304]{1,0:T(8,128)(2,1)S(1)}, bf16[80,2304]{1,0:T(8,128)(2,1)S(1)}, u32[]{:S(2)}, u32[]{:S(2)}) %collective-permute-start.21) | collective-permute-done | bytes 368672 | tf_op jit(solution)/shard_map/ppermute | solution.py:29
  301.9 7.8 %collective-permute-done.22 = bf16[80,2304]{1,0:T(8,128)(2,1)S(1)} collective-permute-done((bf16[80,2304]{1,0:T(8,128)(2,1)S(1)}, bf16[80,2304]{1,0:T(8,128)(2,1)S(1)}, u32[]{:S(2)}, u32[]{:S(2)}) %collective-permute-start.22) | collective-permute-done | bytes 368672 | tf_op jit(solution)/shard_map/ppermute | solution.py:29
  311.6 6.1 copy.149
  317.7 7.2 fusion.1
  324.9 6.8 fusion.36
  331.8 7.7 %multiply_convert_fusion = (bf16[320,1440]{1,0:T(8,128)(2,1)S(1)}, bf16[320,1440]{1,0:T(8,128)(2,1)S(1)}, bf16[320,1440]{1,0:T(8,128)(2,1)S(1)}) fusion(f32[320,1440]{1,0:T(8,128)} %fusion.36, f32[320,1440]{1,0:T(8,128)} %fusion.1, bf16[2304,1440]{1,0:T(8,128)(2,1)} %all-gather.12.cloned.1.call-done, bf16[80,2304]{1,0:T(8,128)(2,1)} %copy-done.51, ...), kind=kOutput, calls=%fused_computation.13 | convolution fusion | flops 2136176640 | bytes 14561280 | tf_op jit(solution)/shard_map/dot_general | solution.py:25
  347.1 6.3 shard_map.154
  353.4 4.9 all-to-all-start.2
  362.8 7.8 %collective-permute-done.27 = bf16[80,2304]{1,0:T(8,128)(2,1)S(1)} collective-permute-done((bf16[80,2304]{1,0:T(8,128)(2,1)S(1)}, bf16[80,2304]{1,0:T(8,128)(2,1)S(1)}, u32[]{:S(2)}, u32[]{:S(2)}) %collective-permute-start.27) | collective-permute-done | bytes 368672 | tf_op jit(solution)/shard_map/ppermute | solution.py:29
  372.8 6.3 shard_map.155
  379.1 6.3 shard_map.156
  385.4 13.2 %all-to-all-done.2 = bf16[4,288,1440]{2,1,0:T(8,128)(2,1)} async-done(((bf16[4,288,1440]{2,1,0:T(8,128)(2,1)}), bf16[4,288,1440]{2,1,0:T(8,128)(2,1)}, u32[]{:S(2)}, u32[]{:S(2)}) %all-to-all-start.2) | async-done | bytes 3317792 | tf_op jit(solution)/shard_map/all_to_all | solution.py:157
  398.6 4.8 all-to-all-start.3
  413.5 10.3 %collective-permute-done.32 = bf16[80,2304]{1,0:T(8,128)(2,1)} collective-permute-done((bf16[80,2304]{1,0:T(8,128)(2,1)}, bf16[80,2304]{1,0:T(8,128)(2,1)}, u32[]{:S(2)}, u32[]{:S(2)}) %collective-permute-start.32) | collective-permute-done | bytes 368672 | tf_op jit(solution)/shard_map/ppermute | solution.py:29
  426.9 6.1 fusion
  436.1 7.3 all-to-all-done.3
  456.4 5.0 all-to-all-start.4
  466.2 23.0 %shard_map.157 = (f32[320,1152]{1,0:T(8,128)}, bf16[4,4,80,1152]{3,2,1,0:T(8,128)(2,1)}, bf16[4,4,80,1152]{3,2,1,0:T(8,128)(2,1)}) custom-call(s32[1]{0:T(128)} %bitcast.row_ref, s32[320,4]{1,0:T(8,128)} %copy.145.query_ref, s32[4,2,640]{2,1,0:T(2,128)} %pad_add_fusion.key_ref, bf16[320,1152]{1,0:T(8,128)(2,1)} %copy.146.q_ref, ...), custom_call_target="tpu_custom_call" | custom-call | flops 117964800000 | bytes 11796480 | tf_op jit(solution)/shard_map/pallas_call | solution.py:378
  489.3 11.8 %all-to-all-done.4 = bf16[4,288,1440]{2,1,0:T(8,128)(2,1)} async-done(((bf16[4,288,1440]{2,1,0:T(8,128)(2,1)}), bf16[4,288,1440]{2,1,0:T(8,128)(2,1)}, u32[]{:S(2)}, u32[]{:S(2)}) %all-to-all-start.4) | async-done | bytes 3317792 | tf_op jit(solution)/shard_map/all_to_all | solution.py:157
  519.7 4.6 all-to-all-start.5
  543.0 4.3 collective-permute-start.42
  558.4 16.8 %all-to-all-done.5 = bf16[4,320,1152]{2,1,0:T(8,128)(2,1)} async-done(((bf16[4,320,1152]{2,1,0:T(8,128)(2,1)}), bf16[4,320,1152]{2,1,0:T(8,128)(2,1)}, u32[]{:S(2)}, u32[]{:S(2)}) %all-to-all-start.5) | async-done | bytes 2949152 | tf_op jit(solution)/shard_map/all_to_all | solution.py:157
  582.0 5.0 fusion.56
  588.5 5.5 collective-permute-done.42
  595.3 12.8 %all-to-all-start.6 = ((bf16[4,288,1152]{2,1,0:T(8,128)(2,1)}), bf16[4,288,1152]{2,1,0:T(8,128)(2,1)}, u32[]{:S(2)}, u32[]{:S(2)}) async-start(bf16[4,288,1152]{2,1,0:T(8,128)(2,1)} %pad_maximum_fusion.3), calls=%async_computation.6 | async-start | bytes 5308416 | tf_op jit(solution)/shard_map/all_to_all | solution.py:157
  615.8 4.8 collective-permute-done.45
  623.9 4.6 shard_map.160
  633.7 7.0 collective-permute-done.46
  658.8 23.3 %collective-permute-done.54 = f32[2,2304]{1,0:T(2,128)S(1)} collective-permute-done((f32[2,2304]{1,0:T(2,128)S(1)}, f32[2,2304]{1,0:T(2,128)S(1)}, u32[]{:S(2)}, u32[]{:S(2)}) %collective-permute-start.54) | collective-permute-done | bytes 18464 | tf_op jit(solution)/shard_map/ppermute | solution.py:606
  696.4 7.7 %collective-permute-start.51 = (bf16[288,1024]{1,0:T(8,128)(2,1)}, bf16[288,1024]{1,0:T(8,128)(2,1)}, u32[]{:S(2)}, u32[]{:S(2)}) collective-permute-start(bf16[288,1024]{1,0:T(8,128)(2,1)} %pad_maximum_fusion.17), channel_id=1, source_target_pairs={{16,0},{24,1},{0,2},{8,3},{18,8},{26,9},{2,10},{10,11},{17,16},{25... | collective-permute-start | bytes 1769480 | tf_op jit(solution)/shard_map/ppermute | solution.py:96
  714.4 29.7 %collective-permute-done.50 = bf16[288,1280]{1,0:T(8,128)(2,1)S(1)} collective-permute-done((bf16[288,1280]{1,0:T(8,128)(2,1)S(1)}, bf16[288,1280]{1,0:T(8,128)(2,1)S(1)}, u32[]{:S(2)}, u32[]{:S(2)}) %collective-permute-start.50) | collective-permute-done | bytes 737312 | tf_op jit(solution)/shard_map/ppermute | solution.py:96
  (466 shorter events, 273.0 us)
Async XLA Ops:
  7.2 86.3 %all-gather.6.cloned.1.call-start = ((), (), s32[]{:S(2)}) async-start(), calls=%async_computation.8 | async-start | bytes 5971968 | tf_op jit(solution)/shard_map/all_gather | solution.py:114
  9.2 27.2 %collective-permute-start.4 = (bf16[288,640]{0,1:T(8,128)(2,1)S(1)}, bf16[288,640]{0,1:T(8,128)(2,1)S(1)}, u32[]{:S(2)}, u32[]{:S(2)}) collective-permute-start(bf16[288,640]{0,1:T(8,128)(2,1)S(1)} %slice.442), channel_id=1, source_target_pairs={{0,0},{1,8},{2,16},{3,24},{8,2},{9,10},{10,18},{11,26},{16,1},{17,... | collective-permute-start | bytes 1105928 | tf_op jit(solution)/shard_map/ppermute | solution.py:96
  13.9 21.2 %collective-permute-start.5 = (bf16[288,512]{0,1:T(8,128)(2,1)S(1)}, bf16[288,512]{0,1:T(8,128)(2,1)S(1)}, u32[]{:S(2)}, u32[]{:S(2)}) collective-permute-start(bf16[288,512]{0,1:T(8,128)(2,1)S(1)} %slice.443), channel_id=1, source_target_pairs={{0,16},{1,24},{2,0},{3,8},{8,18},{9,26},{10,2},{11,10},{16,17},{17... | collective-permute-start | bytes 884744 | tf_op jit(solution)/shard_map/ppermute | solution.py:96
  37.7 118.8 %all-gather.8.cloned.1.call-start = ((), (), s32[]{:S(2)}) async-start(), calls=%async_computation.9 | async-start | bytes 3317760 | tf_op jit(solution)/shard_map/all_gather | solution.py:114
  39.3 32.1 %collective-permute-start = (bf16[81,2304]{1,0:T(8,128)(2,1)}, bf16[81,2304]{1,0:T(8,128)(2,1)}, u32[]{:S(2)}, u32[]{:S(2)}) collective-permute-start(bf16[81,2304]{1,0:T(8,128)(2,1)} %constant_dynamic-update-slice_fusion), channel_id=1, source_target_pairs={{0,8},{8,0},{16,24},{24,16},{1,9},{9,1},{17,25},{25,17},{2,10},{10... | collective-permute-start | bytes 1119752 | tf_op jit(solution)/shard_map/ppermute | solution.py:29
  39.3 25.7 %collective-permute-start.1 = (bf16[81,2304]{1,0:T(8,128)(2,1)}, bf16[81,2304]{1,0:T(8,128)(2,1)}, u32[]{:S(2)}, u32[]{:S(2)}) collective-permute-start(bf16[81,2304]{1,0:T(8,128)(2,1)} %constant_dynamic-update-slice_fusion), channel_id=1, source_target_pairs={{0,16},{8,24},{16,0},{24,8},{1,17},{9,25},{17,1},{25,9},{2,18},{10... | collective-permute-start | bytes 1119752 | tf_op jit(solution)/shard_map/ppermute | solution.py:29
  40.1 29.4 %collective-permute-start.9 = (bf16[288,256]{1,0:T(8,128)(2,1)}, bf16[288,256]{1,0:T(8,128)(2,1)}, u32[]{:S(2)}, u32[]{:S(2)}) collective-permute-start(bf16[288,256]{1,0:T(8,128)(2,1)} %slice.452), channel_id=1, source_target_pairs={{0,16},{1,24},{2,0},{3,8},{8,18},{9,26},{10,2},{11,10},{16,17},{17... | collective-permute-start | bytes 442376 | tf_op jit(solution)/shard_map/ppermute | solution.py:96
  42.1 27.4 %collective-permute-start.8 = (bf16[288,320]{1,0:T(8,128)(2,1)}, bf16[288,320]{1,0:T(8,128)(2,1)}, u32[]{:S(2)}, u32[]{:S(2)}) collective-permute-start(bf16[288,320]{1,0:T(8,128)(2,1)} %slice.451), channel_id=1, source_target_pairs={{0,0},{1,8},{2,16},{3,24},{8,2},{9,10},{10,18},{11,26},{16,1},{17,... | collective-permute-start | bytes 552968 | tf_op jit(solution)/shard_map/ppermute | solution.py:96
  71.4 153.4 %all-gather.10.cloned.1.call-start = ((), (), s32[]{:S(2)}) async-start(), calls=%async_computation.10 | async-start | bytes 3317760 | tf_op jit(solution)/shard_map/all_gather | solution.py:114
  83.1 51.6 %collective-permute-start.14 = (bf16[288,1856]{1,0:T(8,128)(2,1)}, bf16[288,1856]{1,0:T(8,128)(2,1)}, u32[]{:S(2)}, u32[]{:S(2)}) collective-permute-start(bf16[288,1856]{1,0:T(8,128)(2,1)} %pad_maximum_fusion.6), channel_id=1, source_target_pairs={{0,0},{1,8},{2,16},{3,24},{8,2},{9,10},{10,18},{11,26},{16,1},{17,... | collective-permute-start | bytes 3207176 | tf_op jit(solution)/shard_map/ppermute | solution.py:96
  85.0 46.3 %collective-permute-start.15 = (bf16[288,1600]{1,0:T(8,128)(2,1)}, bf16[288,1600]{1,0:T(8,128)(2,1)}, u32[]{:S(2)}, u32[]{:S(2)}) collective-permute-start(bf16[288,1600]{1,0:T(8,128)(2,1)} %concatenate.119), channel_id=1, source_target_pairs={{0,16},{1,24},{2,0},{3,8},{8,18},{9,26},{10,2},{11,10},{16,17},{17... | collective-permute-start | bytes 2764808 | tf_op jit(solution)/shard_map/ppermute | solution.py:96
  137.6 187.3 %all-gather.14.cloned.1.call-start = ((), (), s32[]{:S(2)}) async-start(), calls=%async_computation.12 | async-start | bytes 7962624 | tf_op jit(solution)/shard_map/all_gather | solution.py:114
  144.7 46.3 %all-to-all-start = ((bf16[4,320,1152]{2,1,0:T(8,128)(2,1)}), bf16[4,320,1152]{2,1,0:T(8,128)(2,1)}, u32[]{:S(2)}, u32[]{:S(2)}) async-start(bf16[4,320,1152]{2,1,0:T(8,128)(2,1)} %broadcast_in_dim.30), calls=%async_computation | async-start | bytes 5898240 | tf_op jit(solution)/shard_map/all_to_all | solution.py:157
  149.5 182.3 %all-gather.12.cloned.1.call-start = ((), (), s32[]{:S(2)}) async-start(), calls=%async_computation.11 | async-start | bytes 7962624 | tf_op jit(solution)/shard_map/all_gather | solution.py:114
  149.5 29.3 %collective-permute-start.10 = (bf16[80,2304]{1,0:T(8,128)(2,1)S(1)}, bf16[80,2304]{1,0:T(8,128)(2,1)}, u32[]{:S(2)}, u32[]{:S(2)}) collective-permute-start(bf16[80,2304]{1,0:T(8,128)(2,1)S(1)} %copy-done.28), channel_id=1, source_target_pairs={{0,8},{8,0},{16,24},{24,16},{1,9},{9,1},{17,25},{25,17},{2,10},{10... | collective-permute-start | bytes 1105928 | tf_op jit(solution)/shard_map/ppermute | solution.py:29
  149.6 28.9 %collective-permute-start.11 = (bf16[80,2304]{1,0:T(8,128)(2,1)S(1)}, bf16[80,2304]{1,0:T(8,128)(2,1)}, u32[]{:S(2)}, u32[]{:S(2)}) collective-permute-start(bf16[80,2304]{1,0:T(8,128)(2,1)S(1)} %copy-done.28), channel_id=1, source_target_pairs={{0,16},{8,24},{16,0},{24,8},{1,17},{9,25},{17,1},{25,9},{2,18},{10... | collective-permute-start | bytes 1105928 | tf_op jit(solution)/shard_map/ppermute | solution.py:29
  149.7 39.3 %collective-permute-start.6 = (bf16[288,768]{1,0:T(8,128)(2,1)}, bf16[288,768]{1,0:T(8,128)(2,1)}, u32[]{:S(2)}, u32[]{:S(2)}) collective-permute-start(bf16[288,768]{1,0:T(8,128)(2,1)} %slice.439), channel_id=1, source_target_pairs={{0,0},{1,8},{2,16},{3,24},{8,2},{9,10},{10,18},{11,26},{16,1},{17,... | collective-permute-start | bytes 1327112 | tf_op jit(solution)/shard_map/ppermute | solution.py:96
  153.0 36.0 %collective-permute-start.7 = (bf16[288,672]{1,0:T(8,128)(2,1)}, bf16[288,672]{1,0:T(8,128)(2,1)}, u32[]{:S(2)}, u32[]{:S(2)}) collective-permute-start(bf16[288,672]{1,0:T(8,128)(2,1)} %slice.440), channel_id=1, source_target_pairs={{0,16},{1,24},{2,0},{3,8},{8,18},{9,26},{10,2},{11,10},{16,17},{17... | collective-permute-start | bytes 1161224 | tf_op jit(solution)/shard_map/ppermute | solution.py:96
  197.6 59.6 %all-to-all-start.1 = ((bf16[4,288,1440]{2,1,0:T(8,128)(2,1)}), bf16[4,288,1440]{2,1,0:T(8,128)(2,1)S(1)}, u32[]{:S(2)}, u32[]{:S(2)}) async-start(bf16[4,288,1440]{2,1,0:T(8,128)(2,1)} %broadcast_in_dim.31), calls=%async_computation.1 | async-start | bytes 7077888 | tf_op jit(solution)/shard_map/all_to_all | solution.py:157
  230.6 20.6 %collective-permute-start.17 = (bf16[80,2304]{1,0:T(8,128)(2,1)}, bf16[80,2304]{1,0:T(8,128)(2,1)}, u32[]{:S(2)}, u32[]{:S(2)}) collective-permute-start(bf16[80,2304]{1,0:T(8,128)(2,1)} %get-tuple-element.252), channel_id=1, source_target_pairs={{0,8},{8,0},{16,24},{24,16},{1,9},{9,1},{17,25},{25,17},{2,10},{10... | collective-permute-start | bytes 1105928 | tf_op jit(solution)/shard_map/ppermute | solution.py:29
  243.1 18.9 %collective-permute-start.16 = (bf16[80,2304]{1,0:T(8,128)(2,1)}, bf16[80,2304]{1,0:T(8,128)(2,1)}, u32[]{:S(2)}, u32[]{:S(2)}) collective-permute-start(bf16[80,2304]{1,0:T(8,128)(2,1)} %get-tuple-element.253), channel_id=1, source_target_pairs={{0,8},{8,0},{16,24},{24,16},{1,9},{9,1},{17,25},{25,17},{2,10},{10... | collective-permute-start | bytes 1105928 | tf_op jit(solution)/shard_map/ppermute | solution.py:29
  253.8 17.8 %collective-permute-start.18 = (bf16[80,2304]{1,0:T(8,128)(2,1)}, bf16[80,2304]{1,0:T(8,128)(2,1)}, u32[]{:S(2)}, u32[]{:S(2)}) collective-permute-start(bf16[80,2304]{1,0:T(8,128)(2,1)} %get-tuple-element.234), channel_id=1, source_target_pairs={{0,16},{8,24},{16,0},{24,8},{1,17},{9,25},{17,1},{25,9},{2,18},{10... | collective-permute-start | bytes 1105928 | tf_op jit(solution)/shard_map/ppermute | solution.py:29
  275.2 36.4 %collective-permute-start.19 = (bf16[1152,1440]{0,1:T(8,128)(2,1)}, bf16[1152,1440]{0,1:T(8,128)(2,1)}, u32[]{:S(2)}, u32[]{:S(2)}) collective-permute-start(bf16[1152,1440]{0,1:T(8,128)(2,1)} %copy.148), channel_id=1, source_target_pairs={{0,1},{1,0},{2,3},{3,2},{4,5},{5,4},{6,7},{7,6},{8,9},{9,8},{10,11... | collective-permute-start | bytes 9953288 | tf_op jit(solution)/shard_map/ppermute | solution.py:33
  280.0 18.0 %collective-permute-start.21 = (bf16[80,2304]{1,0:T(8,128)(2,1)S(1)}, bf16[80,2304]{1,0:T(8,128)(2,1)S(1)}, u32[]{:S(2)}, u32[]{:S(2)}) collective-permute-start(bf16[80,2304]{1,0:T(8,128)(2,1)S(1)} %multiply_convert_fusion.4), channel_id=1, source_target_pairs={{0,16},{8,24},{16,0},{24,8},{1,17},{9,25},{17,1},{25,9},{2,18},{10... | collective-permute-start | bytes 1105928 | tf_op jit(solution)/shard_map/ppermute | solution.py:29
  283.8 18.1 %collective-permute-start.20 = (bf16[80,2304]{1,0:T(8,128)(2,1)S(1)}, bf16[80,2304]{1,0:T(8,128)(2,1)S(1)}, u32[]{:S(2)}, u32[]{:S(2)}) collective-permute-start(bf16[80,2304]{1,0:T(8,128)(2,1)S(1)} %multiply_convert_fusion.4), channel_id=1, source_target_pairs={{0,8},{8,0},{16,24},{24,16},{1,9},{9,1},{17,25},{25,17},{2,10},{10... | collective-permute-start | bytes 1105928 | tf_op jit(solution)/shard_map/ppermute | solution.py:29
  300.5 46.5 %collective-permute-start.23 = (bf16[320,1152]{1,0:T(8,128)(2,1)}, bf16[320,1152]{1,0:T(8,128)(2,1)}, u32[]{:S(2)}, u32[]{:S(2)}) collective-permute-start(bf16[320,1152]{1,0:T(8,128)(2,1)} %get-tuple-element.251), channel_id=1, source_target_pairs={{0,1},{1,0},{2,3},{3,2},{4,5},{5,4},{6,7},{7,6},{8,9},{9,8},{10,11... | collective-permute-start | bytes 2211848 | tf_op jit(solution)/shard_map/ppermute | solution.py:33
  310.8 42.5 %collective-permute-start.25 = (bf16[320,1152]{1,0:T(8,128)(2,1)}, bf16[320,1152]{1,0:T(8,128)(2,1)}, u32[]{:S(2)}, u32[]{:S(2)}) collective-permute-start(bf16[320,1152]{1,0:T(8,128)(2,1)} %get-tuple-element.248), channel_id=1, source_target_pairs={{0,1},{1,0},{2,3},{3,2},{4,5},{5,4},{6,7},{7,6},{8,9},{9,8},{10,11... | collective-permute-start | bytes 2211848 | tf_op jit(solution)/shard_map/ppermute | solution.py:33
  353.4 45.2 %all-to-all-start.2 = ((bf16[4,288,1440]{2,1,0:T(8,128)(2,1)}), bf16[4,288,1440]{2,1,0:T(8,128)(2,1)}, u32[]{:S(2)}, u32[]{:S(2)}) async-start(bf16[4,288,1440]{2,1,0:T(8,128)(2,1)} %bitcast.30), calls=%async_computation.2 | async-start | bytes 7077888 | tf_op jit(solution)/shard_map/all_to_all | solution.py:157
  362.2 23.2 %collective-permute-start.26 = (bf16[80,2304]{1,0:T(8,128)(2,1)S(1)}, bf16[80,2304]{1,0:T(8,128)(2,1)}, u32[]{:S(2)}, u32[]{:S(2)}) collective-permute-start(bf16[80,2304]{1,0:T(8,128)(2,1)S(1)} %get-tuple-element.247), channel_id=1, source_target_pairs={{0,8},{8,0},{16,24},{24,16},{1,9},{9,1},{17,25},{25,17},{2,10},{10... | collective-permute-start | bytes 1105928 | tf_op jit(solution)/shard_map/ppermute | solution.py:29
  398.6 44.8 %all-to-all-start.3 = ((bf16[4,288,1440]{2,1,0:T(8,128)(2,1)}), bf16[4,288,1440]{2,1,0:T(8,128)(2,1)}, u32[]{:S(2)}, u32[]{:S(2)}) async-start(bf16[4,288,1440]{2,1,0:T(8,128)(2,1)} %bitcast.31), calls=%async_computation.3 | async-start | bytes 7077888 | tf_op jit(solution)/shard_map/all_to_all | solution.py:157
  407.6 28.4 %collective-permute-start.31 = (bf16[80,2304]{1,0:T(8,128)(2,1)}, bf16[80,2304]{1,0:T(8,128)(2,1)}, u32[]{:S(2)}, u32[]{:S(2)}) collective-permute-start(bf16[80,2304]{1,0:T(8,128)(2,1)} %get-tuple-element.143), channel_id=1, source_target_pairs={{0,8},{8,0},{16,24},{24,16},{1,9},{9,1},{17,25},{25,17},{2,10},{10... | collective-permute-start | bytes 1105928 | tf_op jit(solution)/shard_map/ppermute | solution.py:29
  411.9 24.2 %collective-permute-start.34 = (bf16[320,1152]{1,0:T(8,128)(2,1)}, bf16[320,1152]{1,0:T(8,128)(2,1)S(1)}, u32[]{:S(2)}, u32[]{:S(2)}) collective-permute-start(bf16[320,1152]{1,0:T(8,128)(2,1)} %get-tuple-element.244), channel_id=1, source_target_pairs={{0,1},{1,0},{2,3},{3,2},{4,5},{5,4},{6,7},{7,6},{8,9},{9,8},{10,11... | collective-permute-start | bytes 2211848 | tf_op jit(solution)/shard_map/ppermute | solution.py:33
  456.4 44.8 %all-to-all-start.4 = ((bf16[4,288,1440]{2,1,0:T(8,128)(2,1)}), bf16[4,288,1440]{2,1,0:T(8,128)(2,1)}, u32[]{:S(2)}, u32[]{:S(2)}) async-start(bf16[4,288,1440]{2,1,0:T(8,128)(2,1)} %bitcast.32), calls=%async_computation.4 | async-start | bytes 7077888 | tf_op jit(solution)/shard_map/all_to_all | solution.py:157
  461.3 27.9 %collective-permute-start.35 = (bf16[80,2304]{1,0:T(8,128)(2,1)}, bf16[80,2304]{1,0:T(8,128)(2,1)S(1)}, u32[]{:S(2)}, u32[]{:S(2)}) collective-permute-start(bf16[80,2304]{1,0:T(8,128)(2,1)} %get-tuple-element.243), channel_id=1, source_target_pairs={{0,8},{8,0},{16,24},{24,16},{1,9},{9,1},{17,25},{25,17},{2,10},{10... | collective-permute-start | bytes 1105928 | tf_op jit(solution)/shard_map/ppermute | solution.py:29
  464.2 25.1 %collective-permute-start.37 = (bf16[80,2304]{1,0:T(8,128)(2,1)S(1)}, bf16[80,2304]{1,0:T(8,128)(2,1)S(1)}, u32[]{:S(2)}, u32[]{:S(2)}) collective-permute-start(bf16[80,2304]{1,0:T(8,128)(2,1)S(1)} %get-tuple-element.230), channel_id=1, source_target_pairs={{0,16},{8,24},{16,0},{24,8},{1,17},{9,25},{17,1},{25,9},{2,18},{10... | collective-permute-start | bytes 1105928 | tf_op jit(solution)/shard_map/ppermute | solution.py:29
  509.9 42.6 %collective-permute-start.41 = (bf16[320,576]{1,0:T(8,128)(2,1)S(1)}, bf16[320,576]{1,0:T(8,128)(2,1)S(1)}, u32[]{:S(2)}, u32[]{:S(2)}) collective-permute-start(bf16[320,576]{1,0:T(8,128)(2,1)S(1)} %copy.159.right_ref), channel_id=1, source_target_pairs={{0,1},{1,0},{2,3},{3,2},{4,5},{5,4},{6,7},{7,6},{8,9},{9,8},{10,11... | collective-permute-start | bytes 1105928 | tf_op jit(solution)/shard_map/ppermute | solution.py:33
  519.7 55.5 %all-to-all-start.5 = ((bf16[4,320,1152]{2,1,0:T(8,128)(2,1)}), bf16[4,320,1152]{2,1,0:T(8,128)(2,1)}, u32[]{:S(2)}, u32[]{:S(2)}) async-start(bf16[4,320,1152]{2,1,0:T(8,128)(2,1)} %bitcast.139), calls=%async_computation.5 | async-start | bytes 5898240 | tf_op jit(solution)/shard_map/all_to_all | solution.py:157
  526.6 25.9 %collective-permute-start.40 = (bf16[320,1152]{1,0:T(8,128)(2,1)}, bf16[320,1152]{1,0:T(8,128)(2,1)}, u32[]{:S(2)}, u32[]{:S(2)}) collective-permute-start(bf16[320,1152]{1,0:T(8,128)(2,1)} %get-tuple-element.240), channel_id=1, source_target_pairs={{0,1},{1,0},{2,3},{3,2},{4,5},{5,4},{6,7},{7,6},{8,9},{9,8},{10,11... | collective-permute-start | bytes 2211848 | tf_op jit(solution)/shard_map/ppermute | solution.py:33
  543.0 51.0 %collective-permute-start.42 = (bf16[288,1536]{1,0:T(8,128)(2,1)}, bf16[288,1536]{1,0:T(8,128)(2,1)}, u32[]{:S(2)}, u32[]{:S(2)}) collective-permute-start(bf16[288,1536]{1,0:T(8,128)(2,1)} %pad_maximum_fusion.13), channel_id=1, source_target_pairs={{0,0},{8,1},{16,2},{24,3},{2,8},{10,9},{18,10},{26,11},{1,16},{9,1... | collective-permute-start | bytes 2654216 | tf_op jit(solution)/shard_map/ppermute | solution.py:96
  547.4 41.1 %collective-permute-start.43 = (bf16[288,1344]{1,0:T(8,128)(2,1)}, bf16[288,1344]{1,0:T(8,128)(2,1)}, u32[]{:S(2)}, u32[]{:S(2)}) collective-permute-start(bf16[288,1344]{1,0:T(8,128)(2,1)} %pad_maximum_fusion.16), channel_id=1, source_target_pairs={{16,0},{24,1},{0,2},{8,3},{18,8},{26,9},{2,10},{10,11},{17,16},{25... | collective-permute-start | bytes 2322440 | tf_op jit(solution)/shard_map/ppermute | solution.py:96
  595.3 35.2 %all-to-all-start.6 = ((bf16[4,288,1152]{2,1,0:T(8,128)(2,1)}), bf16[4,288,1152]{2,1,0:T(8,128)(2,1)}, u32[]{:S(2)}, u32[]{:S(2)}) async-start(bf16[4,288,1152]{2,1,0:T(8,128)(2,1)} %pad_maximum_fusion.3), calls=%async_computation.6 | async-start | bytes 5308416 | tf_op jit(solution)/shard_map/all_to_all | solution.py:157
  610.0 23.7 %collective-permute-start.44 = (bf16[80,2304]{1,0:T(8,128)(2,1)}, bf16[80,2304]{1,0:T(8,128)(2,1)}, u32[]{:S(2)}, u32[]{:S(2)}) collective-permute-start(bf16[80,2304]{1,0:T(8,128)(2,1)} %get-tuple-element.239), channel_id=1, source_target_pairs={{0,8},{8,0},{16,24},{24,16},{1,9},{9,1},{17,25},{25,17},{2,10},{10... | collective-permute-start | bytes 1105928 | tf_op jit(solution)/shard_map/ppermute | solution.py:29
  622.5 18.2 %collective-permute-start.46 = (bf16[80,2304]{1,0:T(8,128)(2,1)}, bf16[80,2304]{1,0:T(8,128)(2,1)}, u32[]{:S(2)}, u32[]{:S(2)}) collective-permute-start(bf16[80,2304]{1,0:T(8,128)(2,1)} %get-tuple-element.228), channel_id=1, source_target_pairs={{0,16},{8,24},{16,0},{24,8},{1,17},{9,25},{17,1},{25,9},{2,18},{10... | collective-permute-start | bytes 1105928 | tf_op jit(solution)/shard_map/ppermute | solution.py:29
  647.0 46.6 %all-to-all-start.7 = ((bf16[4,288,1152]{2,1,0:T(8,128)(2,1)}), bf16[4,288,1152]{2,1,0:T(8,128)(2,1)S(1)}, u32[]{:S(2)}, u32[]{:S(2)}) async-start(bf16[4,288,1152]{2,1,0:T(8,128)(2,1)} %bitcast.45), calls=%async_computation.7 | async-start | bytes 5308416 | tf_op jit(solution)/shard_map/all_to_all | solution.py:157
  650.7 39.3 %collective-permute-start.48 = (bf16[288,768]{1,0:T(8,128)(2,1)}, bf16[288,768]{1,0:T(8,128)(2,1)}, u32[]{:S(2)}, u32[]{:S(2)}) collective-permute-start(bf16[288,768]{1,0:T(8,128)(2,1)} %slice.480), channel_id=1, source_target_pairs={{0,0},{8,1},{16,2},{24,3},{2,8},{10,9},{18,10},{26,11},{1,16},{9,1... | collective-permute-start | bytes 1327112 | tf_op jit(solution)/shard_map/ppermute | solution.py:96
  653.1 36.0 %collective-permute-start.49 = (bf16[288,672]{1,0:T(8,128)(2,1)}, bf16[288,672]{1,0:T(8,128)(2,1)S(1)}, u32[]{:S(2)}, u32[]{:S(2)}) collective-permute-start(bf16[288,672]{1,0:T(8,128)(2,1)} %slice.481), channel_id=1, source_target_pairs={{16,0},{24,1},{0,2},{8,3},{18,8},{26,9},{2,10},{10,11},{17,16},{25... | collective-permute-start | bytes 1161224 | tf_op jit(solution)/shard_map/ppermute | solution.py:96
  654.9 27.1 %collective-permute-start.54 = (f32[2,2304]{1,0:T(2,128)S(1)}, f32[2,2304]{1,0:T(2,128)S(1)}, u32[]{:S(2)}, u32[]{:S(2)}) collective-permute-start(f32[2,2304]{1,0:T(2,128)S(1)} %fusion.76), channel_id=1, source_target_pairs={{0,4},{4,0},{1,5},{5,1},{2,6},{6,2},{3,7},{7,3},{8,12},{12,8},{9,1... | collective-permute-start | bytes 55304 | tf_op jit(solution)/shard_map/ppermute | solution.py:606
  704.5 39.6 %collective-permute-start.50 = (bf16[288,1280]{1,0:T(8,128)(2,1)S(1)}, bf16[288,1280]{1,0:T(8,128)(2,1)S(1)}, u32[]{:S(2)}, u32[]{:S(2)}) collective-permute-start(bf16[288,1280]{1,0:T(8,128)(2,1)S(1)} %concatenate.144), channel_id=1, source_target_pairs={{0,0},{8,1},{16,2},{24,3},{2,8},{10,9},{18,10},{26,11},{1,16},{9,1... | collective-permute-start | bytes 2211848 | tf_op jit(solution)/shard_map/ppermute | solution.py:96
  (86 other events, 1094.8 us)
Sparse Core Ops, SparseCore 0:
  37.8 46.0 all-gather.5
  85.8 51.6 all-gather.7
  139.4 54.0 all-gather.9
  195.2 81.5 all-gather.13
  278.6 53.0 all-gather.11

commit v5 on v4

--- a/solution.py
+++ b/solution.py
@@ -151,6 +151,11 @@
         ),
     )(*left, right, swap_core(right))
     return total.reshape(chips, -1, wide)
+
+
+def near_dot(array, parts):
+    half = parts[0].shape[0]
+    return dot(array[:, :half], parts[0]) + dot(array[:, half:], parts[1])
 
 
 def exchange(blocks):
@@ -432,8 +437,8 @@
     x_parts = row_send(rows_of([x_own, small]))
     kv_full = plane_gather(*unbundle(turn(bundle([w_kv], [near * 2 * HD])), [2 * features], [near * 2 * HD]))
     q_full = plane_gather(*unbundle(turn(bundle([w_qkv[0]], [near * HD])), [features], [near * HD]))
-    first = bundle([w_gate_up[0], w_gate_up[1], w_out.T], [near_units, near_units, near * HD])
-    second = bundle([w_down.T], [near_units])
+    first = bundle([w_gate_up[0], w_out.T], [near_units, near * HD])
+    second = bundle([w_gate_up[1], w_down.T], [near_units, near_units])
     x_parts, first, second = fence(x_parts, first, second)
     first = turn(first)
     small = rows_of([part[own:] for part in x_parts])
@@ -480,10 +485,8 @@
     mine, second, branch_f, query_info, key_info = fence(
         mine, second, branch_f, query_info, key_info
     )
-    gate_moved, up_moved, out_moved = unbundle(
-        after(first, mine), [units, units, features], [near_units, near_units, near * HD]
-    )
-    out_full, gate_full, up_full = plane_gather(out_moved), plane_gather(gate_moved), plane_gather(up_moved)
+    gate_moved, out_moved = unbundle(after(first, mine), [units, features], [near_units, near * HD])
+    out_full, gate_full = plane_gather(out_moved), plane_gather(gate_moved)
     second = turn(second)
     f_parts = row_send(branch_f)
     chips = b_n * x_n
@@ -491,7 +494,8 @@
     queries = rotate(dot(after(normed_a, mine), q_full), cosine, sine_table)
     queries = side_by_side(queries.astype(bf16) * bf16(HD**-0.5), None)
     kv, second, queries, f_parts = fence(kv, second, queries, f_parts)
-    (down_moved,) = unbundle(second, [units], [near_units])
+    up_moved, down_moved = unbundle(second, [units, units], [near_units, near_units])
+    up_full = plane_gather(up_moved)
     kv = [t.reshape(chips, rows_n, own, -1) for t in (kv, swap_core(kv))]
     saved = attend(row, query_info, key_info, queries, kv)
     attended = saved.reshape(group, heads, 2, HD)[:, :, 1].reshape(group, -1).astype(bf16)
@@ -500,7 +504,7 @@
     down_near = exchange(jnp.broadcast_to(down_moved[None], (chips,) + down_moved.shape))
     parts, down_near = fence(parts, down_near)
     down_near = down_near.reshape(-1, units)
-    down_full = rows_of([down_near, swap_core(down_near)])
+    down_full = [down_near, swap_core(down_near)]
     mid = x_own.astype(f32) + depth_scale * row_sum(parts)
     inv_f = inverse_rms(mid)
     unit_f = mid * inv_f
@@ -513,7 +517,7 @@
     hidden = (silu * up).astype(bf16)
     gf_twin = with_twin(grad_branch_f)
     nf_twin = with_twin(normed_f)
-    grad_hidden = dot(columns(core_halves(grad_branch_f)), down_full)
+    grad_hidden = near_dot(columns(core_halves(grad_branch_f)), down_full)
     grad_gate = (grad_hidden * up * sig * (1.0 + gate * (1.0 - sig))).astype(bf16)
     grad_up = (grad_hidden * silu).astype(bf16)
     normed_part = dot(grad_gate, gate_full, ((1,), (1,))) + dot(grad_up, up_full, ((1,), (1,)))
@@ -535,7 +539,7 @@
     parts = row_send(branch_a)
     gate_sum = exchange(gate_pair)
     down_sum = chip_sum(down_sum)
-    output_part = dot(after(hidden, branch_a), down_full, ((1,), (1,)))
+    output_part = columns([dot(after(hidden, branch_a), t, ((1,), (1,))) for t in down_full])
     na_twin = with_twin(after(normed_a, branch_a))
     attended = after(attended, branch_a)
     parts, gate_sum, down_sum, up_pair, output_part, na_twin, attended = fence(

time: 769 us -> 763 us (level)
    ppermute x14, waiting for transfers between devices: 100 us -> 72 us  [move(): return lax.ppermute(part, (ROW, 'tx', 'tc'), pairs)]
    ppermute x24, waiting for transfers between devices: 113 us -> 137 us  [send_row(): lax.ppermute(array, ROW, [(i, i ^ distance) for i in range(lax.axis_size(...]
    concatenate x11 -> x15, other arithmetic: 12.5 us -> 17.3 us  [columns(): return jnp.concatenate(parts, axis=1)]
    dot_general x12 -> x14, matrix products: 56.5 us -> 54.1 us  [dot(): return lax.dot_general(a, b, (dims, ((), ())), preferred_element_type=f32)]
    unnamed x138 -> x142, local copies, waits for them, and re-layouts: 15.5 us -> 16.4 us
  transfers between devices with their start and end apart: 70 -> 70, of which waited for: 31 -> 33; matrix products, arithmetic and copies ran while one was open for 28% -> 27% of each run, Pallas kernels for 9% -> 9%
where the time goes in v5:
time: 763 us; the launch traced here: 750 us
  waiting for transfers between devices  297 us (39%)
  starting transfers between devices  138 us (18%)
  other arithmetic  88.9 us (12%)
  local copies, waits for them, and re-layouts  86 us (11%)
  Pallas kernels  70.2 us (9%)
  matrix products  54.1 us (7%)
  between operations  16 us (2%)
    ppermute x24, waiting for transfers between devices, send_row(): lax.ppermute(array, ROW, [(i, i ^ distance) for i in range(lax.axis_size(...  137 us
    ppermute x14, waiting for transfers between devices, move(): return lax.ppermute(part, (ROW, 'tx', 'tc'), pairs)  72 us
    all_to_all x8, waiting for transfers between devices, exchange(): return lax.all_to_all(blocks, CHIPS, 0, 0, tiled=True)  60.2 us
    dot_general x14, matrix products, dot(): return lax.dot_general(a, b, (dims, ((), ())), preferred_element_type=f32)  54.1 us
    ppermute x14, starting transfers between devices, move(): return lax.ppermute(part, (ROW, 'tx', 'tc'), pairs)  46.8 us
    all_to_all x8, starting transfers between devices, exchange(): return lax.all_to_all(blocks, CHIPS, 0, 0, tiled=True)  44.1 us
    pallas_call x6, Pallas kernels, pair_sum(): pl.pallas_call(pair_kernel, grid=(rows // tile,), in_specs=[lefts, lefts,...  30.7 us
    ppermute x24, starting transfers between devices, send_row(): lax.ppermute(array, ROW, [(i, i ^ distance) for i in range(lax.axis_size(...  27.4 us
  transfers between devices with their start and end apart: 70, of which 33 were waited for; matrix products, arithmetic and copies ran while one was open for 27% of the time, Pallas kernels for 9%

profile of v5, /device:TPU:1, one launch (start us, length us, event | category | flops | bytes accessed | tf_op | source)
XLA Modules:
  0.0 749.9 jit_solution(4374369118630357353)
XLA Ops:
  9.2 4.6 collective-permute-start.4
  16.6 18.5 %collective-permute-done.5 = bf16[288,512]{0,1:T(8,128)(2,1)S(1)} collective-permute-done((bf16[288,512]{0,1:T(8,128)(2,1)S(1)}, bf16[288,512]{0,1:T(8,128)(2,1)S(1)}, u32[]{:S(2)}, u32[]{:S(2)}) %collective-permute-start.5) | collective-permute-done | bytes 294944 | tf_op jit(solution)/shard_map/ppermute | solution.py:96
  42.1 6.6 collective-permute-start.8
  53.3 11.8 %collective-permute-done.1 = bf16[81,2304]{1,0:T(8,128)(2,1)} collective-permute-done((bf16[81,2304]{1,0:T(8,128)(2,1)}, bf16[81,2304]{1,0:T(8,128)(2,1)}, u32[]{:S(2)}, u32[]{:S(2)}) %collective-permute-start.1) | collective-permute-done | bytes 373280 | tf_op jit(solution)/shard_map/ppermute | solution.py:29
  70.4 5.4 collective-permute-done.2
  85.0 3.8 collective-permute-start.15
  93.5 6.0 fusion.46
  99.9 15.6 %collective-permute-done.15 = bf16[288,928]{1,0:T(8,128)(2,1)} collective-permute-done((bf16[288,928]{1,0:T(8,128)(2,1)}, bf16[288,928]{1,0:T(8,128)(2,1)}, u32[]{:S(2)}, u32[]{:S(2)}) %collective-permute-start.15) | collective-permute-done | bytes 534560 | tf_op jit(solution)/shard_map/ppermute | solution.py:96
  124.2 4.6 all-to-all-start
  139.4 46.3 %collective-permute-done.11 = bf16[80,2304]{1,0:T(8,128)(2,1)} collective-permute-done((bf16[80,2304]{1,0:T(8,128)(2,1)S(1)}, bf16[80,2304]{1,0:T(8,128)(2,1)}, u32[]{:S(2)}, u32[]{:S(2)}) %collective-permute-start.11) | collective-permute-done | bytes 368672 | tf_op jit(solution)/shard_map/ppermute | solution.py:29
  186.1 7.8 %collective-permute-done.12 = bf16[80,2304]{1,0:T(8,128)(2,1)S(1)} collective-permute-done((bf16[80,2304]{1,0:T(8,128)(2,1)}, bf16[80,2304]{1,0:T(8,128)(2,1)S(1)}, u32[]{:S(2)}, u32[]{:S(2)}) %collective-permute-start.12) | collective-permute-done | bytes 368672 | tf_op jit(solution)/shard_map/ppermute | solution.py:29
  210.4 16.5 %shard_map.153.out_ref = f32[320,1152]{1,0:T(8,128)} custom-call(s32[1]{0:T(128)} %bitcast.row_ref, s32[320,4]{1,0:T(8,128)} %copy.144.query_ref, s32[4,2,640]{2,1,0:T(2,128)} %pad_add_fusion.key_ref, bf16[320,1152]{1,0:T(8,128)(2,1)} %copy.145.q_ref, bf16[4,4,80,1152]{3,2,1,0:T(8,128)(2,1)} %bitcast.25.near_ref, bf16[4,4,80,1152]{3,2,1,0:T(8,128)(2,1)} %bitcast.26.far_ref), custom_call_target="tpu_custom_call" | custom-call | flops 47185920000 | bytes 11796480 | tf_op jit(solution)/shard_map/pallas_call | solution.py:369
  233.2 4.9 fusion.45
  241.3 8.2 %collective-permute-done.17 = bf16[80,2304]{1,0:T(8,128)(2,1)} collective-permute-done((bf16[80,2304]{1,0:T(8,128)(2,1)}, bf16[80,2304]{1,0:T(8,128)(2,1)}, u32[]{:S(2)}, u32[]{:S(2)}) %collective-permute-start.17) | collective-permute-done | bytes 368672 | tf_op jit(solution)/shard_map/ppermute | solution.py:29
  260.9 9.3 %collective-permute-done.18 = bf16[80,2304]{1,0:T(8,128)(2,1)} collective-permute-done((bf16[80,2304]{1,0:T(8,128)(2,1)}, bf16[80,2304]{1,0:T(8,128)(2,1)}, u32[]{:S(2)}, u32[]{:S(2)}) %collective-permute-start.18) | collective-permute-done | bytes 368672 | tf_op jit(solution)/shard_map/ppermute | solution.py:29
  270.2 4.1 copy.147
  284.5 13.7 %collective-permute-done.21 = bf16[80,2304]{1,0:T(8,128)(2,1)S(1)} collective-permute-done((bf16[80,2304]{1,0:T(8,128)(2,1)S(1)}, bf16[80,2304]{1,0:T(8,128)(2,1)S(1)}, u32[]{:S(2)}, u32[]{:S(2)}) %collective-permute-start.21) | collective-permute-done | bytes 368672 | tf_op jit(solution)/shard_map/ppermute | solution.py:29
  301.4 6.8 collective-permute-done.22
  316.6 6.8 fusion.29
  323.5 7.7 %multiply_convert_fusion = (bf16[320,1440]{1,0:T(8,128)(2,1)S(1)}, bf16[320,1440]{1,0:T(8,128)(2,1)S(1)}, bf16[320,1440]{1,0:T(8,128)(2,1)S(1)}) fusion(f32[320,1440]{1,0:T(8,128)} %fusion.29, f32[320,1440]{1,0:T(8,128)} %convolution_add_fusion.2, bf16[2304,1440]{1,0:T(8,128)(2,1)} %all-gather.12.cloned.1.call-done, bf16[80,2304]{1,0:T(8,128)(2,1)} %copy-done.51, ...), kind=kOutput, calls=%fused_computation.12 | convolution fusion | flops 2136176640 | bytes 14561280 | tf_op jit(solution)/shard_map/dot_general | solution.py:25
  334.6 4.1 convolution_add_fusion.1
  338.7 6.4 shard_map.154
  345.1 4.9 all-to-all-start.2
  354.5 7.8 %collective-permute-done.27 = bf16[80,2304]{1,0:T(8,128)(2,1)S(1)} collective-permute-done((bf16[80,2304]{1,0:T(8,128)(2,1)S(1)}, bf16[80,2304]{1,0:T(8,128)(2,1)S(1)}, u32[]{:S(2)}, u32[]{:S(2)}) %collective-permute-start.27) | collective-permute-done | bytes 368672 | tf_op jit(solution)/shard_map/ppermute | solution.py:29
  364.6 6.3 shard_map.155
  370.9 6.4 shard_map.156
  377.2 13.4 %all-to-all-done.2 = bf16[4,288,1440]{2,1,0:T(8,128)(2,1)} async-done(((bf16[4,288,1440]{2,1,0:T(8,128)(2,1)}), bf16[4,288,1440]{2,1,0:T(8,128)(2,1)}, u32[]{:S(2)}, u32[]{:S(2)}) %all-to-all-start.2) | async-done | bytes 3317792 | tf_op jit(solution)/shard_map/all_to_all | solution.py:162
  392.1 4.9 all-to-all-start.3
  415.3 4.5 collective-permute-start.33
  421.6 5.1 collective-permute-done.33
  426.7 10.1 %all-to-all-done.3 = bf16[4,288,1440]{2,1,0:T(8,128)(2,1)} async-done(((bf16[4,288,1440]{2,1,0:T(8,128)(2,1)}), bf16[4,288,1440]{2,1,0:T(8,128)(2,1)}, u32[]{:S(2)}, u32[]{:S(2)}) %all-to-all-start.3) | async-done | bytes 3317792 | tf_op jit(solution)/shard_map/all_to_all | solution.py:162
  449.8 4.9 all-to-all-start.4
  460.3 23.0 %shard_map.157 = (f32[320,1152]{1,0:T(8,128)}, bf16[4,4,80,1152]{3,2,1,0:T(8,128)(2,1)}, bf16[4,4,80,1152]{3,2,1,0:T(8,128)(2,1)}) custom-call(s32[1]{0:T(128)} %bitcast.row_ref, s32[320,4]{1,0:T(8,128)} %copy.144.query_ref, s32[4,2,640]{2,1,0:T(2,128)} %pad_add_fusion.key_ref, bf16[320,1152]{1,0:T(8,128)(2,1)} %copy.145.q_ref, ...), custom_call_target="tpu_custom_call" | custom-call | flops 117964800000 | bytes 11796480 | tf_op jit(solution)/shard_map/pallas_call | solution.py:383
  483.3 11.2 %all-to-all-done.4 = bf16[4,288,1440]{2,1,0:T(8,128)(2,1)} async-done(((bf16[4,288,1440]{2,1,0:T(8,128)(2,1)}), bf16[4,288,1440]{2,1,0:T(8,128)(2,1)}, u32[]{:S(2)}, u32[]{:S(2)}) %all-to-all-start.4) | async-done | bytes 3317792 | tf_op jit(solution)/shard_map/all_to_all | solution.py:162
  508.8 4.2 add_convert_fusion
  513.0 4.6 all-to-all-start.5
  536.4 5.2 collective-permute-start.42
  552.6 15.9 %all-to-all-done.5 = bf16[4,320,1152]{2,1,0:T(8,128)(2,1)} async-done(((bf16[4,320,1152]{2,1,0:T(8,128)(2,1)}), bf16[4,320,1152]{2,1,0:T(8,128)(2,1)}, u32[]{:S(2)}, u32[]{:S(2)}) %all-to-all-start.5) | async-done | bytes 2949152 | tf_op jit(solution)/shard_map/all_to_all | solution.py:162
  575.4 5.0 fusion.52
  581.8 5.5 collective-permute-done.42
  588.6 12.8 %all-to-all-start.6 = ((bf16[4,288,1152]{2,1,0:T(8,128)(2,1)}), bf16[4,288,1152]{2,1,0:T(8,128)(2,1)}, u32[]{:S(2)}, u32[]{:S(2)}) async-start(bf16[4,288,1152]{2,1,0:T(8,128)(2,1)} %pad_maximum_fusion.1), calls=%async_computation.6 | async-start | bytes 5308416 | tf_op jit(solution)/shard_map/all_to_all | solution.py:162
  609.2 4.8 collective-permute-done.45
  617.3 4.6 shard_map.160
  627.0 6.7 collective-permute-done.46
  653.0 22.4 %collective-permute-done.54 = f32[2,2304]{1,0:T(2,128)S(1)} collective-permute-done((f32[2,2304]{1,0:T(2,128)S(1)}, f32[2,2304]{1,0:T(2,128)S(1)}, u32[]{:S(2)}, u32[]{:S(2)}) %collective-permute-start.54) | collective-permute-done | bytes 18464 | tf_op jit(solution)/shard_map/ppermute | solution.py:610
  683.3 4.0 all-to-all-done.7
  690.1 8.2 %collective-permute-start.51 = (bf16[288,1024]{1,0:T(8,128)(2,1)}, bf16[288,1024]{1,0:T(8,128)(2,1)}, u32[]{:S(2)}, u32[]{:S(2)}) collective-permute-start(bf16[288,1024]{1,0:T(8,128)(2,1)} %pad_maximum_fusion.18), channel_id=1, source_target_pairs={{16,0},{24,1},{0,2},{8,3},{18,8},{26,9},{2,10},{10,11},{17,16},{25... | collective-permute-start | bytes 1769480 | tf_op jit(solution)/shard_map/ppermute | solution.py:96
  708.6 29.2 %collective-permute-done.50 = bf16[288,1280]{1,0:T(8,128)(2,1)S(1)} collective-permute-done((bf16[288,1280]{1,0:T(8,128)(2,1)S(1)}, bf16[288,1280]{1,0:T(8,128)(2,1)S(1)}, u32[]{:S(2)}, u32[]{:S(2)}) %collective-permute-start.50) | collective-permute-done | bytes 737312 | tf_op jit(solution)/shard_map/ppermute | solution.py:96
  (476 shorter events, 278.8 us)
Async XLA Ops:
  7.2 86.3 %all-gather.6.cloned.1.call-start = ((), (), s32[]{:S(2)}) async-start(), calls=%async_computation.8 | async-start | bytes 5971968 | tf_op jit(solution)/shard_map/all_gather | solution.py:114
  9.2 27.2 %collective-permute-start.4 = (bf16[288,640]{0,1:T(8,128)(2,1)S(1)}, bf16[288,640]{0,1:T(8,128)(2,1)S(1)}, u32[]{:S(2)}, u32[]{:S(2)}) collective-permute-start(bf16[288,640]{0,1:T(8,128)(2,1)S(1)} %slice.450), channel_id=1, source_target_pairs={{0,0},{1,8},{2,16},{3,24},{8,2},{9,10},{10,18},{11,26},{16,1},{17,... | collective-permute-start | bytes 1105928 | tf_op jit(solution)/shard_map/ppermute | solution.py:96
  13.9 21.2 %collective-permute-start.5 = (bf16[288,512]{0,1:T(8,128)(2,1)S(1)}, bf16[288,512]{0,1:T(8,128)(2,1)S(1)}, u32[]{:S(2)}, u32[]{:S(2)}) collective-permute-start(bf16[288,512]{0,1:T(8,128)(2,1)S(1)} %slice.451), channel_id=1, source_target_pairs={{0,16},{1,24},{2,0},{3,8},{8,18},{9,26},{10,2},{11,10},{16,17},{17... | collective-permute-start | bytes 884744 | tf_op jit(solution)/shard_map/ppermute | solution.py:96
  37.7 98.3 %all-gather.8.cloned.1.call-start = ((), (), s32[]{:S(2)}) async-start(), calls=%async_computation.9 | async-start | bytes 3317760 | tf_op jit(solution)/shard_map/all_gather | solution.py:114
  39.3 31.1 %collective-permute-start = (bf16[81,2304]{1,0:T(8,128)(2,1)}, bf16[81,2304]{1,0:T(8,128)(2,1)}, u32[]{:S(2)}, u32[]{:S(2)}) collective-permute-start(bf16[81,2304]{1,0:T(8,128)(2,1)} %constant_dynamic-update-slice_fusion), channel_id=1, source_target_pairs={{0,8},{8,0},{16,24},{24,16},{1,9},{9,1},{17,25},{25,17},{2,10},{10... | collective-permute-start | bytes 1119752 | tf_op jit(solution)/shard_map/ppermute | solution.py:29
  39.4 25.7 %collective-permute-start.1 = (bf16[81,2304]{1,0:T(8,128)(2,1)}, bf16[81,2304]{1,0:T(8,128)(2,1)}, u32[]{:S(2)}, u32[]{:S(2)}) collective-permute-start(bf16[81,2304]{1,0:T(8,128)(2,1)} %constant_dynamic-update-slice_fusion), channel_id=1, source_target_pairs={{0,16},{8,24},{16,0},{24,8},{1,17},{9,25},{17,1},{25,9},{2,18},{10... | collective-permute-start | bytes 1119752 | tf_op jit(solution)/shard_map/ppermute | solution.py:29
  40.1 28.1 %collective-permute-start.9 = (bf16[288,256]{1,0:T(8,128)(2,1)}, bf16[288,256]{1,0:T(8,128)(2,1)}, u32[]{:S(2)}, u32[]{:S(2)}) collective-permute-start(bf16[288,256]{1,0:T(8,128)(2,1)} %slice.460), channel_id=1, source_target_pairs={{0,16},{1,24},{2,0},{3,8},{8,18},{9,26},{10,2},{11,10},{16,17},{17... | collective-permute-start | bytes 442376 | tf_op jit(solution)/shard_map/ppermute | solution.py:96
  42.1 26.3 %collective-permute-start.8 = (bf16[288,320]{1,0:T(8,128)(2,1)}, bf16[288,320]{1,0:T(8,128)(2,1)}, u32[]{:S(2)}, u32[]{:S(2)}) collective-permute-start(bf16[288,320]{1,0:T(8,128)(2,1)} %slice.459), channel_id=1, source_target_pairs={{0,0},{1,8},{2,16},{3,24},{8,2},{9,10},{10,18},{11,26},{16,1},{17,... | collective-permute-start | bytes 552968 | tf_op jit(solution)/shard_map/ppermute | solution.py:96
  70.4 162.8 %all-gather.10.cloned.1.call-start = ((), (), s32[]{:S(2)}) async-start(), calls=%async_computation.10 | async-start | bytes 3317760 | tf_op jit(solution)/shard_map/all_gather | solution.py:114
  83.1 32.4 %collective-permute-start.14 = (bf16[288,1088]{1,0:T(8,128)(2,1)}, bf16[288,1088]{1,0:T(8,128)(2,1)}, u32[]{:S(2)}, u32[]{:S(2)}) collective-permute-start(bf16[288,1088]{1,0:T(8,128)(2,1)} %pad_maximum_fusion.16), channel_id=1, source_target_pairs={{0,0},{1,8},{2,16},{3,24},{8,2},{9,10},{10,18},{11,26},{16,1},{17,... | collective-permute-start | bytes 1880072 | tf_op jit(solution)/shard_map/ppermute | solution.py:96
  85.0 30.5 %collective-permute-start.15 = (bf16[288,928]{1,0:T(8,128)(2,1)}, bf16[288,928]{1,0:T(8,128)(2,1)}, u32[]{:S(2)}, u32[]{:S(2)}) collective-permute-start(bf16[288,928]{1,0:T(8,128)(2,1)} %pad_maximum_fusion.17), channel_id=1, source_target_pairs={{0,16},{1,24},{2,0},{3,8},{8,18},{9,26},{10,2},{11,10},{16,17},{17... | collective-permute-start | bytes 1603592 | tf_op jit(solution)/shard_map/ppermute | solution.py:96
  118.4 198.1 %all-gather.14.cloned.1.call-start = ((), (), s32[]{:S(2)}) async-start(), calls=%async_computation.12 | async-start | bytes 7962624 | tf_op jit(solution)/shard_map/all_gather | solution.py:114
  124.2 69.7 %all-to-all-start = ((bf16[4,320,1152]{2,1,0:T(8,128)(2,1)}), bf16[4,320,1152]{2,1,0:T(8,128)(2,1)}, u32[]{:S(2)}, u32[]{:S(2)}) async-start(bf16[4,320,1152]{2,1,0:T(8,128)(2,1)} %broadcast_in_dim.30), calls=%async_computation | async-start | bytes 5898240 | tf_op jit(solution)/shard_map/all_to_all | solution.py:162
  128.8 65.1 %collective-permute-start.6 = (bf16[288,1536]{1,0:T(8,128)(2,1)}, bf16[288,1536]{1,0:T(8,128)(2,1)}, u32[]{:S(2)}, u32[]{:S(2)}) collective-permute-start(bf16[288,1536]{1,0:T(8,128)(2,1)} %pad_maximum_fusion.4), channel_id=1, source_target_pairs={{0,0},{1,8},{2,16},{3,24},{8,2},{9,10},{10,18},{11,26},{16,1},{17,... | collective-permute-start | bytes 2654216 | tf_op jit(solution)/shard_map/ppermute | solution.py:96
  130.9 55.2 %collective-permute-start.10 = (bf16[80,2304]{1,0:T(8,128)(2,1)S(1)}, bf16[80,2304]{1,0:T(8,128)(2,1)}, u32[]{:S(2)}, u32[]{:S(2)}) collective-permute-start(bf16[80,2304]{1,0:T(8,128)(2,1)S(1)} %fusion.9), channel_id=1, source_target_pairs={{0,8},{8,0},{16,24},{24,16},{1,9},{9,1},{17,25},{25,17},{2,10},{10... | collective-permute-start | bytes 1105928 | tf_op jit(solution)/shard_map/ppermute | solution.py:29
  131.5 54.2 %collective-permute-start.11 = (bf16[80,2304]{1,0:T(8,128)(2,1)S(1)}, bf16[80,2304]{1,0:T(8,128)(2,1)}, u32[]{:S(2)}, u32[]{:S(2)}) collective-permute-start(bf16[80,2304]{1,0:T(8,128)(2,1)S(1)} %fusion.9), channel_id=1, source_target_pairs={{0,16},{8,24},{16,0},{24,8},{1,17},{9,25},{17,1},{25,9},{2,18},{10... | collective-permute-start | bytes 1105928 | tf_op jit(solution)/shard_map/ppermute | solution.py:29
  134.5 59.3 %collective-permute-start.7 = (bf16[288,1344]{1,0:T(8,128)(2,1)}, bf16[288,1344]{1,0:T(8,128)(2,1)S(1)}, u32[]{:S(2)}, u32[]{:S(2)}) collective-permute-start(bf16[288,1344]{1,0:T(8,128)(2,1)} %pad_maximum_fusion.14), channel_id=1, source_target_pairs={{0,16},{1,24},{2,0},{3,8},{8,18},{9,26},{10,2},{11,10},{16,17},{17... | collective-permute-start | bytes 2322440 | tf_op jit(solution)/shard_map/ppermute | solution.py:96
  204.3 55.5 %all-to-all-start.1 = ((bf16[4,288,1440]{2,1,0:T(8,128)(2,1)}), bf16[4,288,1440]{2,1,0:T(8,128)(2,1)S(1)}, u32[]{:S(2)}, u32[]{:S(2)}) async-start(bf16[4,288,1440]{2,1,0:T(8,128)(2,1)} %broadcast_in_dim.31), calls=%async_computation.1 | async-start | bytes 7077888 | tf_op jit(solution)/shard_map/all_to_all | solution.py:162
  208.1 115.4 %all-gather.12.cloned.1.call-start = ((), (), s32[]{:S(2)}) async-start(), calls=%async_computation.11 | async-start | bytes 7962624 | tf_op jit(solution)/shard_map/all_gather | solution.py:114
  239.8 21.1 %collective-permute-start.16 = (bf16[80,2304]{1,0:T(8,128)(2,1)}, bf16[80,2304]{1,0:T(8,128)(2,1)}, u32[]{:S(2)}, u32[]{:S(2)}) collective-permute-start(bf16[80,2304]{1,0:T(8,128)(2,1)} %get-tuple-element.253), channel_id=1, source_target_pairs={{0,8},{8,0},{16,24},{24,16},{1,9},{9,1},{17,25},{25,17},{2,10},{10... | collective-permute-start | bytes 1105928 | tf_op jit(solution)/shard_map/ppermute | solution.py:29
  252.1 18.1 %collective-permute-start.18 = (bf16[80,2304]{1,0:T(8,128)(2,1)}, bf16[80,2304]{1,0:T(8,128)(2,1)}, u32[]{:S(2)}, u32[]{:S(2)}) collective-permute-start(bf16[80,2304]{1,0:T(8,128)(2,1)} %get-tuple-element.234), channel_id=1, source_target_pairs={{0,16},{8,24},{16,0},{24,8},{1,17},{9,25},{17,1},{25,9},{2,18},{10... | collective-permute-start | bytes 1105928 | tf_op jit(solution)/shard_map/ppermute | solution.py:29
  274.3 36.3 %collective-permute-start.19 = (bf16[1152,1440]{0,1:T(8,128)(2,1)}, bf16[1152,1440]{0,1:T(8,128)(2,1)S(1)}, u32[]{:S(2)}, u32[]{:S(2)}) collective-permute-start(bf16[1152,1440]{0,1:T(8,128)(2,1)} %copy.147), channel_id=1, source_target_pairs={{0,1},{1,0},{2,3},{3,2},{4,5},{5,4},{6,7},{7,6},{8,9},{9,8},{10,11... | collective-permute-start | bytes 9953288 | tf_op jit(solution)/shard_map/ppermute | solution.py:33
  279.0 19.2 %collective-permute-start.21 = (bf16[80,2304]{1,0:T(8,128)(2,1)S(1)}, bf16[80,2304]{1,0:T(8,128)(2,1)S(1)}, u32[]{:S(2)}, u32[]{:S(2)}) collective-permute-start(bf16[80,2304]{1,0:T(8,128)(2,1)S(1)} %multiply_convert_fusion.4), channel_id=1, source_target_pairs={{0,16},{8,24},{16,0},{24,8},{1,17},{9,25},{17,1},{25,9},{2,18},{10... | collective-permute-start | bytes 1105928 | tf_op jit(solution)/shard_map/ppermute | solution.py:29
  281.7 19.7 %collective-permute-start.20 = (bf16[80,2304]{1,0:T(8,128)(2,1)S(1)}, bf16[80,2304]{1,0:T(8,128)(2,1)S(1)}, u32[]{:S(2)}, u32[]{:S(2)}) collective-permute-start(bf16[80,2304]{1,0:T(8,128)(2,1)S(1)} %multiply_convert_fusion.4), channel_id=1, source_target_pairs={{0,8},{8,0},{16,24},{24,16},{1,9},{9,1},{17,25},{25,17},{2,10},{10... | collective-permute-start | bytes 1105928 | tf_op jit(solution)/shard_map/ppermute | solution.py:29
  300.7 38.0 %collective-permute-start.23 = (bf16[320,1152]{1,0:T(8,128)(2,1)}, bf16[320,1152]{1,0:T(8,128)(2,1)}, u32[]{:S(2)}, u32[]{:S(2)}) collective-permute-start(bf16[320,1152]{1,0:T(8,128)(2,1)} %get-tuple-element.251), channel_id=1, source_target_pairs={{0,1},{1,0},{2,3},{3,2},{4,5},{5,4},{6,7},{7,6},{8,9},{9,8},{10,11... | collective-permute-start | bytes 2211848 | tf_op jit(solution)/shard_map/ppermute | solution.py:33
  309.3 35.7 %collective-permute-start.25 = (bf16[320,1152]{1,0:T(8,128)(2,1)}, bf16[320,1152]{1,0:T(8,128)(2,1)}, u32[]{:S(2)}, u32[]{:S(2)}) collective-permute-start(bf16[320,1152]{1,0:T(8,128)(2,1)} %get-tuple-element.248), channel_id=1, source_target_pairs={{0,1},{1,0},{2,3},{3,2},{4,5},{5,4},{6,7},{7,6},{8,9},{9,8},{10,11... | collective-permute-start | bytes 2211848 | tf_op jit(solution)/shard_map/ppermute | solution.py:33
  345.1 45.5 %all-to-all-start.2 = ((bf16[4,288,1440]{2,1,0:T(8,128)(2,1)}), bf16[4,288,1440]{2,1,0:T(8,128)(2,1)}, u32[]{:S(2)}, u32[]{:S(2)}) async-start(bf16[4,288,1440]{2,1,0:T(8,128)(2,1)} %bitcast.30), calls=%async_computation.2 | async-start | bytes 7077888 | tf_op jit(solution)/shard_map/all_to_all | solution.py:162
  354.0 23.3 %collective-permute-start.26 = (bf16[80,2304]{1,0:T(8,128)(2,1)S(1)}, bf16[80,2304]{1,0:T(8,128)(2,1)}, u32[]{:S(2)}, u32[]{:S(2)}) collective-permute-start(bf16[80,2304]{1,0:T(8,128)(2,1)S(1)} %get-tuple-element.247), channel_id=1, source_target_pairs={{0,8},{8,0},{16,24},{24,16},{1,9},{9,1},{17,25},{25,17},{2,10},{10... | collective-permute-start | bytes 1105928 | tf_op jit(solution)/shard_map/ppermute | solution.py:29
  354.2 16.6 %collective-permute-start.30 = (bf16[320,1440]{1,0:T(8,128)(2,1)S(1)}, bf16[320,1440]{1,0:T(8,128)(2,1)S(1)}, u32[]{:S(2)}, u32[]{:S(2)}) collective-permute-start(bf16[320,1440]{1,0:T(8,128)(2,1)S(1)} %get-tuple-element.132.right_ref), channel_id=1, source_target_pairs={{0,1},{1,0},{2,3},{3,2},{4,5},{5,4},{6,7},{7,6},{8,9},{9,8},{10,11... | collective-permute-start | bytes 2764808 | tf_op jit(solution)/shard_map/ppermute | solution.py:33
  392.1 44.7 %all-to-all-start.3 = ((bf16[4,288,1440]{2,1,0:T(8,128)(2,1)}), bf16[4,288,1440]{2,1,0:T(8,128)(2,1)}, u32[]{:S(2)}, u32[]{:S(2)}) async-start(bf16[4,288,1440]{2,1,0:T(8,128)(2,1)} %bitcast.31), calls=%async_computation.3 | async-start | bytes 7077888 | tf_op jit(solution)/shard_map/all_to_all | solution.py:162
  399.4 22.2 %collective-permute-start.31 = (bf16[80,2304]{1,0:T(8,128)(2,1)}, bf16[80,2304]{1,0:T(8,128)(2,1)}, u32[]{:S(2)}, u32[]{:S(2)}) collective-permute-start(bf16[80,2304]{1,0:T(8,128)(2,1)} %get-tuple-element.143), channel_id=1, source_target_pairs={{0,8},{8,0},{16,24},{24,16},{1,9},{9,1},{17,25},{25,17},{2,10},{10... | collective-permute-start | bytes 1105928 | tf_op jit(solution)/shard_map/ppermute | solution.py:29
  406.5 20.2 %collective-permute-start.34 = (bf16[320,1152]{1,0:T(8,128)(2,1)S(1)}, bf16[320,1152]{1,0:T(8,128)(2,1)S(1)}, u32[]{:S(2)}, u32[]{:S(2)}) collective-permute-start(bf16[320,1152]{1,0:T(8,128)(2,1)S(1)} %get-tuple-element.244), channel_id=1, source_target_pairs={{0,1},{1,0},{2,3},{3,2},{4,5},{5,4},{6,7},{7,6},{8,9},{9,8},{10,11... | collective-permute-start | bytes 2211848 | tf_op jit(solution)/shard_map/ppermute | solution.py:33
  449.8 44.8 %all-to-all-start.4 = ((bf16[4,288,1440]{2,1,0:T(8,128)(2,1)}), bf16[4,288,1440]{2,1,0:T(8,128)(2,1)}, u32[]{:S(2)}, u32[]{:S(2)}) async-start(bf16[4,288,1440]{2,1,0:T(8,128)(2,1)} %bitcast.32), calls=%async_computation.4 | async-start | bytes 7077888 | tf_op jit(solution)/shard_map/all_to_all | solution.py:162
  454.7 28.6 %collective-permute-start.35 = (bf16[80,2304]{1,0:T(8,128)(2,1)}, bf16[80,2304]{1,0:T(8,128)(2,1)S(1)}, u32[]{:S(2)}, u32[]{:S(2)}) collective-permute-start(bf16[80,2304]{1,0:T(8,128)(2,1)} %get-tuple-element.243), channel_id=1, source_target_pairs={{0,8},{8,0},{16,24},{24,16},{1,9},{9,1},{17,25},{25,17},{2,10},{10... | collective-permute-start | bytes 1105928 | tf_op jit(solution)/shard_map/ppermute | solution.py:29
  457.6 25.7 %collective-permute-start.37 = (bf16[80,2304]{1,0:T(8,128)(2,1)S(1)}, bf16[80,2304]{1,0:T(8,128)(2,1)S(1)}, u32[]{:S(2)}, u32[]{:S(2)}) collective-permute-start(bf16[80,2304]{1,0:T(8,128)(2,1)S(1)} %get-tuple-element.230), channel_id=1, source_target_pairs={{0,16},{8,24},{16,0},{24,8},{1,17},{9,25},{17,1},{25,9},{2,18},{10... | collective-permute-start | bytes 1105928 | tf_op jit(solution)/shard_map/ppermute | solution.py:29
  503.2 43.5 %collective-permute-start.41 = (bf16[320,576]{1,0:T(8,128)(2,1)S(1)}, bf16[320,576]{1,0:T(8,128)(2,1)S(1)}, u32[]{:S(2)}, u32[]{:S(2)}) collective-permute-start(bf16[320,576]{1,0:T(8,128)(2,1)S(1)} %copy.157.right_ref), channel_id=1, source_target_pairs={{0,1},{1,0},{2,3},{3,2},{4,5},{5,4},{6,7},{7,6},{8,9},{9,8},{10,11... | collective-permute-start | bytes 1105928 | tf_op jit(solution)/shard_map/ppermute | solution.py:33
  513.0 55.5 %all-to-all-start.5 = ((bf16[4,320,1152]{2,1,0:T(8,128)(2,1)}), bf16[4,320,1152]{2,1,0:T(8,128)(2,1)}, u32[]{:S(2)}, u32[]{:S(2)}) async-start(bf16[4,320,1152]{2,1,0:T(8,128)(2,1)} %bitcast.146), calls=%async_computation.5 | async-start | bytes 5898240 | tf_op jit(solution)/shard_map/all_to_all | solution.py:162
  520.0 26.8 %collective-permute-start.40 = (bf16[320,1152]{1,0:T(8,128)(2,1)}, bf16[320,1152]{1,0:T(8,128)(2,1)}, u32[]{:S(2)}, u32[]{:S(2)}) collective-permute-start(bf16[320,1152]{1,0:T(8,128)(2,1)} %get-tuple-element.240), channel_id=1, source_target_pairs={{0,1},{1,0},{2,3},{3,2},{4,5},{5,4},{6,7},{7,6},{8,9},{9,8},{10,11... | collective-permute-start | bytes 2211848 | tf_op jit(solution)/shard_map/ppermute | solution.py:33
  536.4 51.0 %collective-permute-start.42 = (bf16[288,1536]{1,0:T(8,128)(2,1)}, bf16[288,1536]{1,0:T(8,128)(2,1)}, u32[]{:S(2)}, u32[]{:S(2)}) collective-permute-start(bf16[288,1536]{1,0:T(8,128)(2,1)} %pad_maximum_fusion.11), channel_id=1, source_target_pairs={{0,0},{8,1},{16,2},{24,3},{2,8},{10,9},{18,10},{26,11},{1,16},{9,1... | collective-permute-start | bytes 2654216 | tf_op jit(solution)/shard_map/ppermute | solution.py:96
  541.6 40.2 %collective-permute-start.43 = (bf16[288,1344]{1,0:T(8,128)(2,1)}, bf16[288,1344]{1,0:T(8,128)(2,1)}, u32[]{:S(2)}, u32[]{:S(2)}) collective-permute-start(bf16[288,1344]{1,0:T(8,128)(2,1)} %pad_maximum_fusion.15), channel_id=1, source_target_pairs={{16,0},{24,1},{0,2},{8,3},{18,8},{26,9},{2,10},{10,11},{17,16},{25... | collective-permute-start | bytes 2322440 | tf_op jit(solution)/shard_map/ppermute | solution.py:96
  588.6 35.2 %all-to-all-start.6 = ((bf16[4,288,1152]{2,1,0:T(8,128)(2,1)}), bf16[4,288,1152]{2,1,0:T(8,128)(2,1)}, u32[]{:S(2)}, u32[]{:S(2)}) async-start(bf16[4,288,1152]{2,1,0:T(8,128)(2,1)} %pad_maximum_fusion.1), calls=%async_computation.6 | async-start | bytes 5308416 | tf_op jit(solution)/shard_map/all_to_all | solution.py:162
  603.3 23.7 %collective-permute-start.44 = (bf16[80,2304]{1,0:T(8,128)(2,1)}, bf16[80,2304]{1,0:T(8,128)(2,1)}, u32[]{:S(2)}, u32[]{:S(2)}) collective-permute-start(bf16[80,2304]{1,0:T(8,128)(2,1)} %get-tuple-element.239), channel_id=1, source_target_pairs={{0,8},{8,0},{16,24},{24,16},{1,9},{9,1},{17,25},{25,17},{2,10},{10... | collective-permute-start | bytes 1105928 | tf_op jit(solution)/shard_map/ppermute | solution.py:29
  615.9 17.9 %collective-permute-start.46 = (bf16[80,2304]{1,0:T(8,128)(2,1)}, bf16[80,2304]{1,0:T(8,128)(2,1)}, u32[]{:S(2)}, u32[]{:S(2)}) collective-permute-start(bf16[80,2304]{1,0:T(8,128)(2,1)} %get-tuple-element.228), channel_id=1, source_target_pairs={{0,16},{8,24},{16,0},{24,8},{1,17},{9,25},{17,1},{25,9},{2,18},{10... | collective-permute-start | bytes 1105928 | tf_op jit(solution)/shard_map/ppermute | solution.py:29
  640.7 46.6 %all-to-all-start.7 = ((bf16[4,288,1152]{2,1,0:T(8,128)(2,1)}), bf16[4,288,1152]{2,1,0:T(8,128)(2,1)S(1)}, u32[]{:S(2)}, u32[]{:S(2)}) async-start(bf16[4,288,1152]{2,1,0:T(8,128)(2,1)} %bitcast.45), calls=%async_computation.7 | async-start | bytes 5308416 | tf_op jit(solution)/shard_map/all_to_all | solution.py:162
  644.4 38.9 %collective-permute-start.48 = (bf16[288,768]{1,0:T(8,128)(2,1)}, bf16[288,768]{1,0:T(8,128)(2,1)}, u32[]{:S(2)}, u32[]{:S(2)}) collective-permute-start(bf16[288,768]{1,0:T(8,128)(2,1)} %slice.488), channel_id=1, source_target_pairs={{0,0},{8,1},{16,2},{24,3},{2,8},{10,9},{18,10},{26,11},{1,16},{9,1... | collective-permute-start | bytes 1327112 | tf_op jit(solution)/shard_map/ppermute | solution.py:96
  647.4 35.1 %collective-permute-start.49 = (bf16[288,672]{1,0:T(8,128)(2,1)}, bf16[288,672]{1,0:T(8,128)(2,1)S(1)}, u32[]{:S(2)}, u32[]{:S(2)}) collective-permute-start(bf16[288,672]{1,0:T(8,128)(2,1)} %slice.489), channel_id=1, source_target_pairs={{16,0},{24,1},{0,2},{8,3},{18,8},{26,9},{2,10},{10,11},{17,16},{25... | collective-permute-start | bytes 1161224 | tf_op jit(solution)/shard_map/ppermute | solution.py:96
  649.2 26.2 %collective-permute-start.54 = (f32[2,2304]{1,0:T(2,128)S(1)}, f32[2,2304]{1,0:T(2,128)S(1)}, u32[]{:S(2)}, u32[]{:S(2)}) collective-permute-start(f32[2,2304]{1,0:T(2,128)S(1)} %fusion.79), channel_id=1, source_target_pairs={{0,4},{4,0},{1,5},{5,1},{2,6},{6,2},{3,7},{7,3},{8,12},{12,8},{9,1... | collective-permute-start | bytes 55304 | tf_op jit(solution)/shard_map/ppermute | solution.py:610
  698.7 39.1 %collective-permute-start.50 = (bf16[288,1280]{1,0:T(8,128)(2,1)S(1)}, bf16[288,1280]{1,0:T(8,128)(2,1)S(1)}, u32[]{:S(2)}, u32[]{:S(2)}) collective-permute-start(bf16[288,1280]{1,0:T(8,128)(2,1)S(1)} %concatenate.148), channel_id=1, source_target_pairs={{0,0},{8,1},{16,2},{24,3},{2,8},{10,9},{18,10},{26,11},{1,16},{9,1... | collective-permute-start | bytes 2211848 | tf_op jit(solution)/shard_map/ppermute | solution.py:96
  (88 other events, 1184.1 us)
Sparse Core Ops, SparseCore 0:
  37.8 46.0 all-gather.5
  85.8 38.1 all-gather.7
  125.9 54.7 all-gather.9
  182.5 90.4 all-gather.13
  274.6 48.8 all-gather.11

commit v6 on v5

--- a/solution.py
+++ b/solution.py
@@ -136,7 +136,7 @@
     chips = lax.axis_size("pb") * lax.axis_size("tx")
     tokens, rows = left[0].shape
     wide = right.shape[1]
-    tile = 384 if rows % 384 == 0 else rows
+    tile = 128 if rows % 128 == 0 else rows
     lefts = pl.BlockSpec((tokens, tile), lambda i: (0, i))
     rights = pl.BlockSpec((tokens, wide), lambda i: (0, 0))
     total = pl.pallas_call(

time: 763 us -> 766 us (level)
  Pallas kernels: 70.2 us -> 84 us
  waiting for transfers between devices: 297 us -> 285 us
    pallas_call x6, Pallas kernels: 30.7 us -> 44.6 us  [pair_sum(): pl.pallas_call(pair_kernel, grid=(rows // tile,), in_specs=[lefts, lefts,...]
    all_to_all x8, waiting for transfers between devices: 60.2 us -> 48.8 us  [exchange(): return lax.all_to_all(blocks, CHIPS, 0, 0, tiled=True)]
  transfers between devices with their start and end apart: 70 -> 70, of which waited for: 33 -> 33; matrix products, arithmetic and copies ran while one was open for 27% -> 27% of each run, Pallas kernels for 9% -> 11%
where the time goes in v6:
time: 766 us; the launch traced here: 752 us
  waiting for transfers between devices  285 us (37%)
  starting transfers between devices  138 us (18%)
  other arithmetic  88.9 us (12%)
  local copies, waits for them, and re-layouts  86 us (11%)
  Pallas kernels  84 us (11%)
  matrix products  54 us (7%)
  between operations  16 us (2%)
    ppermute x24, waiting for transfers between devices, send_row(): lax.ppermute(array, ROW, [(i, i ^ distance) for i in range(lax.axis_size(...  137 us
    ppermute x14, waiting for transfers between devices, move(): return lax.ppermute(part, (ROW, 'tx', 'tc'), pairs)  72 us
    dot_general x14, matrix products, dot(): return lax.dot_general(a, b, (dims, ((), ())), preferred_element_type=f32)  54 us
    all_to_all x8, waiting for transfers between devices, exchange(): return lax.all_to_all(blocks, CHIPS, 0, 0, tiled=True)  48.8 us
    ppermute x14, starting transfers between devices, move(): return lax.ppermute(part, (ROW, 'tx', 'tc'), pairs)  46.9 us
    pallas_call x6, Pallas kernels, pair_sum(): pl.pallas_call(pair_kernel, grid=(rows // tile,), in_specs=[lefts, lefts,...  44.6 us
    all_to_all x8, starting transfers between devices, exchange(): return lax.all_to_all(blocks, CHIPS, 0, 0, tiled=True)  44.1 us
    ppermute x24, starting transfers between devices, send_row(): lax.ppermute(array, ROW, [(i, i ^ distance) for i in range(lax.axis_size(...  27.4 us
  transfers between devices with their start and end apart: 70, of which 33 were waited for; matrix products, arithmetic and copies ran while one was open for 27% of the time, Pallas kernels for 11%

profile of v6, /device:TPU:1, one launch (start us, length us, event | category | flops | bytes accessed | tf_op | source)
XLA Modules:
  0.0 752.3 jit_solution(4123635999316019790)
XLA Ops:
  9.2 4.6 collective-permute-start.4
  16.6 18.5 %collective-permute-done.5 = bf16[288,512]{0,1:T(8,128)(2,1)S(1)} collective-permute-done((bf16[288,512]{0,1:T(8,128)(2,1)S(1)}, bf16[288,512]{0,1:T(8,128)(2,1)S(1)}, u32[]{:S(2)}, u32[]{:S(2)}) %collective-permute-start.5) | collective-permute-done | bytes 294944 | tf_op jit(solution)/shard_map/ppermute | solution.py:96
  42.1 6.6 collective-permute-start.8
  53.3 11.8 %collective-permute-done.1 = bf16[81,2304]{1,0:T(8,128)(2,1)} collective-permute-done((bf16[81,2304]{1,0:T(8,128)(2,1)}, bf16[81,2304]{1,0:T(8,128)(2,1)}, u32[]{:S(2)}, u32[]{:S(2)}) %collective-permute-start.1) | collective-permute-done | bytes 373280 | tf_op jit(solution)/shard_map/ppermute | solution.py:29
  70.4 5.4 collective-permute-done.2
  93.5 6.0 fusion.46
  99.9 15.6 %collective-permute-done.15 = bf16[288,928]{1,0:T(8,128)(2,1)} collective-permute-done((bf16[288,928]{1,0:T(8,128)(2,1)}, bf16[288,928]{1,0:T(8,128)(2,1)}, u32[]{:S(2)}, u32[]{:S(2)}) %collective-permute-start.15) | collective-permute-done | bytes 534560 | tf_op jit(solution)/shard_map/ppermute | solution.py:96
  124.2 4.6 all-to-all-start
  139.4 46.3 %collective-permute-done.11 = bf16[80,2304]{1,0:T(8,128)(2,1)} collective-permute-done((bf16[80,2304]{1,0:T(8,128)(2,1)S(1)}, bf16[80,2304]{1,0:T(8,128)(2,1)}, u32[]{:S(2)}, u32[]{:S(2)}) %collective-permute-start.11) | collective-permute-done | bytes 368672 | tf_op jit(solution)/shard_map/ppermute | solution.py:29
  186.1 7.8 %collective-permute-done.12 = bf16[80,2304]{1,0:T(8,128)(2,1)S(1)} collective-permute-done((bf16[80,2304]{1,0:T(8,128)(2,1)}, bf16[80,2304]{1,0:T(8,128)(2,1)S(1)}, u32[]{:S(2)}, u32[]{:S(2)}) %collective-permute-start.12) | collective-permute-done | bytes 368672 | tf_op jit(solution)/shard_map/ppermute | solution.py:29
  210.4 16.5 %shard_map.153.out_ref = f32[320,1152]{1,0:T(8,128)} custom-call(s32[1]{0:T(128)} %bitcast.row_ref, s32[320,4]{1,0:T(8,128)} %copy.144.query_ref, s32[4,2,640]{2,1,0:T(2,128)} %pad_add_fusion.key_ref, bf16[320,1152]{1,0:T(8,128)(2,1)} %copy.145.q_ref, bf16[4,4,80,1152]{3,2,1,0:T(8,128)(2,1)} %bitcast.25.near_ref, bf16[4,4,80,1152]{3,2,1,0:T(8,128)(2,1)} %bitcast.26.far_ref), custom_call_target="tpu_custom_call" | custom-call | flops 47185920000 | bytes 11796480 | tf_op jit(solution)/shard_map/pallas_call | solution.py:369
  233.2 4.9 fusion.45
  241.3 8.2 %collective-permute-done.17 = bf16[80,2304]{1,0:T(8,128)(2,1)} collective-permute-done((bf16[80,2304]{1,0:T(8,128)(2,1)}, bf16[80,2304]{1,0:T(8,128)(2,1)}, u32[]{:S(2)}, u32[]{:S(2)}) %collective-permute-start.17) | collective-permute-done | bytes 368672 | tf_op jit(solution)/shard_map/ppermute | solution.py:29
  260.9 9.3 %collective-permute-done.18 = bf16[80,2304]{1,0:T(8,128)(2,1)} collective-permute-done((bf16[80,2304]{1,0:T(8,128)(2,1)}, bf16[80,2304]{1,0:T(8,128)(2,1)}, u32[]{:S(2)}, u32[]{:S(2)}) %collective-permute-start.18) | collective-permute-done | bytes 368672 | tf_op jit(solution)/shard_map/ppermute | solution.py:29
  270.2 4.1 copy.147
  284.5 13.7 %collective-permute-done.21 = bf16[80,2304]{1,0:T(8,128)(2,1)S(1)} collective-permute-done((bf16[80,2304]{1,0:T(8,128)(2,1)S(1)}, bf16[80,2304]{1,0:T(8,128)(2,1)S(1)}, u32[]{:S(2)}, u32[]{:S(2)}) %collective-permute-start.21) | collective-permute-done | bytes 368672 | tf_op jit(solution)/shard_map/ppermute | solution.py:29
  301.4 6.8 collective-permute-done.22
  316.6 6.8 fusion.29
  323.5 7.7 %multiply_convert_fusion = (bf16[320,1440]{1,0:T(8,128)(2,1)S(1)}, bf16[320,1440]{1,0:T(8,128)(2,1)S(1)}, bf16[320,1440]{1,0:T(8,128)(2,1)S(1)}) fusion(f32[320,1440]{1,0:T(8,128)} %fusion.29, f32[320,1440]{1,0:T(8,128)} %convolution_add_fusion.2, bf16[2304,1440]{1,0:T(8,128)(2,1)} %all-gather.12.cloned.1.call-done, bf16[80,2304]{1,0:T(8,128)(2,1)} %copy-done.51, ...), kind=kOutput, calls=%fused_computation.12 | convolution fusion | flops 2136176640 | bytes 14561280 | tf_op jit(solution)/shard_map/dot_general | solution.py:25
  334.6 4.1 convolution_add_fusion.1
  338.7 8.8 %shard_map.154 = bf16[1152,1440]{1,0:T(8,128)(2,1)} custom-call(bf16[320,1152]{1,0:T(8,128)(2,1)S(1)} %get-tuple-element.250.left_ref, bf16[320,1152]{1,0:T(8,128)(2,1)} %collective-permute-done.23.left_far_ref, bf16[320,1440]{1,0:T(8,128)(2,1)S(1)} %get-tuple-element.140.right_ref, bf16[320,1440]{1,0:T(8,128)(2,1)S(1)} %collective-permute-done.24.right_far_ref), custom_call_target="tpu_custom_call" | custom-call | flops 2123366400 | bytes 3317760 | tf_op jit(solution)/shard_map/pallas_call | solution.py:142
  347.5 4.9 all-to-all-start.2
  356.9 7.8 %collective-permute-done.27 = bf16[80,2304]{1,0:T(8,128)(2,1)S(1)} collective-permute-done((bf16[80,2304]{1,0:T(8,128)(2,1)S(1)}, bf16[80,2304]{1,0:T(8,128)(2,1)S(1)}, u32[]{:S(2)}, u32[]{:S(2)}) %collective-permute-start.27) | collective-permute-done | bytes 368672 | tf_op jit(solution)/shard_map/ppermute | solution.py:29
  367.0 8.7 %shard_map.155 = bf16[1152,1440]{1,0:T(8,128)(2,1)} custom-call(bf16[320,1152]{1,0:T(8,128)(2,1)S(1)} %get-tuple-element.129.left_ref, bf16[320,1152]{1,0:T(8,128)(2,1)} %collective-permute-done.25.left_far_ref, bf16[320,1440]{1,0:T(8,128)(2,1)S(1)} %get-tuple-element.131.right_ref, bf16[320,1440]{1,0:T(8,128)(2,1)S(1)} %collective-permute-done.29.right_far_ref), custom_call_target="tpu_custom_call" | custom-call | flops 2123366400 | bytes 3317760 | tf_op jit(solution)/shard_map/pallas_call | solution.py:142
  375.7 8.9 %shard_map.156 = bf16[1152,1440]{1,0:T(8,128)(2,1)} custom-call(bf16[320,1152]{1,0:T(8,128)(2,1)S(1)} %get-tuple-element.129.left_ref, bf16[320,1152]{1,0:T(8,128)(2,1)} %collective-permute-done.25.left_far_ref, bf16[320,1440]{1,0:T(8,128)(2,1)S(1)} %get-tuple-element.132.right_ref, bf16[320,1440]{1,0:T(8,128)(2,1)S(1)} %collective-permute-done.30.right_far_ref), custom_call_target="tpu_custom_call" | custom-call | flops 2123366400 | bytes 3317760 | tf_op jit(solution)/shard_map/pallas_call | solution.py:142
  384.6 8.5 %all-to-all-done.2 = bf16[4,288,1440]{2,1,0:T(8,128)(2,1)} async-done(((bf16[4,288,1440]{2,1,0:T(8,128)(2,1)}), bf16[4,288,1440]{2,1,0:T(8,128)(2,1)}, u32[]{:S(2)}, u32[]{:S(2)}) %all-to-all-start.2) | async-done | bytes 3317792 | tf_op jit(solution)/shard_map/all_to_all | solution.py:162
  394.6 4.9 all-to-all-start.3
  417.7 4.5 collective-permute-start.33
  424.1 5.1 collective-permute-done.33
  429.1 10.2 %all-to-all-done.3 = bf16[4,288,1440]{2,1,0:T(8,128)(2,1)} async-done(((bf16[4,288,1440]{2,1,0:T(8,128)(2,1)}), bf16[4,288,1440]{2,1,0:T(8,128)(2,1)}, u32[]{:S(2)}, u32[]{:S(2)}) %all-to-all-start.3) | async-done | bytes 3317792 | tf_op jit(solution)/shard_map/all_to_all | solution.py:162
  452.2 4.9 all-to-all-start.4
  462.7 23.0 %shard_map.157 = (f32[320,1152]{1,0:T(8,128)}, bf16[4,4,80,1152]{3,2,1,0:T(8,128)(2,1)}, bf16[4,4,80,1152]{3,2,1,0:T(8,128)(2,1)}) custom-call(s32[1]{0:T(128)} %bitcast.row_ref, s32[320,4]{1,0:T(8,128)} %copy.144.query_ref, s32[4,2,640]{2,1,0:T(2,128)} %pad_add_fusion.key_ref, bf16[320,1152]{1,0:T(8,128)(2,1)} %copy.145.q_ref, ...), custom_call_target="tpu_custom_call" | custom-call | flops 117964800000 | bytes 11796480 | tf_op jit(solution)/shard_map/pallas_call | solution.py:383
  485.8 11.2 %all-to-all-done.4 = bf16[4,288,1440]{2,1,0:T(8,128)(2,1)} async-done(((bf16[4,288,1440]{2,1,0:T(8,128)(2,1)}), bf16[4,288,1440]{2,1,0:T(8,128)(2,1)}, u32[]{:S(2)}, u32[]{:S(2)}) %all-to-all-start.4) | async-done | bytes 3317792 | tf_op jit(solution)/shard_map/all_to_all | solution.py:162
  511.2 4.2 add_convert_fusion
  515.4 4.6 all-to-all-start.5
  538.8 5.3 collective-permute-start.42
  545.5 5.2 shard_map.158
  550.8 6.6 shard_map.159
  559.7 11.2 %all-to-all-done.5 = bf16[4,320,1152]{2,1,0:T(8,128)(2,1)} async-done(((bf16[4,320,1152]{2,1,0:T(8,128)(2,1)}), bf16[4,320,1152]{2,1,0:T(8,128)(2,1)}, u32[]{:S(2)}, u32[]{:S(2)}) %all-to-all-start.5) | async-done | bytes 2949152 | tf_op jit(solution)/shard_map/all_to_all | solution.py:162
  577.8 5.0 fusion.52
  584.2 5.5 collective-permute-done.42
  591.0 12.8 %all-to-all-start.6 = ((bf16[4,288,1152]{2,1,0:T(8,128)(2,1)}), bf16[4,288,1152]{2,1,0:T(8,128)(2,1)}, u32[]{:S(2)}, u32[]{:S(2)}) async-start(bf16[4,288,1152]{2,1,0:T(8,128)(2,1)} %pad_maximum_fusion.1), calls=%async_computation.6 | async-start | bytes 5308416 | tf_op jit(solution)/shard_map/all_to_all | solution.py:162
  611.6 4.8 collective-permute-done.45
  619.7 6.4 shard_map.160
  629.5 6.7 collective-permute-done.46
  655.4 22.4 %collective-permute-done.54 = f32[2,2304]{1,0:T(2,128)S(1)} collective-permute-done((f32[2,2304]{1,0:T(2,128)S(1)}, f32[2,2304]{1,0:T(2,128)S(1)}, u32[]{:S(2)}, u32[]{:S(2)}) %collective-permute-start.54) | collective-permute-done | bytes 18464 | tf_op jit(solution)/shard_map/ppermute | solution.py:610
  692.5 8.2 %collective-permute-start.51 = (bf16[288,1024]{1,0:T(8,128)(2,1)}, bf16[288,1024]{1,0:T(8,128)(2,1)}, u32[]{:S(2)}, u32[]{:S(2)}) collective-permute-start(bf16[288,1024]{1,0:T(8,128)(2,1)} %pad_maximum_fusion.18), channel_id=1, source_target_pairs={{16,0},{24,1},{0,2},{8,3},{18,8},{26,9},{2,10},{10,11},{17,16},{25... | collective-permute-start | bytes 1769480 | tf_op jit(solution)/shard_map/ppermute | solution.py:96
  711.0 29.2 %collective-permute-done.50 = bf16[288,1280]{1,0:T(8,128)(2,1)S(1)} collective-permute-done((bf16[288,1280]{1,0:T(8,128)(2,1)S(1)}, bf16[288,1280]{1,0:T(8,128)(2,1)S(1)}, u32[]{:S(2)}, u32[]{:S(2)}) %collective-permute-start.50) | collective-permute-done | bytes 737312 | tf_op jit(solution)/shard_map/ppermute | solution.py:96
  (476 shorter events, 277.6 us)
Async XLA Ops:
  7.2 86.3 %all-gather.6.cloned.1.call-start = ((), (), s32[]{:S(2)}) async-start(), calls=%async_computation.8 | async-start | bytes 5971968 | tf_op jit(solution)/shard_map/all_gather | solution.py:114
  9.2 27.2 %collective-permute-start.4 = (bf16[288,640]{0,1:T(8,128)(2,1)S(1)}, bf16[288,640]{0,1:T(8,128)(2,1)S(1)}, u32[]{:S(2)}, u32[]{:S(2)}) collective-permute-start(bf16[288,640]{0,1:T(8,128)(2,1)S(1)} %slice.450), channel_id=1, source_target_pairs={{0,0},{1,8},{2,16},{3,24},{8,2},{9,10},{10,18},{11,26},{16,1},{17,... | collective-permute-start | bytes 1105928 | tf_op jit(solution)/shard_map/ppermute | solution.py:96
  13.9 21.2 %collective-permute-start.5 = (bf16[288,512]{0,1:T(8,128)(2,1)S(1)}, bf16[288,512]{0,1:T(8,128)(2,1)S(1)}, u32[]{:S(2)}, u32[]{:S(2)}) collective-permute-start(bf16[288,512]{0,1:T(8,128)(2,1)S(1)} %slice.451), channel_id=1, source_target_pairs={{0,16},{1,24},{2,0},{3,8},{8,18},{9,26},{10,2},{11,10},{16,17},{17... | collective-permute-start | bytes 884744 | tf_op jit(solution)/shard_map/ppermute | solution.py:96
  37.7 98.3 %all-gather.8.cloned.1.call-start = ((), (), s32[]{:S(2)}) async-start(), calls=%async_computation.9 | async-start | bytes 3317760 | tf_op jit(solution)/shard_map/all_gather | solution.py:114
  39.3 31.1 %collective-permute-start = (bf16[81,2304]{1,0:T(8,128)(2,1)}, bf16[81,2304]{1,0:T(8,128)(2,1)}, u32[]{:S(2)}, u32[]{:S(2)}) collective-permute-start(bf16[81,2304]{1,0:T(8,128)(2,1)} %constant_dynamic-update-slice_fusion), channel_id=1, source_target_pairs={{0,8},{8,0},{16,24},{24,16},{1,9},{9,1},{17,25},{25,17},{2,10},{10... | collective-permute-start | bytes 1119752 | tf_op jit(solution)/shard_map/ppermute | solution.py:29
  39.4 25.7 %collective-permute-start.1 = (bf16[81,2304]{1,0:T(8,128)(2,1)}, bf16[81,2304]{1,0:T(8,128)(2,1)}, u32[]{:S(2)}, u32[]{:S(2)}) collective-permute-start(bf16[81,2304]{1,0:T(8,128)(2,1)} %constant_dynamic-update-slice_fusion), channel_id=1, source_target_pairs={{0,16},{8,24},{16,0},{24,8},{1,17},{9,25},{17,1},{25,9},{2,18},{10... | collective-permute-start | bytes 1119752 | tf_op jit(solution)/shard_map/ppermute | solution.py:29
  40.1 28.1 %collective-permute-start.9 = (bf16[288,256]{1,0:T(8,128)(2,1)}, bf16[288,256]{1,0:T(8,128)(2,1)}, u32[]{:S(2)}, u32[]{:S(2)}) collective-permute-start(bf16[288,256]{1,0:T(8,128)(2,1)} %slice.460), channel_id=1, source_target_pairs={{0,16},{1,24},{2,0},{3,8},{8,18},{9,26},{10,2},{11,10},{16,17},{17... | collective-permute-start | bytes 442376 | tf_op jit(solution)/shard_map/ppermute | solution.py:96
  42.1 26.3 %collective-permute-start.8 = (bf16[288,320]{1,0:T(8,128)(2,1)}, bf16[288,320]{1,0:T(8,128)(2,1)}, u32[]{:S(2)}, u32[]{:S(2)}) collective-permute-start(bf16[288,320]{1,0:T(8,128)(2,1)} %slice.459), channel_id=1, source_target_pairs={{0,0},{1,8},{2,16},{3,24},{8,2},{9,10},{10,18},{11,26},{16,1},{17,... | collective-permute-start | bytes 552968 | tf_op jit(solution)/shard_map/ppermute | solution.py:96
  70.4 162.8 %all-gather.10.cloned.1.call-start = ((), (), s32[]{:S(2)}) async-start(), calls=%async_computation.10 | async-start | bytes 3317760 | tf_op jit(solution)/shard_map/all_gather | solution.py:114
  83.1 32.4 %collective-permute-start.14 = (bf16[288,1088]{1,0:T(8,128)(2,1)}, bf16[288,1088]{1,0:T(8,128)(2,1)}, u32[]{:S(2)}, u32[]{:S(2)}) collective-permute-start(bf16[288,1088]{1,0:T(8,128)(2,1)} %pad_maximum_fusion.16), channel_id=1, source_target_pairs={{0,0},{1,8},{2,16},{3,24},{8,2},{9,10},{10,18},{11,26},{16,1},{17,... | collective-permute-start | bytes 1880072 | tf_op jit(solution)/shard_map/ppermute | solution.py:96
  85.0 30.5 %collective-permute-start.15 = (bf16[288,928]{1,0:T(8,128)(2,1)}, bf16[288,928]{1,0:T(8,128)(2,1)}, u32[]{:S(2)}, u32[]{:S(2)}) collective-permute-start(bf16[288,928]{1,0:T(8,128)(2,1)} %pad_maximum_fusion.17), channel_id=1, source_target_pairs={{0,16},{1,24},{2,0},{3,8},{8,18},{9,26},{10,2},{11,10},{16,17},{17... | collective-permute-start | bytes 1603592 | tf_op jit(solution)/shard_map/ppermute | solution.py:96
  118.4 198.1 %all-gather.14.cloned.1.call-start = ((), (), s32[]{:S(2)}) async-start(), calls=%async_computation.12 | async-start | bytes 7962624 | tf_op jit(solution)/shard_map/all_gather | solution.py:114
  124.2 69.7 %all-to-all-start = ((bf16[4,320,1152]{2,1,0:T(8,128)(2,1)}), bf16[4,320,1152]{2,1,0:T(8,128)(2,1)}, u32[]{:S(2)}, u32[]{:S(2)}) async-start(bf16[4,320,1152]{2,1,0:T(8,128)(2,1)} %broadcast_in_dim.30), calls=%async_computation | async-start | bytes 5898240 | tf_op jit(solution)/shard_map/all_to_all | solution.py:162
  128.8 65.1 %collective-permute-start.6 = (bf16[288,1536]{1,0:T(8,128)(2,1)}, bf16[288,1536]{1,0:T(8,128)(2,1)}, u32[]{:S(2)}, u32[]{:S(2)}) collective-permute-start(bf16[288,1536]{1,0:T(8,128)(2,1)} %pad_maximum_fusion.4), channel_id=1, source_target_pairs={{0,0},{1,8},{2,16},{3,24},{8,2},{9,10},{10,18},{11,26},{16,1},{17,... | collective-permute-start | bytes 2654216 | tf_op jit(solution)/shard_map/ppermute | solution.py:96
  130.9 55.2 %collective-permute-start.10 = (bf16[80,2304]{1,0:T(8,128)(2,1)S(1)}, bf16[80,2304]{1,0:T(8,128)(2,1)}, u32[]{:S(2)}, u32[]{:S(2)}) collective-permute-start(bf16[80,2304]{1,0:T(8,128)(2,1)S(1)} %fusion.9), channel_id=1, source_target_pairs={{0,8},{8,0},{16,24},{24,16},{1,9},{9,1},{17,25},{25,17},{2,10},{10... | collective-permute-start | bytes 1105928 | tf_op jit(solution)/shard_map/ppermute | solution.py:29
  131.5 54.2 %collective-permute-start.11 = (bf16[80,2304]{1,0:T(8,128)(2,1)S(1)}, bf16[80,2304]{1,0:T(8,128)(2,1)}, u32[]{:S(2)}, u32[]{:S(2)}) collective-permute-start(bf16[80,2304]{1,0:T(8,128)(2,1)S(1)} %fusion.9), channel_id=1, source_target_pairs={{0,16},{8,24},{16,0},{24,8},{1,17},{9,25},{17,1},{25,9},{2,18},{10... | collective-permute-start | bytes 1105928 | tf_op jit(solution)/shard_map/ppermute | solution.py:29
  134.5 59.3 %collective-permute-start.7 = (bf16[288,1344]{1,0:T(8,128)(2,1)}, bf16[288,1344]{1,0:T(8,128)(2,1)S(1)}, u32[]{:S(2)}, u32[]{:S(2)}) collective-permute-start(bf16[288,1344]{1,0:T(8,128)(2,1)} %pad_maximum_fusion.14), channel_id=1, source_target_pairs={{0,16},{1,24},{2,0},{3,8},{8,18},{9,26},{10,2},{11,10},{16,17},{17... | collective-permute-start | bytes 2322440 | tf_op jit(solution)/shard_map/ppermute | solution.py:96
  204.3 55.5 %all-to-all-start.1 = ((bf16[4,288,1440]{2,1,0:T(8,128)(2,1)}), bf16[4,288,1440]{2,1,0:T(8,128)(2,1)S(1)}, u32[]{:S(2)}, u32[]{:S(2)}) async-start(bf16[4,288,1440]{2,1,0:T(8,128)(2,1)} %broadcast_in_dim.31), calls=%async_computation.1 | async-start | bytes 7077888 | tf_op jit(solution)/shard_map/all_to_all | solution.py:162
  208.1 115.4 %all-gather.12.cloned.1.call-start = ((), (), s32[]{:S(2)}) async-start(), calls=%async_computation.11 | async-start | bytes 7962624 | tf_op jit(solution)/shard_map/all_gather | solution.py:114
  239.8 21.1 %collective-permute-start.16 = (bf16[80,2304]{1,0:T(8,128)(2,1)}, bf16[80,2304]{1,0:T(8,128)(2,1)}, u32[]{:S(2)}, u32[]{:S(2)}) collective-permute-start(bf16[80,2304]{1,0:T(8,128)(2,1)} %get-tuple-element.253), channel_id=1, source_target_pairs={{0,8},{8,0},{16,24},{24,16},{1,9},{9,1},{17,25},{25,17},{2,10},{10... | collective-permute-start | bytes 1105928 | tf_op jit(solution)/shard_map/ppermute | solution.py:29
  252.1 18.1 %collective-permute-start.18 = (bf16[80,2304]{1,0:T(8,128)(2,1)}, bf16[80,2304]{1,0:T(8,128)(2,1)}, u32[]{:S(2)}, u32[]{:S(2)}) collective-permute-start(bf16[80,2304]{1,0:T(8,128)(2,1)} %get-tuple-element.234), channel_id=1, source_target_pairs={{0,16},{8,24},{16,0},{24,8},{1,17},{9,25},{17,1},{25,9},{2,18},{10... | collective-permute-start | bytes 1105928 | tf_op jit(solution)/shard_map/ppermute | solution.py:29
  274.3 36.3 %collective-permute-start.19 = (bf16[1152,1440]{0,1:T(8,128)(2,1)}, bf16[1152,1440]{0,1:T(8,128)(2,1)S(1)}, u32[]{:S(2)}, u32[]{:S(2)}) collective-permute-start(bf16[1152,1440]{0,1:T(8,128)(2,1)} %copy.147), channel_id=1, source_target_pairs={{0,1},{1,0},{2,3},{3,2},{4,5},{5,4},{6,7},{7,6},{8,9},{9,8},{10,11... | collective-permute-start | bytes 9953288 | tf_op jit(solution)/shard_map/ppermute | solution.py:33
  279.0 19.2 %collective-permute-start.21 = (bf16[80,2304]{1,0:T(8,128)(2,1)S(1)}, bf16[80,2304]{1,0:T(8,128)(2,1)S(1)}, u32[]{:S(2)}, u32[]{:S(2)}) collective-permute-start(bf16[80,2304]{1,0:T(8,128)(2,1)S(1)} %multiply_convert_fusion.4), channel_id=1, source_target_pairs={{0,16},{8,24},{16,0},{24,8},{1,17},{9,25},{17,1},{25,9},{2,18},{10... | collective-permute-start | bytes 1105928 | tf_op jit(solution)/shard_map/ppermute | solution.py:29
  281.7 19.7 %collective-permute-start.20 = (bf16[80,2304]{1,0:T(8,128)(2,1)S(1)}, bf16[80,2304]{1,0:T(8,128)(2,1)S(1)}, u32[]{:S(2)}, u32[]{:S(2)}) collective-permute-start(bf16[80,2304]{1,0:T(8,128)(2,1)S(1)} %multiply_convert_fusion.4), channel_id=1, source_target_pairs={{0,8},{8,0},{16,24},{24,16},{1,9},{9,1},{17,25},{25,17},{2,10},{10... | collective-permute-start | bytes 1105928 | tf_op jit(solution)/shard_map/ppermute | solution.py:29
  300.7 38.0 %collective-permute-start.23 = (bf16[320,1152]{1,0:T(8,128)(2,1)}, bf16[320,1152]{1,0:T(8,128)(2,1)}, u32[]{:S(2)}, u32[]{:S(2)}) collective-permute-start(bf16[320,1152]{1,0:T(8,128)(2,1)} %get-tuple-element.251), channel_id=1, source_target_pairs={{0,1},{1,0},{2,3},{3,2},{4,5},{5,4},{6,7},{7,6},{8,9},{9,8},{10,11... | collective-permute-start | bytes 2211848 | tf_op jit(solution)/shard_map/ppermute | solution.py:33
  309.3 38.1 %collective-permute-start.25 = (bf16[320,1152]{1,0:T(8,128)(2,1)}, bf16[320,1152]{1,0:T(8,128)(2,1)}, u32[]{:S(2)}, u32[]{:S(2)}) collective-permute-start(bf16[320,1152]{1,0:T(8,128)(2,1)} %get-tuple-element.248), channel_id=1, source_target_pairs={{0,1},{1,0},{2,3},{3,2},{4,5},{5,4},{6,7},{7,6},{8,9},{9,8},{10,11... | collective-permute-start | bytes 2211848 | tf_op jit(solution)/shard_map/ppermute | solution.py:33
  347.5 45.6 %all-to-all-start.2 = ((bf16[4,288,1440]{2,1,0:T(8,128)(2,1)}), bf16[4,288,1440]{2,1,0:T(8,128)(2,1)}, u32[]{:S(2)}, u32[]{:S(2)}) async-start(bf16[4,288,1440]{2,1,0:T(8,128)(2,1)} %bitcast.30), calls=%async_computation.2 | async-start | bytes 7077888 | tf_op jit(solution)/shard_map/all_to_all | solution.py:162
  356.4 28.2 %collective-permute-start.26 = (bf16[80,2304]{1,0:T(8,128)(2,1)S(1)}, bf16[80,2304]{1,0:T(8,128)(2,1)}, u32[]{:S(2)}, u32[]{:S(2)}) collective-permute-start(bf16[80,2304]{1,0:T(8,128)(2,1)S(1)} %get-tuple-element.247), channel_id=1, source_target_pairs={{0,8},{8,0},{16,24},{24,16},{1,9},{9,1},{17,25},{25,17},{2,10},{10... | collective-permute-start | bytes 1105928 | tf_op jit(solution)/shard_map/ppermute | solution.py:29
  356.6 19.1 %collective-permute-start.30 = (bf16[320,1440]{1,0:T(8,128)(2,1)S(1)}, bf16[320,1440]{1,0:T(8,128)(2,1)S(1)}, u32[]{:S(2)}, u32[]{:S(2)}) collective-permute-start(bf16[320,1440]{1,0:T(8,128)(2,1)S(1)} %get-tuple-element.132.right_ref), channel_id=1, source_target_pairs={{0,1},{1,0},{2,3},{3,2},{4,5},{5,4},{6,7},{7,6},{8,9},{9,8},{10,11... | collective-permute-start | bytes 2764808 | tf_op jit(solution)/shard_map/ppermute | solution.py:33
  364.8 19.8 %collective-permute-start.28 = (bf16[80,2304]{1,0:T(8,128)(2,1)S(1)}, bf16[80,2304]{1,0:T(8,128)(2,1)}, u32[]{:S(2)}, u32[]{:S(2)}) collective-permute-start(bf16[80,2304]{1,0:T(8,128)(2,1)S(1)} %get-tuple-element.232), channel_id=1, source_target_pairs={{0,16},{8,24},{16,0},{24,8},{1,17},{9,25},{17,1},{25,9},{2,18},{10... | collective-permute-start | bytes 1105928 | tf_op jit(solution)/shard_map/ppermute | solution.py:29
  394.6 44.7 %all-to-all-start.3 = ((bf16[4,288,1440]{2,1,0:T(8,128)(2,1)}), bf16[4,288,1440]{2,1,0:T(8,128)(2,1)}, u32[]{:S(2)}, u32[]{:S(2)}) async-start(bf16[4,288,1440]{2,1,0:T(8,128)(2,1)} %bitcast.31), calls=%async_computation.3 | async-start | bytes 7077888 | tf_op jit(solution)/shard_map/all_to_all | solution.py:162
  401.9 22.2 %collective-permute-start.31 = (bf16[80,2304]{1,0:T(8,128)(2,1)}, bf16[80,2304]{1,0:T(8,128)(2,1)}, u32[]{:S(2)}, u32[]{:S(2)}) collective-permute-start(bf16[80,2304]{1,0:T(8,128)(2,1)} %get-tuple-element.143), channel_id=1, source_target_pairs={{0,8},{8,0},{16,24},{24,16},{1,9},{9,1},{17,25},{25,17},{2,10},{10... | collective-permute-start | bytes 1105928 | tf_op jit(solution)/shard_map/ppermute | solution.py:29
  409.0 20.2 %collective-permute-start.34 = (bf16[320,1152]{1,0:T(8,128)(2,1)S(1)}, bf16[320,1152]{1,0:T(8,128)(2,1)S(1)}, u32[]{:S(2)}, u32[]{:S(2)}) collective-permute-start(bf16[320,1152]{1,0:T(8,128)(2,1)S(1)} %get-tuple-element.244), channel_id=1, source_target_pairs={{0,1},{1,0},{2,3},{3,2},{4,5},{5,4},{6,7},{7,6},{8,9},{9,8},{10,11... | collective-permute-start | bytes 2211848 | tf_op jit(solution)/shard_map/ppermute | solution.py:33
  452.2 44.8 %all-to-all-start.4 = ((bf16[4,288,1440]{2,1,0:T(8,128)(2,1)}), bf16[4,288,1440]{2,1,0:T(8,128)(2,1)}, u32[]{:S(2)}, u32[]{:S(2)}) async-start(bf16[4,288,1440]{2,1,0:T(8,128)(2,1)} %bitcast.32), calls=%async_computation.4 | async-start | bytes 7077888 | tf_op jit(solution)/shard_map/all_to_all | solution.py:162
  457.1 28.6 %collective-permute-start.35 = (bf16[80,2304]{1,0:T(8,128)(2,1)}, bf16[80,2304]{1,0:T(8,128)(2,1)S(1)}, u32[]{:S(2)}, u32[]{:S(2)}) collective-permute-start(bf16[80,2304]{1,0:T(8,128)(2,1)} %get-tuple-element.243), channel_id=1, source_target_pairs={{0,8},{8,0},{16,24},{24,16},{1,9},{9,1},{17,25},{25,17},{2,10},{10... | collective-permute-start | bytes 1105928 | tf_op jit(solution)/shard_map/ppermute | solution.py:29
  460.1 25.7 %collective-permute-start.37 = (bf16[80,2304]{1,0:T(8,128)(2,1)S(1)}, bf16[80,2304]{1,0:T(8,128)(2,1)S(1)}, u32[]{:S(2)}, u32[]{:S(2)}) collective-permute-start(bf16[80,2304]{1,0:T(8,128)(2,1)S(1)} %get-tuple-element.230), channel_id=1, source_target_pairs={{0,16},{8,24},{16,0},{24,8},{1,17},{9,25},{17,1},{25,9},{2,18},{10... | collective-permute-start | bytes 1105928 | tf_op jit(solution)/shard_map/ppermute | solution.py:29
  505.6 45.1 %collective-permute-start.41 = (bf16[320,576]{1,0:T(8,128)(2,1)S(1)}, bf16[320,576]{1,0:T(8,128)(2,1)S(1)}, u32[]{:S(2)}, u32[]{:S(2)}) collective-permute-start(bf16[320,576]{1,0:T(8,128)(2,1)S(1)} %copy.157.right_ref), channel_id=1, source_target_pairs={{0,1},{1,0},{2,3},{3,2},{4,5},{5,4},{6,7},{7,6},{8,9},{9,8},{10,11... | collective-permute-start | bytes 1105928 | tf_op jit(solution)/shard_map/ppermute | solution.py:33
  515.4 55.5 %all-to-all-start.5 = ((bf16[4,320,1152]{2,1,0:T(8,128)(2,1)}), bf16[4,320,1152]{2,1,0:T(8,128)(2,1)}, u32[]{:S(2)}, u32[]{:S(2)}) async-start(bf16[4,320,1152]{2,1,0:T(8,128)(2,1)} %bitcast.146), calls=%async_computation.5 | async-start | bytes 5898240 | tf_op jit(solution)/shard_map/all_to_all | solution.py:162
  522.4 28.4 %collective-permute-start.40 = (bf16[320,1152]{1,0:T(8,128)(2,1)}, bf16[320,1152]{1,0:T(8,128)(2,1)}, u32[]{:S(2)}, u32[]{:S(2)}) collective-permute-start(bf16[320,1152]{1,0:T(8,128)(2,1)} %get-tuple-element.240), channel_id=1, source_target_pairs={{0,1},{1,0},{2,3},{3,2},{4,5},{5,4},{6,7},{7,6},{8,9},{9,8},{10,11... | collective-permute-start | bytes 2211848 | tf_op jit(solution)/shard_map/ppermute | solution.py:33
  538.8 51.0 %collective-permute-start.42 = (bf16[288,1536]{1,0:T(8,128)(2,1)}, bf16[288,1536]{1,0:T(8,128)(2,1)}, u32[]{:S(2)}, u32[]{:S(2)}) collective-permute-start(bf16[288,1536]{1,0:T(8,128)(2,1)} %pad_maximum_fusion.11), channel_id=1, source_target_pairs={{0,0},{8,1},{16,2},{24,3},{2,8},{10,9},{18,10},{26,11},{1,16},{9,1... | collective-permute-start | bytes 2654216 | tf_op jit(solution)/shard_map/ppermute | solution.py:96
  544.0 40.2 %collective-permute-start.43 = (bf16[288,1344]{1,0:T(8,128)(2,1)}, bf16[288,1344]{1,0:T(8,128)(2,1)}, u32[]{:S(2)}, u32[]{:S(2)}) collective-permute-start(bf16[288,1344]{1,0:T(8,128)(2,1)} %pad_maximum_fusion.15), channel_id=1, source_target_pairs={{16,0},{24,1},{0,2},{8,3},{18,8},{26,9},{2,10},{10,11},{17,16},{25... | collective-permute-start | bytes 2322440 | tf_op jit(solution)/shard_map/ppermute | solution.py:96
  591.0 35.2 %all-to-all-start.6 = ((bf16[4,288,1152]{2,1,0:T(8,128)(2,1)}), bf16[4,288,1152]{2,1,0:T(8,128)(2,1)}, u32[]{:S(2)}, u32[]{:S(2)}) async-start(bf16[4,288,1152]{2,1,0:T(8,128)(2,1)} %pad_maximum_fusion.1), calls=%async_computation.6 | async-start | bytes 5308416 | tf_op jit(solution)/shard_map/all_to_all | solution.py:162
  605.7 23.7 %collective-permute-start.44 = (bf16[80,2304]{1,0:T(8,128)(2,1)}, bf16[80,2304]{1,0:T(8,128)(2,1)}, u32[]{:S(2)}, u32[]{:S(2)}) collective-permute-start(bf16[80,2304]{1,0:T(8,128)(2,1)} %get-tuple-element.239), channel_id=1, source_target_pairs={{0,8},{8,0},{16,24},{24,16},{1,9},{9,1},{17,25},{25,17},{2,10},{10... | collective-permute-start | bytes 1105928 | tf_op jit(solution)/shard_map/ppermute | solution.py:29
  643.1 46.6 %all-to-all-start.7 = ((bf16[4,288,1152]{2,1,0:T(8,128)(2,1)}), bf16[4,288,1152]{2,1,0:T(8,128)(2,1)S(1)}, u32[]{:S(2)}, u32[]{:S(2)}) async-start(bf16[4,288,1152]{2,1,0:T(8,128)(2,1)} %bitcast.45), calls=%async_computation.7 | async-start | bytes 5308416 | tf_op jit(solution)/shard_map/all_to_all | solution.py:162
  646.8 38.9 %collective-permute-start.48 = (bf16[288,768]{1,0:T(8,128)(2,1)}, bf16[288,768]{1,0:T(8,128)(2,1)}, u32[]{:S(2)}, u32[]{:S(2)}) collective-permute-start(bf16[288,768]{1,0:T(8,128)(2,1)} %slice.488), channel_id=1, source_target_pairs={{0,0},{8,1},{16,2},{24,3},{2,8},{10,9},{18,10},{26,11},{1,16},{9,1... | collective-permute-start | bytes 1327112 | tf_op jit(solution)/shard_map/ppermute | solution.py:96
  649.8 35.1 %collective-permute-start.49 = (bf16[288,672]{1,0:T(8,128)(2,1)}, bf16[288,672]{1,0:T(8,128)(2,1)S(1)}, u32[]{:S(2)}, u32[]{:S(2)}) collective-permute-start(bf16[288,672]{1,0:T(8,128)(2,1)} %slice.489), channel_id=1, source_target_pairs={{16,0},{24,1},{0,2},{8,3},{18,8},{26,9},{2,10},{10,11},{17,16},{25... | collective-permute-start | bytes 1161224 | tf_op jit(solution)/shard_map/ppermute | solution.py:96
  651.6 26.2 %collective-permute-start.54 = (f32[2,2304]{1,0:T(2,128)S(1)}, f32[2,2304]{1,0:T(2,128)S(1)}, u32[]{:S(2)}, u32[]{:S(2)}) collective-permute-start(f32[2,2304]{1,0:T(2,128)S(1)} %fusion.79), channel_id=1, source_target_pairs={{0,4},{4,0},{1,5},{5,1},{2,6},{6,2},{3,7},{7,3},{8,12},{12,8},{9,1... | collective-permute-start | bytes 55304 | tf_op jit(solution)/shard_map/ppermute | solution.py:610
  701.2 39.1 %collective-permute-start.50 = (bf16[288,1280]{1,0:T(8,128)(2,1)S(1)}, bf16[288,1280]{1,0:T(8,128)(2,1)S(1)}, u32[]{:S(2)}, u32[]{:S(2)}) collective-permute-start(bf16[288,1280]{1,0:T(8,128)(2,1)S(1)} %concatenate.148), channel_id=1, source_target_pairs={{0,0},{8,1},{16,2},{24,3},{2,8},{10,9},{18,10},{26,11},{1,16},{9,1... | collective-permute-start | bytes 2211848 | tf_op jit(solution)/shard_map/ppermute | solution.py:96
  (88 other events, 1181.0 us)
Sparse Core Ops, SparseCore 0:
  37.8 46.0 all-gather.5
  85.8 38.1 all-gather.7
  125.9 54.7 all-gather.9
  182.5 90.4 all-gather.13
  274.6 48.8 all-gather.11
